TPU v7x, 32 devices: a whole 2x2x4 slice. The times are simulated.
32 devices in a mesh: seq: 8 (over z, x), head: 4 (over y, core).
Axes of the slice: x: 2, y: 2, z: 4, core: 2. Of those that a mesh axis runs over, the one named last changes fastest.
Arguments:
- queries: bfloat16 [4096, 8192], P('seq', 'head'), may hold values from -0.5 to 0.5
- keys: bfloat16 [4096, 8192], P('seq', 'head'), may hold values from -6 to 6
- values: bfloat16 [4096, 8192], P('seq', 'head'), may hold values from -6 to 6
- cotangent: bfloat16 [4096, 8192], P('seq', 'head'), may hold values from -6 to 6
- log_decay: float32 [64, 4096], P('head', 'seq'), may hold values from -0.6 to 0
- starts: int32 [4096], P('seq'), may hold values 0 or 1
Outputs:
- attn_out: bfloat16 [4096, 8192], P('seq', 'head')
- grad_query: bfloat16 [4096, 8192], P('seq', 'head')
- grad_key: bfloat16 [4096, 8192], P('seq', 'head')
- grad_value: bfloat16 [4096, 8192], P('seq', 'head')
All inputs are finite; a program needn't handle non-finite values. No bound on the sum of `starts` on one device may be relied on, other than what follows from the above.
Results may differ from a plain program's by a relative error of at most 0.0095.
Values may be sent and summed in bfloat16 or wider, within the bound.
No kernel may reach another device: no remote copies, remote signals or barrier semaphores. Data moves between devices by JAX's collectives and lax.ppermute only.
A program may use at most 128 MiB of HBM per device.

v0:
```python
import jax
import jax.numpy as jnp
from jax import lax
from jax.sharding import PartitionSpec as P

HEAD_TOTAL = 64
HEAD_DIM = 128


EPS = 1e-05


def prefix(part, axis, combine, identity):
    count = lax.axis_size(axis)
    place = lax.axis_index(axis)
    ahead = count - 1 - place
    gathered = jax.tree.map(lambda a: lax.all_gather(a, axis), part)
    state = jax.tree.map(lambda a, e: jnp.zeros_like(a) + jnp.asarray(e, a.dtype), part, identity)

    def one(lap, state):
        source = count - 1 - lap
        return combine(
            state, jax.tree.map(lambda a: lax.dynamic_index_in_dim(a, source, 0, False), gathered)
        )

    return lax.fori_loop(0, ahead, one, state)


def block_factors(log_rates, start_flags):
    cum_log = jnp.cumsum(log_rates, axis=1)
    doc_count = jnp.cumsum(start_flags)
    length = start_flags.shape[0]
    position = jnp.arange(length, dtype=jnp.int32)
    inside = (position[:, None] >= position[None, :]) & (doc_count[:, None] == doc_count[None, :])
    gap = cum_log[:, :, None] - cum_log[:, None, :]
    weight = jnp.where(inside[None], jnp.exp(jnp.minimum(gap, 0.0)), 0.0)
    entering = jnp.where(doc_count[None, :] == 0, jnp.exp(cum_log), 0.0)
    leaving = jnp.where(
        doc_count[None, :] == doc_count[-1], jnp.exp(cum_log[:, -1:] - cum_log), 0.0
    )
    carried = jnp.where(doc_count[-1] == 0, jnp.exp(cum_log[:, -1]), 0.0)
    return (weight, entering, leaving, carried)


def combine(earlier, later):
    return (earlier[0] * later[0], later[0][:, None, None] * earlier[1] + later[1])


def carry_factors(totals, my_index):
    shard_count = totals.shape[0]
    source = jnp.arange(shard_count, dtype=jnp.int32)[:, None]
    middle = jnp.arange(shard_count, dtype=jnp.int32)[None, :]
    between = (middle > source) & (middle < my_index)
    valid = source < my_index
    factor = jnp.prod(jnp.where(between[:, :, None], totals[None, :, :], 1.0), axis=1)
    return jnp.where(valid, factor, 0.0)


def per_device(queries, keys, values, cotangent, log_decay, starts):
    length, row_width = queries.shape
    head_count = log_decay.shape[0]
    head_dim = row_width // head_count
    full_width = HEAD_TOTAL * HEAD_DIM

    def by_head(array):
        return array.reshape(length, head_count, head_dim).transpose(1, 0, 2)

    def by_token(array):
        return array.transpose(1, 0, 2).reshape(length, row_width)

    query_heads = by_head(queries)
    key_heads = by_head(keys)
    value_heads = by_head(values)
    cotangent_heads = by_head(cotangent)

    def local_forward(pieces):
        query_head, key_head, value_head, log_rates = pieces
        weight, entering, leaving, carried = block_factors(log_rates[None], starts)
        scores = jnp.einsum("td,sd->ts", query_head, key_head, preferred_element_type=jnp.float32)
        weights_rounded = (scores * weight[0]).astype(jnp.bfloat16)
        intra_out = jnp.dot(weights_rounded, value_head, preferred_element_type=jnp.float32)
        keys_decayed = (leaving[0][:, None] * key_head).astype(jnp.bfloat16)
        update = jnp.einsum(
            "sd,se->de", keys_decayed, value_head, preferred_element_type=jnp.float32
        ).astype(jnp.bfloat16)
        return (weights_rounded, intra_out, update, entering[0], carried[0])

    weights_all, intra_out, update, entering, carried = lax.map(
        local_forward, (query_heads, key_heads, value_heads, log_decay)
    )
    unit_decay = jnp.ones((head_count,), jnp.float32)
    zero_state = jnp.zeros((head_count, head_dim, head_dim), jnp.float32)
    totals = lax.all_gather(carried[None, :], "seq", axis=0, tiled=True)
    factor = carry_factors(totals, lax.axis_index("seq"))
    prefix_state = jnp.sum(
        factor[:, :, None, None]
        * lax.all_gather(update[None], "seq", axis=0, tiled=True).astype(jnp.float32),
        axis=0,
    )
    state_rounded = prefix_state.astype(jnp.bfloat16)
    carried_out = jnp.einsum(
        "htd,hde->hte", query_heads, state_rounded, preferred_element_type=jnp.float32
    )
    outputs = intra_out + entering[:, :, None] * carried_out
    square_part = jnp.sum(outputs * outputs, axis=(0, 2))
    grad_part = jnp.sum(cotangent_heads * outputs, axis=(0, 2))
    square_sum = lax.psum(square_part, "head")
    inverse_scale = lax.rsqrt(square_sum / full_width + EPS)
    attn_heads = (outputs * inverse_scale[None, :, None]).astype(jnp.bfloat16)
    grad_sum = lax.psum(grad_part, "head")
    cubed = inverse_scale * inverse_scale * inverse_scale
    grad_out = (
        inverse_scale[None, :, None] * cotangent_heads
        - (cubed * grad_sum / full_width)[None, :, None] * outputs
    ).astype(jnp.bfloat16)
    queries_decayed = (entering[:, :, None] * query_heads).astype(jnp.bfloat16)
    grad_state = jnp.einsum(
        "htd,hte->hde", queries_decayed, grad_out, preferred_element_type=jnp.float32
    ).astype(jnp.bfloat16)
    decay_out, back_state = prefix(
        (carried, grad_state.astype(jnp.float32)), "seq", combine, (unit_decay, zero_state)
    )
    back_rounded = back_state.astype(jnp.bfloat16)

    def local_backward(pieces):
        (
            query_head,
            key_head,
            value_head,
            grad_head,
            log_rates,
            weights_rounded,
            state_head,
            back_head,
        ) = pieces
        weight, entering_one, leaving_one, carried_one = block_factors(log_rates[None], starts)
        grads_rounded = (
            jnp.einsum("td,sd->ts", grad_head, value_head, preferred_element_type=jnp.float32)
            * weight[0]
        ).astype(jnp.bfloat16)
        grad_query = jnp.dot(grads_rounded, key_head, preferred_element_type=jnp.float32)
        grad_query = grad_query + entering_one[0][:, None] * jnp.einsum(
            "te,de->td", grad_head, state_head, preferred_element_type=jnp.float32
        )
        grad_key = jnp.einsum(
            "ts,td->sd", grads_rounded, query_head, preferred_element_type=jnp.float32
        )
        grad_key = grad_key + leaving_one[0][:, None] * jnp.einsum(
            "se,de->sd", value_head, back_head, preferred_element_type=jnp.float32
        )
        grad_value = jnp.einsum(
            "ts,td->sd", weights_rounded, grad_head, preferred_element_type=jnp.float32
        )
        grad_value = grad_value + leaving_one[0][:, None] * jnp.einsum(
            "sd,de->se", key_head, back_head, preferred_element_type=jnp.float32
        )
        return (
            grad_query.astype(jnp.bfloat16),
            grad_key.astype(jnp.bfloat16),
            grad_value.astype(jnp.bfloat16),
        )

    grad_query, grad_key, grad_value = lax.map(
        local_backward,
        (
            query_heads,
            key_heads,
            value_heads,
            grad_out,
            log_decay,
            weights_all,
            state_rounded,
            back_rounded,
        ),
    )
    return (by_token(attn_heads), by_token(grad_query), by_token(grad_key), by_token(grad_value))


def solution(mesh):
    in_specs = (
        P("seq", "head"),
        P("seq", "head"),
        P("seq", "head"),
        P("seq", "head"),
        P("head", "seq"),
        P("seq"),
    )
    out_specs = (P("seq", "head"), P("seq", "head"), P("seq", "head"), P("seq", "head"))
    return jax.shard_map(
        per_device, mesh=mesh, in_specs=in_specs, out_specs=out_specs, check_vma=False
    )
```

profile of v0, /device:TPU:0, one launch (start us, length us, event | category | flops | bytes accessed | tf_op | source)
XLA Modules:
  0.0 713.0 jit_solution(2687192372985139560)
XLA Ops:
  8.4 2.9 copy.64
  11.3 2.4 copy.67
  13.7 3.9 copy.65
  17.6 3.9 copy.68
  21.5 3.9 copy.66
  25.4 3.9 copy.70
  29.4 186.4 %while.50 = (s32[]{:T(128)}, bf16[16,512,512]{2,1,0:T(8,128)(2,1)}, f32[16,512,128]{1,2,0:T(8,128)}, bf16[16,128,128]{2,1,0:T(8,128)(2,1)}, f32[16,512]{1,0:T(8,...) while((s32[]{:T(128)}, bf16[16,512,512]{2,1,0:T(8,128)(2,1)}, ...), condition=%wide.region_5.6_spmd, body=%wide.region_2.5_spmd.sunk | while | flops 153374736 | bytes 2575827 | solution.py:88
  33.5 2.2 bitcast_dynamic-update-slice_fusion.2
  45.2 2.2 bitcast_dynamic-update-slice_fusion.2
  56.9 2.2 bitcast_dynamic-update-slice_fusion.2
  80.2 2.2 bitcast_dynamic-update-slice_fusion.2
  91.8 2.2 bitcast_dynamic-update-slice_fusion.2
  115.1 2.2 bitcast_dynamic-update-slice_fusion.2
  126.8 2.2 bitcast_dynamic-update-slice_fusion.2
  138.4 2.2 bitcast_dynamic-update-slice_fusion.2
  161.7 2.2 bitcast_dynamic-update-slice_fusion.2
  173.4 2.2 bitcast_dynamic-update-slice_fusion.2
  185.1 2.2 bitcast_dynamic-update-slice_fusion.2
  208.3 2.2 bitcast_dynamic-update-slice_fusion.2
  217.4 23.4 %all-reduce = f32[128]{0:T(128)S(1)} all-reduce(f32[128]{0:T(128)S(1)} %dynamic-update-slice), channel_id=2, replica_groups=mesh['seq'=8,'head'=4] {'seq'}, use_global_device_ids=true, to_apply=%add | all-reduce | flops 128 | bytes 1024
  240.9 4.1 copy.74
  245.2 47.0 %all-gather.6.cloned.1.call-done = bf16[128,128,128]{2,1,0:T(8,128)(2,1)} async-done(((bf16[16,128,128]{2,1,0:T(8,128)(2,1)}), bf16[128,128,128]{2,1,0:T(8,128)(2,1)}) %all-gather.6.cloned.1.call-update) | async-done | bytes 4194320 | tf_op jit(solution)/shard_map/all_gather | solution.py:97
  292.2 3.2 fusion.69
  295.7 5.5 multiply_reduce_fusion
  301.1 5.6 all-reduce.1
  306.8 6.2 subtract_convert_fusion
  316.1 3.9 copy.84
  320.0 119.7 %all-gather.8.cloned.1.call-done = f32[128,128,128]{2,1,0:T(8,128)} async-done(((f32[16,128,128]{2,1,0:T(8,128)}), f32[128,128,128]{2,1,0:T(8,128)}) %all-gather.8.cloned.1.call-update) | async-done | bytes 8388624 | tf_op jit(solution)/shard_map/all_gather | solution.py:17
  439.8 10.5 %while.51 = (s32[]{:T(128)}, f32[16,128,128]{2,1,0:T(8,128)S(1)}, s32[]{:T(128)}, f32[8,16]{1,0:T(8,128)S(1)}, f32[8,16,128,128]{3,2,1,0:T(8,128)}, /*index=5*/s32[]{:T(128)}, s32[]{:T(128)}, s32[]{:T(128)}, s32[]{:T(128)}) while((s32[]{:T(128)}, f32[16,128,128]{2,1,0:T(8,128)S(1)}, s32[]{:T(128)}, f32[8,16]{1,0:T(8,128)S(1)}, ...), condition=%wide.region_13.14_spmd, body=%wide.region_12.13_spmd.sunk | while | flops 524294 | bytes 3146067 | solution.py:26
  450.3 249.8 %while.52 = (s32[]{:T(128)}, bf16[16,512,128]{2,1,0:T(8,128)(2,1)}, bf16[16,512,128]{2,1,0:T(8,128)(2,1)}, bf16[16,512,128]{2,1,0:T(8,128)(2,1)}, bf16[16,512,12...) while((s32[]{:T(128)}, bf16[16,512,128]{2,1,0:T(8,128)(2,1)}, ...), condition=%wide.region_17.18_spmd, body=%wide.region_14.17_spmd.sunk | while | flops 321522688 | bytes 5261185 | solution.py:163
  700.2 3.4 copy_bitcast_fusion.2
  703.5 2.6 copy_bitcast_fusion
  (648 shorter events, 384.9 us)
Async XLA Ops:
  7.2 285.1 %all-gather.6.cloned.1.call-start = ((), (), s32[]{:S(2)}) async-start(), calls=%async_computation | async-start | bytes 4718592 | tf_op jit(solution)/shard_map/all_gather | solution.py:97
  29.4 186.5 %copy-start.4 = (u32[32]{0:T(128)S(1)}, u32[32]{0:T(128)}, u32[]{:S(2)}) copy-start(u32[32]{0:T(128)} %constant.141) | copy-start | bytes 388
  215.8 223.9 %all-gather.8.cloned.1.call-start = ((), (), s32[]{:S(2)}) async-start(), calls=%async_computation.1 | async-start | bytes 9437184 | tf_op jit(solution)/shard_map/all_gather | solution.py:17
  292.2 3.4 copy-start
  313.0 1.4 copy-start.1
  700.2 3.4 copy-start.2
  700.2 3.4 copy-start.3
Sparse Core Ops, SparseCore 0:
  215.9 76.2 all-gather.5
  316.2 123.4 all-gather.7
where the time goes:
time: 720 us; the launch traced here: 713 us
  matrix products  272 us (38%)
  waiting for transfers between devices  167 us (23%)
  local copies, waits for them, and re-layouts  116 us (16%)
  other arithmetic  73 us (10%)
  loops' own time  41.5 us (6%)
  blocking collectives  29.1 us (4%)
  between operations  14.8 us (2%)
    all_gather x1, waiting for transfers between devices, prefix(): gathered = jax.tree.map(lambda a: lax.all_gather(a, axis), part)  120 us
    all_gather x1, waiting for transfers between devices, per_device(): lax.all_gather(update[None], 'seq', axis=0, tiled=True).astype(jnp.float32)  47 us
    dot_general x16, matrix products, local_forward(): jnp.einsum('td,sd->ts', query_head, key_head, preferred_element_type=jnp....  34.8 us
    select_n x32, other arithmetic, block_factors(): jnp.where(doc_count[None, :] == doc_count[-1], jnp.exp(cum_log[:, -1:] -...  31.1 us
    dot_general x16, matrix products, local_forward(): jnp.einsum('sd,se->de', keys_decayed, value_head, preferred_element_type=...  30.8 us
    dot_general x16, matrix products, local_forward(): jnp.dot(weights_rounded, value_head, preferred_element_type=jnp.float32)  30.8 us
    dot_general x16, matrix products, local_backward(): jnp.einsum('te,de->td', grad_head, state_head, preferred_element_type=jnp...  28.4 us
    dot_general x16, matrix products, local_backward(): jnp.einsum('se,de->sd', value_head, back_head, preferred_element_type=jnp...  28.1 us
  transfers between devices with their start and end apart: 2, of which 2 were waited for; matrix products, arithmetic and copies ran while one was open for 1% of the time, Pallas kernels for 0%

commit v1 on v0

v1 whole, which is shorter than its diff:
```python
import functools

import jax
import jax.numpy as jnp
from jax import lax
from jax.experimental import pallas as pl
from jax.experimental.pallas import tpu as pltpu
from jax.sharding import PartitionSpec as P

HEAD_TOTAL = 64
HEAD_DIM = 128
EPS = 1e-05
LOG2E = 1.4426950408889634
MASKED = -1e30
ROWS = 16
HALF = 256
F32 = jnp.float32
BF16 = jnp.bfloat16


def dot(a, b, dims=((1,), (0,))):
    return lax.dot_general(a, b, (dims, ((), ())), preferred_element_type=F32)


def dot_nt(a, b):
    return dot(a, b, ((1,), (1,)))


def running_sum(x):
    width = x.shape[1]
    lane = lax.broadcasted_iota(jnp.int32, x.shape, 1)
    step = 1
    while step < width:
        x = x + jnp.where(lane >= step, pltpu.roll(x, step, 1), 0.0)
        step *= 2
    return x


def three_parts(x):
    high = x.astype(BF16).astype(F32)
    rest = x - high
    middle = rest.astype(BF16).astype(F32)
    return high, middle, rest - middle


def block_mask(table, transposed):
    length = table.shape[1]
    row = table[ROWS - 1 :, :]
    column = table.T[:, ROWS - 1 :]
    down = lax.broadcasted_iota(jnp.int32, (length, length), 0)
    across = lax.broadcasted_iota(jnp.int32, (length, length), 1)
    order = (across >= down) if transposed else (down >= across)
    return jnp.where(order & (row == column), 0.0, MASKED)


def update_kernel(group, hpo, logs_ref, starts_ref, k_ref, v_ref, payload_ref, table_ref):
    step = pl.program_id(0)
    heads, length = logs_ref.shape
    dim = k_ref.shape[1] // group

    @pl.when(step == 0)
    def _():
        logs = running_sum(logs_ref[...]) * LOG2E
        count = running_sum(jnp.broadcast_to(starts_ref[...].astype(F32), (8, length)))[:1]
        enter = jnp.where(count == 0.0, jnp.exp2(logs), 0.0)
        last = slice(length - 1, length)
        leave = jnp.where(count == count[:, last], jnp.exp2(logs[:, last] - logs), 0.0)
        fill = jnp.broadcast_to(count, (ROWS - 3 * group, length))
        for g in range(heads // group):
            rows = slice(g * group, (g + 1) * group)
            table_ref[g] = jnp.concatenate([logs[rows], enter[rows], leave[rows], fill], axis=0)

    table = table_ref[step]
    columns = table.T
    carry = jnp.broadcast_to(table[group : 2 * group, length - 1 :], (group, dim))
    parts = three_parts(carry)
    line = lax.broadcasted_iota(jnp.int32, (ROWS, dim), 0)
    for owner in range(group // hpo):
        tile = jnp.zeros((ROWS, dim), F32)
        for i in range(hpo):
            h = owner * hpo + i
            lanes = slice(h * dim, (h + 1) * dim)
            decayed = (columns[:, 2 * group + h : 2 * group + h + 1] * k_ref[:, lanes].astype(F32)).astype(BF16)
            update = dot(decayed.T, v_ref[:, lanes])
            payload_ref[owner, i * dim : (i + 1) * dim, :] = update.astype(BF16)
            for j, part in enumerate(parts):
                tile = jnp.where(line == 3 * i + j, part[h : h + 1], tile)
        payload_ref[owner, hpo * dim :, :] = tile.astype(BF16)


def forward_scan_kernel(hpo, dim, in_ref, out_ref, carry_ref):
    state = [jnp.zeros((dim, dim), F32) for _ in range(hpo)]
    for b in range(in_ref.shape[0]):
        tile = in_ref[b, hpo * dim :, :].astype(F32)
        for i in range(hpo):
            rows = slice(i * dim, (i + 1) * dim)
            carry = tile[3 * i : 3 * i + 1] + tile[3 * i + 1 : 3 * i + 2] + tile[3 * i + 2 : 3 * i + 3]
            carry_ref[b, i : i + 1, :] = carry
            out_ref[b, rows, :] = state[i].astype(BF16)
            state[i] = carry * state[i] + in_ref[b, rows, :].astype(F32)


def backward_scan_kernel(hpo, dim, in_ref, carry_ref, out_ref):
    state = [jnp.zeros((dim, dim), F32) for _ in range(hpo)]
    for b in reversed(range(in_ref.shape[0])):
        for i in range(hpo):
            rows = slice(i * dim, (i + 1) * dim)
            out_ref[b, rows, :] = state[i].astype(BF16)
            state[i] = carry_ref[b, i : i + 1, :] * state[i] + in_ref[b, rows, :].astype(F32)


def intra_kernel(group, table_ref, q_ref, k_ref, v_ref, out_ref, mask_ref):
    length = q_ref.shape[0]
    dim = q_ref.shape[1] // group
    table = table_ref[0]

    @pl.when(pl.program_id(0) == 0)
    def _():
        mask_ref[...] = block_mask(table, False)

    columns = table.T
    for h in range(group):
        lanes = slice(h * dim, (h + 1) * dim)
        for first in range(0, length, HALF):
            rows, seen = slice(first, first + HALF), slice(0, first + HALF)
            scores = dot_nt(q_ref[rows, lanes], k_ref[seen, lanes])
            gap = columns[rows, h : h + 1] - table[h : h + 1, seen]
            weight = jnp.exp2(gap + mask_ref[rows, seen])
            out_ref[rows, lanes] = dot((scores * weight).astype(BF16), v_ref[seen, lanes])


def token_rows(total):
    length = total.shape[0]
    return jnp.concatenate(
        [jnp.sum(total[i : i + 128].T, axis=0, keepdims=True) for i in range(0, length, 128)], axis=0
    )


def output_kernel(group, table_ref, q_ref, state_ref, intra_ref, cot_ref, out_ref, sums_ref, square_ref, cross_ref):
    step = pl.program_id(0)
    dim = q_ref.shape[1] // group
    columns = table_ref[0].T

    @pl.when(step == 0)
    def _():
        square_ref[...] = jnp.zeros_like(square_ref)
        cross_ref[...] = jnp.zeros_like(cross_ref)

    square, cross = square_ref[...], cross_ref[...]
    for h in range(group):
        lanes = slice(h * dim, (h + 1) * dim)
        carried = dot(q_ref[:, lanes], state_ref[h])
        out = intra_ref[:, lanes] + columns[:, group + h : group + h + 1] * carried
        out_ref[:, lanes] = out
        square = square + out * out
        cross = cross + cot_ref[:, lanes].astype(F32) * out
    square_ref[...] = square
    cross_ref[...] = cross

    @pl.when(step == pl.num_programs(0) - 1)
    def _():
        sums_ref[...] = jnp.concatenate([token_rows(square), token_rows(cross)], axis=0)


def gout_kernel(group, hpo, count, *refs):
    sums_refs, refs = refs[:count], refs[count:]
    table_ref, q_ref, out_ref, cot_ref, attn_ref, gout_ref, payload_ref, factor_ref = refs
    dim = q_ref.shape[1] // group
    columns = table_ref[0].T

    @pl.when(pl.program_id(0) == 0)
    def _():
        total = sums_refs[0][...]
        for ref in sums_refs[1:]:
            total = total + ref[...]
        lines = total.shape[0] // 2
        full = HEAD_TOTAL * HEAD_DIM
        scale = lax.rsqrt(total[:lines] / full + EPS)
        slope = scale * scale * scale * total[lines:] / full
        turned = jnp.concatenate([scale, slope], axis=0).T
        for i in range(lines):
            rows = slice(i * 128, (i + 1) * 128)
            factor_ref[rows, 0:1] = turned[:, i : i + 1]
            factor_ref[rows, 1:2] = turned[:, lines + i : lines + i + 1]

    scale = factor_ref[:, 0:1]
    slope = factor_ref[:, 1:2]
    for h in range(group):
        lanes = slice(h * dim, (h + 1) * dim)
        out = out_ref[:, lanes]
        attn_ref[:, lanes] = (out * scale).astype(BF16)
        gout = (scale * cot_ref[:, lanes].astype(F32) - slope * out).astype(BF16)
        gout_ref[:, lanes] = gout
        decayed = (columns[:, group + h : group + h + 1] * q_ref[:, lanes].astype(F32)).astype(BF16)
        update = dot(decayed.T, gout)
        payload_ref[h // hpo, (h % hpo) * dim : (h % hpo + 1) * dim, :] = update.astype(BF16)


def gradient_kernel(group, table_ref, q_ref, k_ref, v_ref, gout_ref, state_ref, gq_ref, gk_ref, gv_ref, mask_ref):
    length = q_ref.shape[0]
    dim = q_ref.shape[1] // group
    table = table_ref[0]

    @pl.when(pl.program_id(0) == 0)
    def _():
        mask_ref[...] = block_mask(table, True)

    columns = table.T
    for h in range(group):
        lanes = slice(h * dim, (h + 1) * dim)
        pieces = []
        for first in range(0, length, HALF):
            rows, later = slice(first, first + HALF), slice(first, length)
            key, value = k_ref[rows, lanes], v_ref[rows, lanes]
            query, gout = q_ref[later, lanes], gout_ref[later, lanes]
            gap = table[h : h + 1, later] - columns[rows, h : h + 1]
            weight = jnp.exp2(gap + mask_ref[rows, later])
            probs = (dot_nt(key, query) * weight).astype(BF16)
            gv_ref[rows, lanes] = dot(probs, gout)
            grads = (dot_nt(value, gout) * weight).astype(BF16)
            gk_ref[rows, lanes] = dot(grads, query)
            pieces.append(dot(key.T, grads))
        carried = dot_nt(gout_ref[:, lanes], state_ref[h])
        for first in range(0, length, HALF):
            rows = slice(first, first + HALF)
            total = pieces[0][:, first : first + HALF]
            for i in range(1, first // HALF + 1):
                total = total + pieces[i][:, first - i * HALF : first - (i - 1) * HALF]
            enter = columns[rows, group + h : group + h + 1]
            gq_ref[rows, lanes] = (total.T + enter * carried[rows]).astype(BF16)


def final_kernel(group, table_ref, k_ref, v_ref, back_ref, gkp_ref, gvp_ref, gk_ref, gv_ref):
    dim = k_ref.shape[1] // group
    columns = table_ref[0].T
    for h in range(group):
        lanes = slice(h * dim, (h + 1) * dim)
        leave = columns[:, 2 * group + h : 2 * group + h + 1]
        gk_ref[:, lanes] = (gkp_ref[:, lanes] + leave * dot_nt(v_ref[:, lanes], back_ref[h])).astype(BF16)
        gv_ref[:, lanes] = (gvp_ref[:, lanes] + leave * dot(k_ref[:, lanes], back_ref[h])).astype(BF16)


def per_device(queries, keys, values, cotangent, log_decay, starts):
    length, width = queries.shape
    heads = log_decay.shape[0]
    dim = width // heads
    blocks = lax.axis_size("seq")
    shares = lax.axis_size("head")
    hpo = -(-heads // blocks)
    group = min(4, heads)
    groups = heads // group
    params = pltpu.CompilerParams(dimension_semantics=("arbitrary",), vmem_limit_bytes=48 << 20)

    wide = pl.BlockSpec((length, group * dim), lambda g: (0, g))
    table_spec = pl.BlockSpec((1, ROWS, length), lambda g: (g, 0, 0))
    state_spec = pl.BlockSpec((group, dim, dim), lambda g: (g, 0, 0))

    def whole(*shape):
        return pl.BlockSpec(shape, lambda g: (0,) * len(shape))

    def array(dtype):
        return jax.ShapeDtypeStruct((length, width), dtype)

    def cost(products, moved, exps=0):
        return pl.CostEstimate(flops=2 * heads * products, bytes_accessed=moved * length * width, transcendentals=heads * exps)

    big, small = length * length * dim, length * dim * dim
    payload, table = pl.pallas_call(
        functools.partial(update_kernel, group, hpo),
        grid=(groups,),
        in_specs=[whole(heads, length), whole(1, length), wide, wide],
        out_specs=[
            pl.BlockSpec((group // hpo, hpo * dim + ROWS, dim), lambda g: (g, 0, 0)),
            whole(groups, ROWS, length),
        ],
        out_shape=[
            jax.ShapeDtypeStruct((blocks, hpo * dim + ROWS, dim), BF16),
            jax.ShapeDtypeStruct((groups, ROWS, length), F32),
        ],
        compiler_params=params,
        cost_estimate=cost(small, 4),
        name="update",
    )(log_decay, starts.reshape(1, length), keys, values)

    received = lax.all_to_all(payload, "seq", 0, 0)

    intra = pl.pallas_call(
        functools.partial(intra_kernel, group),
        grid=(groups,),
        in_specs=[table_spec, wide, wide, wide],
        out_specs=wide,
        out_shape=array(F32),
        scratch_shapes=[pltpu.VMEM((length, length), F32)],
        compiler_params=params,
        cost_estimate=cost(2 * big, 10, length * length),
        name="intra",
    )(table, queries, keys, values)

    states, carries = pl.pallas_call(
        functools.partial(forward_scan_kernel, hpo, dim),
        out_shape=[
            jax.ShapeDtypeStruct((blocks, hpo * dim, dim), BF16),
            jax.ShapeDtypeStruct((blocks, 8, dim), F32),
        ],
        compiler_params=pltpu.CompilerParams(vmem_limit_bytes=48 << 20),
        name="forward_scan",
    )(received)
    states = lax.all_to_all(states, "seq", 0, 0).reshape(blocks * hpo, dim, dim)

    lines = 2 * length // 128
    outputs, sums = pl.pallas_call(
        functools.partial(output_kernel, group),
        grid=(groups,),
        in_specs=[table_spec, wide, state_spec, wide, wide],
        out_specs=[wide, whole(lines, 128)],
        out_shape=[array(F32), jax.ShapeDtypeStruct((lines, 128), F32)],
        scratch_shapes=[pltpu.VMEM((length, dim), F32)] * 2,
        compiler_params=params,
        cost_estimate=cost(small, 12),
        name="output",
    )(table, queries, states, intra, cotangent)

    everyone = [sums] + [
        lax.ppermute(sums, "head", [(i, (i + k) % shares) for i in range(shares)]) for k in range(1, shares)
    ]

    attn, gout, payload = pl.pallas_call(
        functools.partial(gout_kernel, group, hpo, shares),
        grid=(groups,),
        in_specs=[whole(lines, 128)] * shares + [table_spec, wide, wide, wide],
        out_specs=[wide, wide, pl.BlockSpec((group // hpo, hpo * dim, dim), lambda g: (g, 0, 0))],
        out_shape=[array(BF16), array(BF16), jax.ShapeDtypeStruct((blocks, hpo * dim, dim), BF16)],
        scratch_shapes=[pltpu.VMEM((length, 2), F32)],
        compiler_params=params,
        cost_estimate=cost(small, 12),
        name="gout",
    )(*everyone, table, queries, outputs, cotangent)

    received = lax.all_to_all(payload, "seq", 0, 0)

    gq, gk_part, gv_part = pl.pallas_call(
        functools.partial(gradient_kernel, group),
        grid=(groups,),
        in_specs=[table_spec, wide, wide, wide, wide, state_spec],
        out_specs=[wide, wide, wide],
        out_shape=[array(BF16), array(F32), array(F32)],
        scratch_shapes=[pltpu.VMEM((length, length), F32)],
        compiler_params=params,
        cost_estimate=cost(5 * big + small, 18, length * length),
        name="gradient",
    )(table, queries, keys, values, gout, states)

    back = pl.pallas_call(
        functools.partial(backward_scan_kernel, hpo, dim),
        out_shape=jax.ShapeDtypeStruct((blocks, hpo * dim, dim), BF16),
        compiler_params=pltpu.CompilerParams(vmem_limit_bytes=48 << 20),
        name="backward_scan",
    )(received, carries)
    back = lax.all_to_all(back, "seq", 0, 0).reshape(blocks * hpo, dim, dim)

    gk, gv = pl.pallas_call(
        functools.partial(final_kernel, group),
        grid=(groups,),
        in_specs=[table_spec, wide, wide, state_spec, wide, wide],
        out_specs=[wide, wide],
        out_shape=[array(BF16), array(BF16)],
        compiler_params=params,
        cost_estimate=cost(2 * small, 16),
        name="final",
    )(table, keys, values, back, gk_part, gv_part)
    return (attn, gq, gk, gv)


def solution(mesh):
    wide = P("seq", "head")
    return jax.shard_map(
        per_device,
        mesh=mesh,
        in_specs=(wide, wide, wide, wide, P("head", "seq"), P("seq")),
        out_specs=(wide, wide, wide, wide),
        check_vma=False,
    )
```

time: 720 us -> 121 us (0.17)
  matrix products: 272 us -> 0 us
  waiting for transfers between devices: 167 us -> 6.05 us
  local copies, waits for them, and re-layouts: 116 us -> 14.7 us
  other arithmetic: 73 us -> 0 us
  Pallas kernels: 0 us -> 50.3 us
  loops' own time: 41.5 us -> 0 us
  between operations: 14.8 us -> 0.72 us
  blocking collectives: 29.1 us -> 39.8 us
  starting transfers between devices: 0.08 us -> 8.88 us
    dot_general x162 -> x0, matrix products: 272 us -> none  [the longest x16 34.8 us: local_forward(): jnp.einsum('td,sd->ts', query_head, key_head, preferred_element_type=jnp....]
    all_gather x2 -> x0, waiting for transfers between devices: 167 us -> none  [the longest x1 120 us: prefix(): gathered = jax.tree.map(lambda a: lax.all_gather(a, axis), part)]
    pallas_call x0 -> x8, Pallas kernels: none -> 50.3 us  [the longest x1 16.2 us: per_device(): pl.pallas_call(functools.partial(gradient_kernel, group), grid=(groups,),...]
    slice x80 -> x0, local copies, waits for them, and re-layouts: 46.2 us -> none  [the longest x48 27.5 us: block_factors(): cum_log[:, -1:] - cum_log]
    another operation x3 -> x0, loops' own time: 41.5 us -> none  [the longest x1 21.3 us: per_device(): lax.map(local_forward, (query_heads, key_heads, value_heads, log_decay))]
    all_to_all x0 -> x2, blocking collectives: none -> 39.8 us  [per_device(): received = lax.all_to_all(payload, 'seq', 0, 0)]
    select_n x65 -> x0, other arithmetic: 31.4 us -> none  [the longest x32 31.1 us: block_factors(): jnp.where(doc_count[None, :] == doc_count[-1], jnp.exp(cum_log[:, -1:] -...]
    unnamed x1 -> x0, blocking collectives: 23.4 us -> none
  transfers between devices with their start and end apart: 2 -> 5, of which waited for: 2 -> 3; matrix products, arithmetic and copies ran while one was open for 1% -> 0% of each run, Pallas kernels for 0% -> 21%
where the time goes in v1:
time: 121 us; the launch traced here: 120 us
  Pallas kernels  50.3 us (42%)
  blocking collectives  39.8 us (33%)
  local copies, waits for them, and re-layouts  14.7 us (12%)
  starting transfers between devices  8.88 us (7%)
  waiting for transfers between devices  6.05 us (5%)
    all_to_all x2, blocking collectives, per_device(): received = lax.all_to_all(payload, 'seq', 0, 0)  39.8 us
    pallas_call x1, Pallas kernels, per_device(): pl.pallas_call(functools.partial(gradient_kernel, group), grid=(groups,),...  16.2 us
    unnamed x24, local copies, waits for them, and re-layouts  14.7 us
    pallas_call x1, Pallas kernels, per_device(): pl.pallas_call(functools.partial(intra_kernel, group), grid=(groups,), in...  8.91 us
    pallas_call x1, Pallas kernels, per_device(): pl.pallas_call(functools.partial(gout_kernel, group, hpo, shares), grid=(...  6.79 us
    pallas_call x1, Pallas kernels, per_device(): pl.pallas_call(functools.partial(final_kernel, group), grid=(groups,), in...  6.69 us
    pallas_call x1, Pallas kernels, per_device(): pl.pallas_call(functools.partial(output_kernel, group), grid=(groups,), i...  6.22 us
    pallas_call x1, Pallas kernels, per_device(): pl.pallas_call(functools.partial(update_kernel, group, hpo), grid=(groups...  4.47 us
  transfers between devices with their start and end apart: 5, of which 3 were waited for; matrix products, arithmetic and copies ran while one was open for 0% of the time, Pallas kernels for 21%

profile of v1, /device:TPU:0, one launch (start us, length us, event | category | flops | bytes accessed | tf_op | source)
XLA Modules:
  0.0 120.5 jit_solution(2125804317301684684)
XLA Ops:
  0.6 0.0 copy-start.1
  0.6 1.6 %copy-done.1 = bf16[512,2048]{1,0:T(8,128)(2,1)S(1)} copy-done((bf16[512,2048]{1,0:T(8,128)(2,1)S(1)}, bf16[512,2048]{1,0:T(8,128)(2,1)}, u32[]{:S(2)}) %copy-start.1) | copy-done | bytes 2097176
  2.2 1.6 %copy-done.5 = bf16[512,2048]{1,0:T(8,128)(2,1)S(1)} copy-done((bf16[512,2048]{1,0:T(8,128)(2,1)S(1)}, bf16[512,2048]{1,0:T(8,128)(2,1)}, u32[]{:S(2)}) %copy-start.5) | copy-done | bytes 2097176
  3.8 0.8 copy-done.9
  4.6 0.7 copy-done.10
  5.3 4.5 %update.1 = (bf16[8,272,128]{2,1,0:T(8,128)(2,1)S(1)}, f32[4,16,512]{2,1,0:T(8,128)S(1)}) custom-call(f32[16,512]{1,0:T(8,128)S(1)} %copy-done.9, s32[1,512]{1,0:T(1,128)S(1)} %bitcast.6, bf16[512,2048]{1,0:T(8,128)(2,1)S(1)} %copy-done.1, bf16[512,2048]{1,0:T(8,128)(2,1)S(1)} %copy-done.5), custom_call_target="tpu_custom_call" | custom-call | flops 268435456 | bytes 4194304 | tf_op jit(solution)/shard_map/update/pallas_call | solution.py:268
  9.7 0.0 copy-start
  9.7 23.2 %all_to_all.20.in_ref = bf16[8,272,128]{2,1,0:T(8,128)(2,1)S(1)} all-to-all(bf16[8,272,128]{2,1,0:T(8,128)(2,1)S(1)} %get-tuple-element.19), channel_id=1, replica_groups=mesh['seq'=8,'head'=4] {'seq'}, dimensions={0} | all-to-all | bytes 1114112 | tf_op jit(solution)/shard_map/all_to_all | solution.py:285
  32.9 0.9 forward_scan.1
  33.8 3.5 %all-to-all-start.1 = ((bf16[8,256,128]{2,1,0:T(8,128)(2,1)}), bf16[8,256,128]{2,1,0:T(8,128)(2,1)S(1)}, u32[]{:S(2)}, u32[]{:S(2)}) async-start(bf16[8,256,128]{2,1,0:T(8,128)(2,1)} %get-tuple-element.20), calls=%async_computation.1 | async-start | bytes 1048576 | tf_op jit(solution)/shard_map/all_to_all | solution.py:308
  37.4 0.0 copy-start.2
  37.4 1.6 %copy-done.2 = bf16[512,2048]{1,0:T(8,128)(2,1)S(1)} copy-done((bf16[512,2048]{1,0:T(8,128)(2,1)S(1)}, bf16[512,2048]{1,0:T(8,128)(2,1)}, u32[]{:S(2)}) %copy-start.2) | copy-done | bytes 2097176
  38.9 8.9 %intra.1.intra_ref = f32[512,2048]{1,0:T(8,128)} custom-call(f32[4,16,512]{2,1,0:T(8,128)S(1)} %get-tuple-element.18.table_ref.refs_4_, bf16[512,2048]{1,0:T(8,128)(2,1)S(1)} %copy-done, bf16[512,2048]{1,0:T(8,128)(2,1)S(1)} %copy-done.2, bf16[512,2048]{1,0:T(8,128)(2,1)} %v_ref.7), custom_call_target="tpu_custom_call" | custom-call | flops 2147483648 | bytes 10485760 | tf_op jit(solution)/shard_map/intra/pallas_call | solution.py:287
  47.9 3.2 %all-to-all-done.1 = bf16[8,256,128]{2,1,0:T(8,128)(2,1)S(1)} async-done(((bf16[8,256,128]{2,1,0:T(8,128)(2,1)}), bf16[8,256,128]{2,1,0:T(8,128)(2,1)S(1)}, u32[]{:S(2)}, u32[]{:S(2)}) %all-to-all-start.1) | async-done | bytes 524320 | tf_op jit(solution)/shard_map/all_to_all | solution.py:308
  51.1 1.6 %copy-done.7 = bf16[512,2048]{1,0:T(8,128)(2,1)S(1)} copy-done((bf16[512,2048]{1,0:T(8,128)(2,1)S(1)}, bf16[512,2048]{1,0:T(8,128)(2,1)}, u32[]{:S(2)}) %copy-start.7) | copy-done | bytes 2097176
  52.7 6.2 %output.1 = (f32[512,2048]{1,0:T(8,128)}, f32[8,128]{1,0:T(8,128)S(1)}) custom-call(f32[4,16,512]{2,1,0:T(8,128)S(1)} %get-tuple-element.18.table_ref.refs_4_, bf16[512,2048]{1,0:T(8,128)(2,1)S(1)} %copy-done, bf16[16,128,128]{2,1,0:T(8,128)(2,1)S(1)} %bitcast.3, f32[512,2048]{1,0:T(8,128)} %intra.1.intra_ref, bf16[512,2048]{1,0:T(8,128)(2,1)S(1)} %copy-done.7), custom_call_target="tpu_custom_call" | custom-call | flops 268435456 | bytes 12582912 | tf_op jit(solution)/shard_map/output/pallas_call | solution.py:311
  58.9 1.5 %collective-permute-start.1 = (f32[8,128]{1,0:T(8,128)S(1)}, f32[8,128]{1,0:T(8,128)S(1)}, u32[]{:S(2)}, u32[]{:S(2)}) collective-permute-start(f32[8,128]{1,0:T(8,128)S(1)} %get-tuple-element.21.refs_0_), channel_id=1, source_target_pairs={{0,2},{1,3},{2,0},{3,1},{4,6},{5,7},{6,4},{7,5},{8,10},{9,11},{10,... | collective-permute-start | bytes 12296 | tf_op jit(solution)/shard_map/ppermute | solution.py:324
  60.4 0.2 collective-permute-start
  60.7 1.9 %collective-permute-done.1.refs_2_ = f32[8,128]{1,0:T(8,128)S(1)} collective-permute-done((f32[8,128]{1,0:T(8,128)S(1)}, f32[8,128]{1,0:T(8,128)S(1)}, u32[]{:S(2)}, u32[]{:S(2)}) %collective-permute-start.1) | collective-permute-done | bytes 4128 | tf_op jit(solution)/shard_map/ppermute | solution.py:324
  62.5 0.9 collective-permute-done.refs_1_
  63.5 6.8 %gout.1 = (bf16[512,2048]{1,0:T(8,128)(2,1)}, bf16[512,2048]{1,0:T(8,128)(2,1)S(1)}, bf16[8,256,128]{2,1,0:T(8,128)(2,1)S(1)}) custom-call(f32[8,128]{1,0:T(8,128)S(1)} %get-tuple-element.21.refs_0_, f32[8,128]{1,0:T(8,128)S(1)} %collective-permute-done.refs_1_, f32[8,128]{1,0:T(8,128)S(1)} %collective-permute-done.1.refs_2_, ...), custom_call_target="tpu_custom_call" | custom-call | flops 268435456 | bytes 12582912 | tf_op jit(solution)/shard_map/gout/pallas_call | solution.py:327
  70.3 1.3 %copy-done.11 = bf16[512,2048]{1,0:T(8,128)(2,1)} copy-done((bf16[512,2048]{1,0:T(8,128)(2,1)}, bf16[512,2048]{1,0:T(8,128)(2,1)S(1)}, u32[]{:S(2)}) %copy-start.11) | copy-done | bytes 2097176
  71.6 16.7 %all_to_all.21.in_ref = bf16[8,256,128]{2,1,0:T(8,128)(2,1)S(1)} all-to-all(bf16[8,256,128]{2,1,0:T(8,128)(2,1)S(1)} %get-tuple-element.26), channel_id=1, replica_groups=mesh['seq'=8,'head'=4] {'seq'}, dimensions={0} | all-to-all | bytes 1048576 | tf_op jit(solution)/shard_map/all_to_all | solution.py:339
  88.2 0.1 backward_scan.1
  88.3 0.0 copy-start.8
  88.4 0.8 copy-done.8
  89.1 3.6 %all-to-all-start.3 = ((bf16[8,256,128]{2,1,0:T(8,128)(2,1)}), bf16[8,256,128]{2,1,0:T(8,128)(2,1)S(1)}, u32[]{:S(2)}, u32[]{:S(2)}) async-start(bf16[8,256,128]{2,1,0:T(8,128)(2,1)} %copy-done.8), calls=%async_computation.3 | async-start | bytes 1048576 | tf_op jit(solution)/shard_map/all_to_all | solution.py:359
  92.8 1.6 %copy-done.3 = bf16[512,2048]{1,0:T(8,128)(2,1)S(1)} copy-done((bf16[512,2048]{1,0:T(8,128)(2,1)S(1)}, bf16[512,2048]{1,0:T(8,128)(2,1)}, u32[]{:S(2)}) %copy-start.3) | copy-done | bytes 2097176
  94.4 16.2 %gradient.1 = (bf16[512,2048]{1,0:T(8,128)(2,1)}, f32[512,2048]{1,0:T(8,128)}, f32[512,2048]{1,0:T(8,128)}) custom-call(f32[4,16,512]{2,1,0:T(8,128)S(1)} %get-tuple-element.18.table_ref.refs_4_, bf16[512,2048]{1,0:T(8,128)(2,1)S(1)} %copy-done, bf16[512,2048]{1,0:T(8,128)(2,1)S(1)} %copy-done.3, bf16[512,2048]{1,0:T(8,128)(2,1)} %v_ref.7, ...), custom_call_target="tpu_custom_call" | custom-call | flops 5637144576 | bytes 18874368 | tf_op jit(solution)/shard_map/gradient/pallas_call | solution.py:341
  110.6 1.6 %copy-done.4 = bf16[512,2048]{1,0:T(8,128)(2,1)S(1)} copy-done((bf16[512,2048]{1,0:T(8,128)(2,1)S(1)}, bf16[512,2048]{1,0:T(8,128)(2,1)}, u32[]{:S(2)}) %copy-start.4) | copy-done | bytes 2097176
  112.2 1.6 %copy-done.6 = bf16[512,2048]{1,0:T(8,128)(2,1)S(1)} copy-done((bf16[512,2048]{1,0:T(8,128)(2,1)S(1)}, bf16[512,2048]{1,0:T(8,128)(2,1)}, u32[]{:S(2)}) %copy-start.6) | copy-done | bytes 2097176
  113.8 6.7 %final.1 = (bf16[512,2048]{1,0:T(8,128)(2,1)}, bf16[512,2048]{1,0:T(8,128)(2,1)}) custom-call(f32[4,16,512]{2,1,0:T(8,128)S(1)} %get-tuple-element.18.table_ref.refs_4_, bf16[512,2048]{1,0:T(8,128)(2,1)S(1)} %copy-done.4, bf16[512,2048]{1,0:T(8,128)(2,1)S(1)} %copy-done.6, bf16[16,128,128]{2,1,0:T(8,128)(2,1)S(1)} %bitcast.5, ...), custom_call_target="tpu_custom_call" | custom-call | flops 536870912 | bytes 16777216 | tf_op jit(solution)/shard_map/final/pallas_call | solution.py:361
  (12 shorter events, 0.0 us)
Async XLA Ops:
  0.6 1.6 %copy-start.1 = (bf16[512,2048]{1,0:T(8,128)(2,1)S(1)}, bf16[512,2048]{1,0:T(8,128)(2,1)}, u32[]{:S(2)}) copy-start(bf16[512,2048]{1,0:T(8,128)(2,1)} %k_ref.7) | copy-start | bytes 6291460
  2.2 1.6 %copy-start.5 = (bf16[512,2048]{1,0:T(8,128)(2,1)S(1)}, bf16[512,2048]{1,0:T(8,128)(2,1)}, u32[]{:S(2)}) copy-start(bf16[512,2048]{1,0:T(8,128)(2,1)} %v_ref.7) | copy-start | bytes 6291460
  3.8 0.8 copy-start.9
  4.6 0.7 copy-start.10
  9.7 27.6 %copy-start = (bf16[512,2048]{1,0:T(8,128)(2,1)S(1)}, bf16[512,2048]{1,0:T(8,128)(2,1)}, u32[]{:S(2)}) copy-start(bf16[512,2048]{1,0:T(8,128)(2,1)} %q_ref.5) | copy-start | bytes 6291460
  33.8 17.3 %all-to-all-start.1 = ((bf16[8,256,128]{2,1,0:T(8,128)(2,1)}), bf16[8,256,128]{2,1,0:T(8,128)(2,1)S(1)}, u32[]{:S(2)}, u32[]{:S(2)}) async-start(bf16[8,256,128]{2,1,0:T(8,128)(2,1)} %get-tuple-element.20), calls=%async_computation.1 | async-start | bytes 1048576 | tf_op jit(solution)/shard_map/all_to_all | solution.py:308
  37.4 1.6 %copy-start.2 = (bf16[512,2048]{1,0:T(8,128)(2,1)S(1)}, bf16[512,2048]{1,0:T(8,128)(2,1)}, u32[]{:S(2)}) copy-start(bf16[512,2048]{1,0:T(8,128)(2,1)} %k_ref.7) | copy-start | bytes 6291460
  51.1 1.6 %copy-start.7 = (bf16[512,2048]{1,0:T(8,128)(2,1)S(1)}, bf16[512,2048]{1,0:T(8,128)(2,1)}, u32[]{:S(2)}) copy-start(bf16[512,2048]{1,0:T(8,128)(2,1)} %refs_7_.1) | copy-start | bytes 6291460
  58.9 1.8 %collective-permute-start.2 = (f32[8,128]{1,0:T(8,128)S(1)}, f32[8,128]{1,0:T(8,128)S(1)}, u32[]{:S(2)}, u32[]{:S(2)}) collective-permute-start(f32[8,128]{1,0:T(8,128)S(1)} %get-tuple-element.21.refs_0_), channel_id=1, source_target_pairs={{0,3},{1,0},{2,1},{3,2},{4,7},{5,4},{6,5},{7,6},{8,11},{9,8},{10,9... | collective-permute-start | bytes 12296 | tf_op jit(solution)/shard_map/ppermute | solution.py:324
  58.9 3.6 %collective-permute-start.1 = (f32[8,128]{1,0:T(8,128)S(1)}, f32[8,128]{1,0:T(8,128)S(1)}, u32[]{:S(2)}, u32[]{:S(2)}) collective-permute-start(f32[8,128]{1,0:T(8,128)S(1)} %get-tuple-element.21.refs_0_), channel_id=1, source_target_pairs={{0,2},{1,3},{2,0},{3,1},{4,6},{5,7},{6,4},{7,5},{8,10},{9,11},{10,... | collective-permute-start | bytes 12296 | tf_op jit(solution)/shard_map/ppermute | solution.py:324
  60.4 3.0 %collective-permute-start = (f32[8,128]{1,0:T(8,128)S(1)}, f32[8,128]{1,0:T(8,128)S(1)}, u32[]{:S(2)}, u32[]{:S(2)}) collective-permute-start(f32[8,128]{1,0:T(8,128)S(1)} %get-tuple-element.21.refs_0_), channel_id=1, source_target_pairs={{0,1},{1,2},{2,3},{3,0},{4,5},{5,6},{6,7},{7,4},{8,9},{9,10},{10,1... | collective-permute-start | bytes 12296 | tf_op jit(solution)/shard_map/ppermute | solution.py:324
  70.3 1.3 %copy-start.11 = (bf16[512,2048]{1,0:T(8,128)(2,1)}, bf16[512,2048]{1,0:T(8,128)(2,1)S(1)}, u32[]{:S(2)}) copy-start(bf16[512,2048]{1,0:T(8,128)(2,1)S(1)} %get-tuple-element.24.gout_ref) | copy-start | bytes 6291460
  88.3 0.8 copy-start.8
  89.1 21.5 %all-to-all-start.3 = ((bf16[8,256,128]{2,1,0:T(8,128)(2,1)}), bf16[8,256,128]{2,1,0:T(8,128)(2,1)S(1)}, u32[]{:S(2)}, u32[]{:S(2)}) async-start(bf16[8,256,128]{2,1,0:T(8,128)(2,1)} %copy-done.8), calls=%async_computation.3 | async-start | bytes 1048576 | tf_op jit(solution)/shard_map/all_to_all | solution.py:359
  92.8 1.6 %copy-start.3 = (bf16[512,2048]{1,0:T(8,128)(2,1)S(1)}, bf16[512,2048]{1,0:T(8,128)(2,1)}, u32[]{:S(2)}) copy-start(bf16[512,2048]{1,0:T(8,128)(2,1)} %k_ref.7) | copy-start | bytes 6291460
  110.6 1.6 %copy-start.4 = (bf16[512,2048]{1,0:T(8,128)(2,1)S(1)}, bf16[512,2048]{1,0:T(8,128)(2,1)}, u32[]{:S(2)}) copy-start(bf16[512,2048]{1,0:T(8,128)(2,1)} %k_ref.7) | copy-start | bytes 6291460
  112.2 1.6 %copy-start.6 = (bf16[512,2048]{1,0:T(8,128)(2,1)S(1)}, bf16[512,2048]{1,0:T(8,128)(2,1)}, u32[]{:S(2)}) copy-start(bf16[512,2048]{1,0:T(8,128)(2,1)} %v_ref.7) | copy-start | bytes 6291460

commit v2 on v0

v2 whole, which is shorter than its diff:
```python
import functools

import jax
import jax.numpy as jnp
from jax import lax
from jax.experimental import pallas as pl
from jax.experimental.pallas import tpu as pltpu
from jax.sharding import PartitionSpec as P

HEAD_TOTAL = 64
HEAD_DIM = 128
EPS = 1e-05
LOG2E = 1.4426950408889634
MASKED = -1e30
ROWS = 16
HALF = 256
F32 = jnp.float32
BF16 = jnp.bfloat16


def dot(a, b, dims=((1,), (0,))):
    return lax.dot_general(a, b, (dims, ((), ())), preferred_element_type=F32)


def dot_nt(a, b):
    return dot(a, b, ((1,), (1,)))


def running_sum(x):
    width = x.shape[1]
    lane = lax.broadcasted_iota(jnp.int32, x.shape, 1)
    step = 1
    while step < width:
        x = x + jnp.where(lane >= step, pltpu.roll(x, step, 1), 0.0)
        step *= 2
    return x


def three_parts(x):
    high = x.astype(BF16).astype(F32)
    rest = x - high
    middle = rest.astype(BF16).astype(F32)
    return high, middle, rest - middle


def lanes_of(index, size):
    return pl.ds(index * size if isinstance(index, int) else pl.multiple_of(index * size, size), size)


def send_to(place, slot, size):
    return place ^ slot if size & (size - 1) == 0 else lax.rem(place + slot, size)


def sent_by(place, slot, size):
    return place ^ slot if size & (size - 1) == 0 else lax.rem(place + size - slot, size)


def my_place(size):
    return lax.rem(lax.axis_index("seq"), size)


def block_mask(table, transposed):
    length = table.shape[1]
    row = table[ROWS - 1 :, :]
    column = table.T[:, ROWS - 1 :]
    down = lax.broadcasted_iota(jnp.int32, (length, length), 0)
    across = lax.broadcasted_iota(jnp.int32, (length, length), 1)
    order = (across >= down) if transposed else (down >= across)
    return jnp.where(order & (row == column), 0.0, MASKED)


def update_kernel(group, hpo, size, logs_hbm, starts_hbm, k_hbm, v_hbm, q_hbm, *refs):
    sent_refs, refs = refs[:size], refs[size:]
    table_ref, rows_ref, k_ref, v_ref, q_ref, logs_ref, starts_ref, sems = refs
    heads, length = logs_ref.shape
    dim = k_ref.shape[1] // heads
    pairs = ((logs_hbm, logs_ref), (starts_hbm, starts_ref), (k_hbm, k_ref), (v_hbm, v_ref), (q_hbm, q_ref))
    copies = [pltpu.make_async_copy(a, b, sems.at[i]) for i, (a, b) in enumerate(pairs)]
    for copy in copies[:4]:
        copy.start()
    copies[0].wait()
    copies[1].wait()

    flags = jnp.broadcast_to(starts_ref[...].astype(F32), (8, length))
    sums = running_sum(jnp.concatenate([logs_ref[...], flags], axis=0))
    logs, count = sums[:heads] * LOG2E, sums[heads : heads + 1]
    last = slice(length - 1, length)
    enter = jnp.where(count == 0.0, jnp.exp2(logs), 0.0)
    leave = jnp.where(count == count[:, last], jnp.exp2(logs[:, last] - logs), 0.0)
    fill = jnp.broadcast_to(count, (ROWS - 3 * group, length))
    for g in range(heads // group):
        rows = slice(g * group, (g + 1) * group)
        table_ref[g] = jnp.concatenate([logs[rows], enter[rows], leave[rows], fill], axis=0)
    for h in range(heads):
        rows_ref[h] = enter[h : h + 1]
        rows_ref[heads + h] = leave[h : h + 1]
    line = lax.broadcasted_iota(jnp.int32, (ROWS, dim), 0)
    copies[2].wait()
    copies[3].wait()
    copies[4].start()

    me = my_place(size)
    for slot, sent_ref in enumerate(sent_refs):
        owner = send_to(me, slot, size)

        @pl.when(owner * hpo < heads)
        def _():
            tile = jnp.zeros((ROWS, dim), F32)
            for i in range(hpo):
                head = owner * hpo + i
                lanes = lanes_of(head, dim)
                turned = k_ref[:, lanes].T.astype(F32)
                decayed = (turned * rows_ref[heads + head]).astype(BF16)
                sent_ref[i * dim : (i + 1) * dim, :] = dot(decayed, v_ref[:, lanes]).astype(BF16)
                carry = rows_ref[head][:, length - 1 :]
                for j, part in enumerate(three_parts(jnp.broadcast_to(carry, (ROWS, dim)))):
                    tile = jnp.where(line == 3 * i + j, part, tile)
            sent_ref[hpo * dim :, :] = tile.astype(BF16)

    copies[4].wait()


def scan_kernel(hpo, size, forward, *refs):
    in_refs, refs = refs[:size], refs[size:]
    if forward:
        _, local_ref, total_ref, factor_ref, carry_ref, ordered_ref = refs
    else:
        carry_ref, _, local_ref, total_ref, factor_ref, ordered_ref = refs
    dim = in_refs[0].shape[1]
    me = my_place(size)
    for slot, in_ref in enumerate(in_refs):
        ordered_ref[sent_by(me, slot, size)] = in_ref[...]
    if forward:
        for b in range(size):
            tile = ordered_ref[b, hpo * dim :, :].astype(F32)
            for i in range(hpo):
                carry_ref[b, i : i + 1, :] = tile[3 * i : 3 * i + 1] + tile[3 * i + 1 : 3 * i + 2] + tile[3 * i + 2 : 3 * i + 3]
    for i in range(hpo):
        rows = slice(i * dim, (i + 1) * dim)
        state = jnp.zeros((dim, dim), F32)
        factor = jnp.ones((1, dim), F32)
        for b in range(size) if forward else reversed(range(size)):
            carry = carry_ref[b, i : i + 1, :]
            local_ref[b, rows, :] = state
            factor_ref[b, i : i + 1, :] = factor
            state = carry * state + ordered_ref[b, rows, :].astype(F32)
            factor = factor * carry
        total_ref[rows, :] = state.astype(BF16)


def return_kernel(hpo, size, local_ref, factor_ref, outer_ref, _, *out_refs):
    dim = local_ref.shape[2]
    me = my_place(size)
    for i in range(hpo):
        rows = slice(i * dim, (i + 1) * dim)
        outer = outer_ref[rows, :].astype(F32)
        for slot, out_ref in enumerate(out_refs):
            b = send_to(me, slot, size)
            out_ref[rows, :] = (local_ref[b, rows, :] + factor_ref[b, i : i + 1, :] * outer).astype(BF16)


def ordered_states(hpo, size, state_ref, in_refs):
    dim = in_refs[0].shape[1]
    me = my_place(size)
    for slot, in_ref in enumerate(in_refs):
        owner = sent_by(me, slot, size)
        for i in range(hpo):
            state_ref[owner * hpo + i] = in_ref[i * dim : (i + 1) * dim, :]


def intra_kernel(group, dim, begin, end, table_ref, q_ref, k_ref, v_ref, *refs):
    length = q_ref.shape[0]
    copy = None
    if begin == 0:
        cot_hbm, out_ref, cot_ref, mask_ref, sems = refs
        copy = pltpu.make_async_copy(cot_hbm, cot_ref, sems.at[0])
        copy.start()
    else:
        out_ref, mask_ref = refs
    mask_ref[...] = block_mask(table_ref[0], False)

    def one(g, _):
        table = table_ref[g]
        columns = table.T
        for h in range(group):
            lanes = lanes_of(g * group + h, dim)
            local = lanes_of((g - begin) * group + h, dim)
            for first in range(0, length, HALF):
                rows, seen = pl.ds(first, HALF), pl.ds(0, first + HALF)
                scores = dot_nt(q_ref[rows, lanes], k_ref[seen, lanes])
                gap = columns[first : first + HALF, h : h + 1] - table[h : h + 1, : first + HALF]
                weight = jnp.exp2(gap + mask_ref[rows, seen])
                out_ref[rows, local] = dot((scores * weight).astype(BF16), v_ref[seen, lanes])
        return 0

    lax.fori_loop(begin, end, one, 0)
    if copy is not None:
        copy.wait()


def token_rows(total):
    length = total.shape[0]
    return jnp.concatenate(
        [jnp.sum(total[i : i + 128].T, axis=0, keepdims=True) for i in range(0, length, 128)], axis=0
    )


def output_kernel(group, hpo, size, cuts, table_ref, q_ref, cot_ref, *refs):
    intra_refs, refs = refs[: len(cuts)], refs[len(cuts) :]
    in_refs, refs = refs[:size], refs[size:]
    out_ref, state_ref, sums_ref, square_ref, cross_ref = refs
    dim = in_refs[0].shape[1]
    ordered_states(hpo, size, state_ref, in_refs)
    square_ref[...] = jnp.zeros_like(square_ref)
    cross_ref[...] = jnp.zeros_like(cross_ref)
    for (begin, end), intra_ref in zip(cuts, intra_refs):

        def one(g, _):
            columns = table_ref[g].T
            square, cross = square_ref[...], cross_ref[...]
            for h in range(group):
                lanes = lanes_of(g * group + h, dim)
                local = lanes_of((g - begin) * group + h, dim)
                carried = dot(q_ref[:, lanes], state_ref[g * group + h])
                out = intra_ref[:, local] + columns[:, group + h : group + h + 1] * carried
                out_ref[:, lanes] = out
                square = square + out * out
                cross = cross + cot_ref[:, lanes].astype(F32) * out
            square_ref[...] = square
            cross_ref[...] = cross
            return 0

        lax.fori_loop(begin, end, one, 0)
    sums_ref[...] = jnp.concatenate([token_rows(square_ref[...]), token_rows(cross_ref[...])], axis=0)


def gout_kernel(hpo, size, count, *refs):
    sums_refs, refs = refs[:count], refs[count:]
    rows_ref, q_ref, out_ref, cot_ref, attn_hbm, gout_ref = refs[:6]
    sent_refs, (attn_ref, factor_ref, sems) = refs[6 : 6 + size], refs[6 + size :]
    heads = rows_ref.shape[0] // 2
    dim = q_ref.shape[1] // heads
    total = sums_refs[0][...]
    for ref in sums_refs[1:]:
        total = total + ref[...]
    lines = total.shape[0] // 2
    full = HEAD_TOTAL * HEAD_DIM
    scale = lax.rsqrt(total[:lines] / full + EPS)
    slope = scale * scale * scale * total[lines:] / full
    turned = jnp.concatenate([scale, slope], axis=0).T
    for i in range(lines):
        rows = slice(i * 128, (i + 1) * 128)
        factor_ref[0, rows, :] = jnp.broadcast_to(turned[:, i : i + 1], (128, dim))
        factor_ref[1, rows, :] = jnp.broadcast_to(turned[:, lines + i : lines + i + 1], (128, dim))

    me = my_place(size)

    def store(slot):
        lanes = lanes_of(send_to(me, slot, size), hpo * dim)
        return pltpu.make_async_copy(attn_ref.at[:, lanes], attn_hbm.at[:, lanes], sems.at[slot])

    for slot, sent_ref in enumerate(sent_refs):
        owner = send_to(me, slot, size)

        @pl.when(owner * hpo < heads)
        def _():
            for i in range(hpo):
                head = owner * hpo + i
                lanes = lanes_of(head, dim)
                scale, slope = factor_ref[0], factor_ref[1]
                out = out_ref[:, lanes]
                attn_ref[:, lanes] = (scale * out).astype(BF16)
                gout = (scale * cot_ref[:, lanes].astype(F32) - slope * out).astype(BF16)
                gout_ref[:, lanes] = gout
                decayed = (q_ref[:, lanes].T.astype(F32) * rows_ref[head]).astype(BF16)
                sent_ref[i * dim : (i + 1) * dim, :] = dot(decayed, gout).astype(BF16)
            store(slot).start()

    for slot in range(size):

        @pl.when(send_to(me, slot, size) * hpo < heads)
        def _():
            store(slot).wait()


def gradient_kernel(group, dim, begin, end, table_ref, q_ref, k_ref, v_ref, gout_ref, state_ref, *refs):
    if begin > 0:
        refs = refs[1:]
    gq_hbm, gk_ref, gv_ref, gq_ref, mask_ref, sems = refs
    length = q_ref.shape[0]
    wide = group * dim
    mask_ref[...] = block_mask(table_ref[0], True)

    def store(g):
        return pltpu.make_async_copy(
            gq_ref.at[:, lanes_of(g - begin, wide)], gq_hbm.at[:, lanes_of(g, wide)], sems.at[g - begin]
        )

    def one(g, _):
        table = table_ref[g]
        columns = table.T
        for h in range(group):
            lanes = lanes_of(g * group + h, dim)
            local = lanes_of((g - begin) * group + h, dim)
            query_turned, gout_turned = q_ref[:, lanes].T, gout_ref[:, lanes].T
            carried = dot(state_ref[g * group + h], gout_turned)
            pieces = [table[group + h : group + h + 1] * carried]
            for first in range(0, length, HALF):
                rows, later = pl.ds(first, HALF), pl.ds(first, length - first)
                key, value = k_ref[rows, lanes], v_ref[rows, lanes]
                gap = table[h : h + 1, first:] - columns[first : first + HALF, h : h + 1]
                weight = jnp.exp2(gap + mask_ref[rows, later])
                probs = (dot(key, query_turned[:, first:]) * weight).astype(BF16)
                gv_ref[rows, local] = dot(probs, gout_ref[later, lanes])
                grads = (dot(value, gout_turned[:, first:]) * weight).astype(BF16)
                gk_ref[rows, local] = dot(grads, q_ref[later, lanes])
                pieces.append(dot(key.T, grads))
            for first in range(0, length, HALF):
                total = pieces[0][:, first : first + HALF]
                for i in range(first // HALF + 1):
                    total = total + pieces[i + 1][:, first - i * HALF : first - (i - 1) * HALF]
                gq_ref[first : first + HALF, local] = total.astype(BF16).T
        store(g).start()
        return 0

    lax.fori_loop(begin, end, one, 0)
    for g in range(begin, end):
        store(g).wait()


def final_kernel(group, hpo, size, cuts, table_ref, k_ref, v_ref, *refs):
    parts, refs = refs[: 2 * len(cuts)], refs[2 * len(cuts) :]
    in_refs, refs = refs[:size], refs[size:]
    gk_hbm, gv_hbm, gk_ref, gv_ref, back_ref, sems = refs
    dim = in_refs[0].shape[1]
    wide = group * dim
    ordered_states(hpo, size, back_ref, in_refs)

    def stores(g):
        lanes = lanes_of(g, wide)
        return (
            pltpu.make_async_copy(gk_ref.at[:, lanes], gk_hbm.at[:, lanes], sems.at[0, g]),
            pltpu.make_async_copy(gv_ref.at[:, lanes], gv_hbm.at[:, lanes], sems.at[1, g]),
        )

    for (begin, end), gkp_ref, gvp_ref in zip(cuts, parts[::2], parts[1::2]):

        def one(g, _):
            columns = table_ref[g].T
            for h in range(group):
                lanes = lanes_of(g * group + h, dim)
                local = lanes_of((g - begin) * group + h, dim)
                leave = columns[:, 2 * group + h : 2 * group + h + 1]
                back = back_ref[g * group + h]
                gk_ref[:, lanes] = (gkp_ref[:, local] + leave * dot_nt(v_ref[:, lanes], back)).astype(BF16)
                gv_ref[:, lanes] = (gvp_ref[:, local] + leave * dot(k_ref[:, lanes], back)).astype(BF16)
            for copy in stores(g):
                copy.start()
            return 0

        lax.fori_loop(begin, end, one, 0)
    for g in range(table_ref.shape[0]):
        for copy in stores(g):
            copy.wait()


def exchange(arrays, size, halves):
    def pairs(slot):
        return [
            (base + place, base + int(send_to(place, slot, size) if size & (size - 1) == 0 else (place + slot) % size))
            for base in range(0, halves * size, size)
            for place in range(size)
        ]

    return [arrays[0]] + [lax.ppermute(arrays[slot], "seq", pairs(slot)) for slot in range(1, size)]


def split(groups, parts):
    edges = [round(i * groups / parts) for i in range(parts + 1)]
    return [(a, b) for a, b in zip(edges, edges[1:]) if b > a]


def per_device(queries, keys, values, cotangent, log_decay, starts):
    length, width = queries.shape
    heads = log_decay.shape[0]
    dim = width // heads
    blocks = lax.axis_size("seq")
    shares = lax.axis_size("head")
    halves = 2 if blocks % 2 == 0 else 1
    size = blocks // halves
    hpo = -(-heads // size)
    group = min(4, heads)
    groups = heads // group
    params = pltpu.CompilerParams(vmem_limit_bytes=16 << 20)

    inside = pl.BlockSpec(memory_space=pltpu.VMEM)
    unused = pl.BlockSpec(memory_space=pl.ANY)
    hbm = pl.BlockSpec(memory_space=pltpu.HBM)
    dma = pltpu.SemaphoreType.DMA

    def outside(array):
        return pltpu.with_memory_space_constraint(array, pltpu.HBM)

    def held(columns, dtype):
        return pltpu.VMEM((length, columns), dtype)

    def cost(products, exps=0, share=1.0):
        return pl.CostEstimate(
            flops=int(2 * heads * products * share),
            bytes_accessed=int(length * width * share),
            transcendentals=int(heads * exps * share),
        )

    def scan(arrays, carries, after, later):
        forward = carries is None
        local = pltpu.VMEM((size, hpo * dim, dim), F32)
        factor = pltpu.VMEM((size, 8, dim), F32)
        total = pltpu.VMEM((hpo * dim, dim), BF16)
        local, total, factor, *rest = pl.pallas_call(
            functools.partial(scan_kernel, hpo, size, forward),
            in_specs=[inside] * (size if forward else size + 1) + [unused],
            out_specs=[inside] * (4 if forward else 3),
            out_shape=[local, total, factor] + ([factor] if forward else []),
            scratch_shapes=[pltpu.VMEM((size, *arrays[0].shape), BF16)],
            compiler_params=params,
            name="scan",
        )(*arrays, *([] if forward else [carries]), after)
        if halves == 2:
            pairs = [(i, i + size) if forward else (i + size, i) for i in range(size)]
            outer = lax.ppermute(total, "seq", pairs)
        else:
            outer = jnp.zeros_like(total)
        back = pl.pallas_call(
            functools.partial(return_kernel, hpo, size),
            in_specs=[inside] * 3 + [unused],
            out_specs=[inside] * size,
            out_shape=[pltpu.VMEM((hpo * dim, dim), BF16)] * size,
            compiler_params=params,
            name="return",
        )(local, factor, outer, later)
        return exchange(back, size, halves), (rest[0] if forward else None)

    big, small = length * length * dim, length * dim * dim
    queries, keys, values, cotangent = (outside(a) for a in (queries, keys, values, cotangent))
    *sent, table, rows, k, v, q = pl.pallas_call(
        functools.partial(update_kernel, group, hpo, size),
        in_specs=[hbm] * 5,
        out_specs=[inside] * (size + 5),
        out_shape=[pltpu.VMEM((hpo * dim + ROWS, dim), BF16)] * size
        + [pltpu.VMEM((groups, ROWS, length), F32), pltpu.VMEM((2 * heads, 1, length), F32)]
        + [held(width, BF16)] * 3,
        scratch_shapes=[pltpu.VMEM((heads, length), F32), pltpu.VMEM((1, length), jnp.int32), dma((5,))],
        compiler_params=params,
        cost_estimate=cost(small),
        name="update",
    )(outside(log_decay), outside(starts.reshape(1, length)), keys, values, queries)
    received = exchange(sent, size, halves)

    cuts = split(groups, 2)
    intras = []
    cot = None
    for begin, end in cuts:
        first = begin == 0
        intra, *rest = pl.pallas_call(
            functools.partial(intra_kernel, group, dim, begin, end),
            in_specs=[inside] * 4 + [hbm] * first,
            out_specs=[inside] * (1 + first),
            out_shape=[held((end - begin) * group * dim, F32)] + [held(width, BF16)] * first,
            scratch_shapes=[pltpu.VMEM((length, length), F32)] + [dma((1,))] * first,
            compiler_params=params,
            cost_estimate=cost(2 * big, length * length, (end - begin) / groups),
            name="intra",
        )(table, q, k, v, *([cotangent] if first else []))
        intras.append(intra)
        cot = rest[0] if first else cot

    received, carries = scan(received, None, intras[0], intras[-1])

    lines = 2 * length // 128
    outputs, states, sums = pl.pallas_call(
        functools.partial(output_kernel, group, hpo, size, cuts),
        in_specs=[inside] * (3 + len(cuts) + size),
        out_specs=[inside] * 3,
        out_shape=[held(width, F32), pltpu.VMEM((size * hpo, dim, dim), BF16), pltpu.VMEM((lines, 128), F32)],
        scratch_shapes=[held(dim, F32)] * 2,
        compiler_params=params,
        cost_estimate=cost(small),
        name="output",
    )(table, q, cot, *intras, *received)

    everyone = [sums] + [
        lax.ppermute(sums, "head", [(i, (i + k) % shares) for i in range(shares)]) for k in range(1, shares)
    ]

    attn, gout, *sent = pl.pallas_call(
        functools.partial(gout_kernel, hpo, size, shares),
        in_specs=[inside] * (shares + 4),
        out_specs=[hbm] + [inside] * (1 + size),
        out_shape=[pltpu.HBM((length, width), BF16), held(width, BF16)] + [pltpu.VMEM((hpo * dim, dim), BF16)] * size,
        scratch_shapes=[held(width, BF16), pltpu.VMEM((2, length, dim), F32), dma((size,))],
        compiler_params=params,
        cost_estimate=cost(small),
        name="gout",
    )(*everyone, rows, q, outputs, cot)
    received = exchange(sent, size, halves)

    cuts = split(groups, 3)
    parts = []
    gq = None
    for begin, end in cuts:
        span = (end - begin) * group * dim
        gq, *rest = pl.pallas_call(
            functools.partial(gradient_kernel, group, dim, begin, end),
            in_specs=[inside] * 6 + [hbm] * (begin > 0),
            out_specs=[hbm] + [inside] * 2,
            out_shape=[pltpu.HBM((length, width), BF16)] + [held(span, F32)] * 2,
            scratch_shapes=[held(span, BF16), pltpu.VMEM((length, length), F32), dma((end - begin,))],
            input_output_aliases={6: 0} if begin > 0 else {},
            compiler_params=params,
            cost_estimate=cost(5 * big + small, length * length, (end - begin) / groups),
            name="gradient",
        )(table, q, k, v, gout, states, *([gq] if begin > 0 else []))
        parts += rest

    received, _ = scan(received, carries, parts[0], parts[-3 if len(cuts) > 2 else 0])

    gk, gv = pl.pallas_call(
        functools.partial(final_kernel, group, hpo, size, cuts),
        in_specs=[inside] * (3 + 2 * len(cuts) + size),
        out_specs=[hbm] * 2,
        out_shape=[pltpu.HBM((length, width), BF16)] * 2,
        scratch_shapes=[held(width, BF16)] * 2 + [pltpu.VMEM((size * hpo, dim, dim), BF16), dma((2, groups))],
        compiler_params=params,
        cost_estimate=cost(2 * small),
        name="final",
    )(table, k, v, *parts, *received)
    return (attn, gq, gk, gv)


def solution(mesh):
    wide = P("seq", "head")
    return jax.shard_map(
        per_device,
        mesh=mesh,
        in_specs=(wide, wide, wide, wide, P("head", "seq"), P("seq")),
        out_specs=(wide, wide, wide, wide),
        check_vma=False,
    )
```

time: 720 us -> 74.6 us (0.10)
  matrix products: 272 us -> 0 us
  waiting for transfers between devices: 167 us -> 12 us
  local copies, waits for them, and re-layouts: 116 us -> 0 us
  other arithmetic: 73 us -> 0 us
  loops' own time: 41.5 us -> 0 us
  Pallas kernels: 0 us -> 38.3 us
  blocking collectives: 29.1 us -> 0 us
  starting transfers between devices: 0.08 us -> 23.1 us
  between operations: 14.8 us -> 0.95 us
    dot_general x162 -> x0, matrix products: 272 us -> none  [the longest x16 34.8 us: local_forward(): jnp.einsum('td,sd->ts', query_head, key_head, preferred_element_type=jnp....]
    all_gather x2 -> x0, waiting for transfers between devices: 167 us -> none  [the longest x1 120 us: prefix(): gathered = jax.tree.map(lambda a: lax.all_gather(a, axis), part)]
    slice x80 -> x0, local copies, waits for them, and re-layouts: 46.2 us -> none  [the longest x48 27.5 us: block_factors(): cum_log[:, -1:] - cum_log]
    another operation x3 -> x0, loops' own time: 41.5 us -> none  [the longest x1 21.3 us: per_device(): lax.map(local_forward, (query_heads, key_heads, value_heads, log_decay))]
    pallas_call x0 -> x13, Pallas kernels: none -> 38.3 us  [the longest x3 16 us: per_device(): pl.pallas_call(functools.partial(gradient_kernel, group, dim, begin, end)...]
    select_n x65 -> x0, other arithmetic: 31.4 us -> none  [the longest x32 31.1 us: block_factors(): jnp.where(doc_count[None, :] == doc_count[-1], jnp.exp(cum_log[:, -1:] -...]
    unnamed x1 -> x0, blocking collectives: 23.4 us -> none
    dynamic_slice x32 -> x0, local copies, waits for them, and re-layouts: 23.2 us -> none  [per_device(): lax.map(local_forward, (query_heads, key_heads, value_heads, log_decay))]
  transfers between devices with their start and end apart: 2 -> 17, of which waited for: 2 -> 10; matrix products, arithmetic and copies ran while one was open for 1% -> 0% of each run, Pallas kernels for 0% -> 31%
where the time goes in v2:
time: 74.6 us; the launch traced here: 74.4 us
  Pallas kernels  38.3 us (51%)
  starting transfers between devices  23.1 us (31%)
  waiting for transfers between devices  12 us (16%)
  between operations  0.95 us (1%)
    pallas_call x3, Pallas kernels, per_device(): pl.pallas_call(functools.partial(gradient_kernel, group, dim, begin, end)...  16 us
    ppermute x12, starting transfers between devices, exchange(): lax.ppermute(arrays[slot], 'seq', pairs(slot))  15.4 us
    ppermute x12, waiting for transfers between devices, exchange(): lax.ppermute(arrays[slot], 'seq', pairs(slot))  8.89 us
    pallas_call x2, Pallas kernels, per_device(): pl.pallas_call(functools.partial(intra_kernel, group, dim, begin, end), i...  6.91 us
    ppermute x2, starting transfers between devices, scan(): outer = lax.ppermute(total, 'seq', pairs)  5.96 us
    pallas_call x1, Pallas kernels, per_device(): pl.pallas_call(functools.partial(update_kernel, group, hpo, size), in_spe...  4.17 us
    pallas_call x1, Pallas kernels, per_device(): pl.pallas_call(functools.partial(gout_kernel, hpo, size, shares), in_spec...  3.83 us
    pallas_call x1, Pallas kernels, per_device(): pl.pallas_call(functools.partial(final_kernel, group, hpo, size, cuts), i...  3.68 us
  transfers between devices with their start and end apart: 17, of which 10 were waited for; matrix products, arithmetic and copies ran while one was open for 0% of the time, Pallas kernels for 31%

profile of v2, /device:TPU:0, one launch (start us, length us, event | category | flops | bytes accessed | tf_op | source)
XLA Modules:
  0.0 74.4 jit_solution(5626938747562950133)
XLA Ops:
  0.6 4.2 %update.1 = (bf16[528,128]{1,0:T(8,128)(2,1)S(1)}, bf16[528,128]{1,0:T(8,128)(2,1)S(1)}, bf16[528,128]{1,0:T(8,128)(2,1)S(1)}, bf16[528,128]{1,0:T(8,128)(2,1)S(...) custom-call(f32[16,512]{1,0:T(8,128)} %logs_hbm.1, ...), custom_call_target="tpu_custom_call" | custom-call | flops 268435456 | bytes 1048576 | tf_op jit(solution)/shard_map/update/pallas_call | solution.py:445
  4.8 3.0 %collective-permute-start = (bf16[528,128]{1,0:T(8,128)(2,1)S(1)}, bf16[528,128]{1,0:T(8,128)(2,1)S(1)}, u32[]{:S(2)}, u32[]{:S(2)}) collective-permute-start(bf16[528,128]{1,0:T(8,128)(2,1)S(1)} %get-tuple-element.57), channel_id=1, source_target_pairs={{0,4},{4,0},{8,12},{12,8},{16,20},{20,16},{24,28},{28,24},{1,5},{5... | collective-permute-start | bytes 405512 | tf_op jit(solution)/shard_map/ppermute | solution.py:375
  7.8 1.6 %collective-permute-start.1 = (bf16[528,128]{1,0:T(8,128)(2,1)S(1)}, bf16[528,128]{1,0:T(8,128)(2,1)S(1)}, u32[]{:S(2)}, u32[]{:S(2)}) collective-permute-start(bf16[528,128]{1,0:T(8,128)(2,1)S(1)} %get-tuple-element.58), channel_id=1, source_target_pairs={{0,8},{4,12},{8,0},{12,4},{16,24},{20,28},{24,16},{28,20},{1,9},{5... | collective-permute-start | bytes 405512 | tf_op jit(solution)/shard_map/ppermute | solution.py:375
  9.4 3.5 %intra.2 = (f32[512,1024]{1,0:T(8,128)S(1)}, bf16[512,2048]{1,0:T(8,128)(2,1)S(1)}) custom-call(f32[4,16,512]{2,1,0:T(8,128)S(1)} %get-tuple-element.50.table_ref, bf16[512,2048]{1,0:T(8,128)(2,1)S(1)} %get-tuple-element.51.q_ref.refs_5_, bf16[512,2048]{1,0:T(8,128)(2,1)S(1)} %get-tuple-element.52.k_ref, bf16[512,2048]{1,0:T(8,128)(2,1)S(1)} %get-tuple-element.53.v_ref, ...), custom_call_target="tpu_custom_call" | custom-call | flops 1073741824 | bytes 524288 | tf_op jit(solution)/shard_map/intra/pallas_call | solution.py:464
  12.9 1.4 %collective-permute-done.1.refs_2_ = bf16[528,128]{1,0:T(8,128)(2,1)S(1)} collective-permute-done((bf16[528,128]{1,0:T(8,128)(2,1)S(1)}, bf16[528,128]{1,0:T(8,128)(2,1)S(1)}, u32[]{:S(2)}, u32[]{:S(2)}) %collective-permute-start.1) | collective-permute-done | bytes 135200 | tf_op jit(solution)/shard_map/ppermute | solution.py:375
  14.3 1.3 %collective-permute-done.2.refs_3_ = bf16[528,128]{1,0:T(8,128)(2,1)S(1)} collective-permute-done((bf16[528,128]{1,0:T(8,128)(2,1)S(1)}, bf16[528,128]{1,0:T(8,128)(2,1)S(1)}, u32[]{:S(2)}, u32[]{:S(2)}) %collective-permute-start.2) | collective-permute-done | bytes 135200 | tf_op jit(solution)/shard_map/ppermute | solution.py:375
  15.7 4.7 %collective-permute-start.3 = (bf16[512,128]{1,0:T(8,128)(2,1)S(1)}, bf16[512,128]{1,0:T(8,128)(2,1)S(1)}, u32[]{:S(2)}, u32[]{:S(2)}) collective-permute-start(bf16[512,128]{1,0:T(8,128)(2,1)S(1)} %get-tuple-element.62), channel_id=1, source_target_pairs={{0,16},{4,20},{8,24},{12,28},{1,17},{5,21},{9,25},{13,29},{2,18},{... | collective-permute-start | bytes 393224 | tf_op jit(solution)/shard_map/ppermute | solution.py:430
  20.4 3.4 %intra.3._.refs_1_ = f32[512,1024]{1,0:T(8,128)S(1)} custom-call(f32[4,16,512]{2,1,0:T(8,128)S(1)} %get-tuple-element.50.table_ref, bf16[512,2048]{1,0:T(8,128)(2,1)S(1)} %get-tuple-element.51.q_ref.refs_5_, bf16[512,2048]{1,0:T(8,128)(2,1)S(1)} %get-tuple-element.52.k_ref, bf16[512,2048]{1,0:T(8,128)(2,1)S(1)} %get-tuple-element.53.v_ref), custom_call_target="tpu_custom_call" | custom-call | flops 1073741824 | bytes 524288 | tf_op jit(solution)/shard_map/intra/pallas_call | solution.py:464
  24.0 1.6 %collective-permute-start.4 = (bf16[512,128]{1,0:T(8,128)(2,1)S(1)}, bf16[512,128]{1,0:T(8,128)(2,1)S(1)}, u32[]{:S(2)}, u32[]{:S(2)}) collective-permute-start(bf16[512,128]{1,0:T(8,128)(2,1)S(1)} %get-tuple-element.64), channel_id=1, source_target_pairs={{0,4},{4,0},{8,12},{12,8},{16,20},{20,16},{24,28},{28,24},{1,5},{5... | collective-permute-start | bytes 393224 | tf_op jit(solution)/shard_map/ppermute | solution.py:375
  25.5 2.0 %collective-permute-start.5 = (bf16[512,128]{1,0:T(8,128)(2,1)S(1)}, bf16[512,128]{1,0:T(8,128)(2,1)S(1)}, u32[]{:S(2)}, u32[]{:S(2)}) collective-permute-start(bf16[512,128]{1,0:T(8,128)(2,1)S(1)} %get-tuple-element.65), channel_id=1, source_target_pairs={{0,8},{4,12},{8,0},{12,4},{16,24},{20,28},{24,16},{28,20},{1,9},{5... | collective-permute-start | bytes 393224 | tf_op jit(solution)/shard_map/ppermute | solution.py:375
  27.7 2.8 %collective-permute-done.4.refs_3_ = bf16[512,128]{1,0:T(8,128)(2,1)S(1)} collective-permute-done((bf16[512,128]{1,0:T(8,128)(2,1)S(1)}, bf16[512,128]{1,0:T(8,128)(2,1)S(1)}, u32[]{:S(2)}, u32[]{:S(2)}) %collective-permute-start.4) | collective-permute-done | bytes 131104 | tf_op jit(solution)/shard_map/ppermute | solution.py:375
  30.4 0.9 %collective-permute-done.5.refs_4_ = bf16[512,128]{1,0:T(8,128)(2,1)S(1)} collective-permute-done((bf16[512,128]{1,0:T(8,128)(2,1)S(1)}, bf16[512,128]{1,0:T(8,128)(2,1)S(1)}, u32[]{:S(2)}, u32[]{:S(2)}) %collective-permute-start.5) | collective-permute-done | bytes 131104 | tf_op jit(solution)/shard_map/ppermute | solution.py:375
  31.3 2.2 %collective-permute-done.6.refs_5_ = bf16[512,128]{1,0:T(8,128)(2,1)S(1)} collective-permute-done((bf16[512,128]{1,0:T(8,128)(2,1)S(1)}, bf16[512,128]{1,0:T(8,128)(2,1)S(1)}, u32[]{:S(2)}, u32[]{:S(2)}) %collective-permute-start.6) | collective-permute-done | bytes 131104 | tf_op jit(solution)/shard_map/ppermute | solution.py:375
  33.5 3.2 %output.1 = (f32[512,2048]{1,0:T(8,128)S(1)}, bf16[16,128,128]{2,1,0:T(8,128)(2,1)S(1)}, f32[8,128]{1,0:T(8,128)S(1)}) custom-call(f32[4,16,512]{2,1,0:T(8,128)S(1)} %get-tuple-element.50.table_ref, bf16[512,2048]{1,0:T(8,128)(2,1)S(1)} %get-tuple-element.51.q_ref.refs_5_, bf16[512,2048]{1,0:T(8,128)(2,1)S(1)} %get-tuple-element.54.cot_ref.refs_7_, ...), custom_call_target="tpu_custom_call" | custom-call | flops 268435456 | bytes 1048576 | tf_op jit(solution)/shard_map/output/pallas_call | solution.py:480
  36.7 1.6 %collective-permute-start.8 = (f32[8,128]{1,0:T(8,128)S(1)}, f32[8,128]{1,0:T(8,128)S(1)}, u32[]{:S(2)}, u32[]{:S(2)}) collective-permute-start(f32[8,128]{1,0:T(8,128)S(1)} %get-tuple-element.67.refs_0_), channel_id=1, source_target_pairs={{0,2},{1,3},{2,0},{3,1},{4,6},{5,7},{6,4},{7,5},{8,10},{9,11},{10,... | collective-permute-start | bytes 12296 | tf_op jit(solution)/shard_map/ppermute | solution.py:492
  38.4 1.9 %collective-permute-done.8.refs_2_ = f32[8,128]{1,0:T(8,128)S(1)} collective-permute-done((f32[8,128]{1,0:T(8,128)S(1)}, f32[8,128]{1,0:T(8,128)S(1)}, u32[]{:S(2)}, u32[]{:S(2)}) %collective-permute-start.8) | collective-permute-done | bytes 4128 | tf_op jit(solution)/shard_map/ppermute | solution.py:492
  40.4 0.9 %collective-permute-done.7.refs_1_ = f32[8,128]{1,0:T(8,128)S(1)} collective-permute-done((f32[8,128]{1,0:T(8,128)S(1)}, f32[8,128]{1,0:T(8,128)S(1)}, u32[]{:S(2)}, u32[]{:S(2)}) %collective-permute-start.7) | collective-permute-done | bytes 4128 | tf_op jit(solution)/shard_map/ppermute | solution.py:492
  41.3 3.8 %gout.1 = (bf16[512,2048]{1,0:T(8,128)(2,1)}, bf16[512,2048]{1,0:T(8,128)(2,1)S(1)}, bf16[512,128]{1,0:T(8,128)(2,1)S(1)}, bf16[512,128]{1,0:T(8,128)(2,1)S(1)},...) custom-call(f32[8,128]{1,0:T(8,128)S(1)} %get-tuple-element.67.refs_0_, ...), custom_call_target="tpu_custom_call" | custom-call | flops 268435456 | bytes 1048576 | tf_op jit(solution)/shard_map/gout/pallas_call | solution.py:495
  45.1 0.8 %collective-permute-start.10 = (bf16[512,128]{1,0:T(8,128)(2,1)S(1)}, bf16[512,128]{1,0:T(8,128)(2,1)S(1)}, u32[]{:S(2)}, u32[]{:S(2)}) collective-permute-start(bf16[512,128]{1,0:T(8,128)(2,1)S(1)} %get-tuple-element.83), channel_id=1, source_target_pairs={{0,4},{4,0},{8,12},{12,8},{16,20},{20,16},{24,28},{28,24},{1,5},{5... | collective-permute-start | bytes 393224 | tf_op jit(solution)/shard_map/ppermute | solution.py:375
  46.0 1.2 %collective-permute-start.11 = (bf16[512,128]{1,0:T(8,128)(2,1)S(1)}, bf16[512,128]{1,0:T(8,128)(2,1)S(1)}, u32[]{:S(2)}, u32[]{:S(2)}) collective-permute-start(bf16[512,128]{1,0:T(8,128)(2,1)S(1)} %get-tuple-element.84), channel_id=1, source_target_pairs={{0,8},{4,12},{8,0},{12,4},{16,24},{20,28},{24,16},{28,20},{1,9},{5... | collective-permute-start | bytes 393224 | tf_op jit(solution)/shard_map/ppermute | solution.py:375
  47.2 1.5 %collective-permute-start.12 = (bf16[512,128]{1,0:T(8,128)(2,1)S(1)}, bf16[512,128]{1,0:T(8,128)(2,1)S(1)}, u32[]{:S(2)}, u32[]{:S(2)}) collective-permute-start(bf16[512,128]{1,0:T(8,128)(2,1)S(1)} %get-tuple-element.85), channel_id=1, source_target_pairs={{0,12},{4,8},{8,4},{12,0},{16,28},{20,24},{24,20},{28,16},{1,13},{... | collective-permute-start | bytes 393224 | tf_op jit(solution)/shard_map/ppermute | solution.py:375
  48.7 4.1 %gradient.3 = (bf16[512,2048]{1,0:T(8,128)(2,1)}, f32[512,512]{1,0:T(8,128)S(1)}, f32[512,512]{1,0:T(8,128)S(1)}) custom-call(f32[4,16,512]{2,1,0:T(8,128)S(1)} %get-tuple-element.50.table_ref, bf16[512,2048]{1,0:T(8,128)(2,1)S(1)} %get-tuple-element.51.q_ref.refs_5_, bf16[512,2048]{1,0:T(8,128)(2,1)S(1)} %get-tuple-element.52.k_ref, ...), custom_call_target="tpu_custom_call" | custom-call | flops 1409286144 | bytes 262144 | tf_op jit(solution)/shard_map/gradient/pallas_call | solution.py:512
  52.8 0.2 collective-permute-done.12.refs_3_
  53.2 1.3 %collective-permute-start.13 = (bf16[512,128]{1,0:T(8,128)(2,1)S(1)}, bf16[512,128]{1,0:T(8,128)(2,1)S(1)}, u32[]{:S(2)}, u32[]{:S(2)}) collective-permute-start(bf16[512,128]{1,0:T(8,128)(2,1)S(1)} %get-tuple-element.89), channel_id=1, source_target_pairs={{16,0},{20,4},{24,8},{28,12},{17,1},{21,5},{25,9},{29,13},{18,2},{... | collective-permute-start | bytes 393224 | tf_op jit(solution)/shard_map/ppermute | solution.py:430
  54.5 7.8 %gradient.4 = (bf16[512,2048]{1,0:T(8,128)(2,1)}, f32[512,1024]{1,0:T(8,128)S(1)}, f32[512,1024]{1,0:T(8,128)S(1)}) custom-call(f32[4,16,512]{2,1,0:T(8,128)S(1)} %get-tuple-element.50.table_ref, bf16[512,2048]{1,0:T(8,128)(2,1)S(1)} %get-tuple-element.51.q_ref.refs_5_, ...), custom_call_target="tpu_custom_call", output_to_operand_aliasing={{0}: (6, {})} | custom-call | flops 2818572288 | bytes 524288 | tf_op jit(solution)/shard_map/gradient/pallas_call | solution.py:512
  62.3 0.3 collective-permute-done.13.outer_ref
  62.6 1.0 %collective-permute-start.14 = (bf16[512,128]{1,0:T(8,128)(2,1)S(1)}, bf16[512,128]{1,0:T(8,128)(2,1)S(1)}, u32[]{:S(2)}, u32[]{:S(2)}) collective-permute-start(bf16[512,128]{1,0:T(8,128)(2,1)S(1)} %get-tuple-element.91), channel_id=1, source_target_pairs={{0,4},{4,0},{8,12},{12,8},{16,20},{20,16},{24,28},{28,24},{1,5},{5... | collective-permute-start | bytes 393224 | tf_op jit(solution)/shard_map/ppermute | solution.py:375
  63.6 0.9 %collective-permute-start.15 = (bf16[512,128]{1,0:T(8,128)(2,1)S(1)}, bf16[512,128]{1,0:T(8,128)(2,1)S(1)}, u32[]{:S(2)}, u32[]{:S(2)}) collective-permute-start(bf16[512,128]{1,0:T(8,128)(2,1)S(1)} %get-tuple-element.92), channel_id=1, source_target_pairs={{0,8},{4,12},{8,0},{12,4},{16,24},{20,28},{24,16},{28,20},{1,9},{5... | collective-permute-start | bytes 393224 | tf_op jit(solution)/shard_map/ppermute | solution.py:375
  64.5 1.7 %collective-permute-start.16 = (bf16[512,128]{1,0:T(8,128)(2,1)S(1)}, bf16[512,128]{1,0:T(8,128)(2,1)S(1)}, u32[]{:S(2)}, u32[]{:S(2)}) collective-permute-start(bf16[512,128]{1,0:T(8,128)(2,1)S(1)} %get-tuple-element.93), channel_id=1, source_target_pairs={{0,12},{4,8},{8,4},{12,0},{16,28},{20,24},{24,20},{28,16},{1,13},{... | collective-permute-start | bytes 393224 | tf_op jit(solution)/shard_map/ppermute | solution.py:375
  66.2 4.1 %gradient.5 = (bf16[512,2048]{1,0:T(8,128)(2,1)}, f32[512,512]{1,0:T(8,128)S(1)}, f32[512,512]{1,0:T(8,128)S(1)}) custom-call(f32[4,16,512]{2,1,0:T(8,128)S(1)} %get-tuple-element.50.table_ref, bf16[512,2048]{1,0:T(8,128)(2,1)S(1)} %get-tuple-element.51.q_ref.refs_5_, ...), custom_call_target="tpu_custom_call", output_to_operand_aliasing={{0}: (6, {})} | custom-call | flops 1409286144 | bytes 262144 | tf_op jit(solution)/shard_map/gradient/pallas_call | solution.py:512
  70.3 0.2 collective-permute-done.16.refs_9_
  70.5 3.7 %final.1 = (bf16[512,2048]{1,0:T(8,128)(2,1)}, bf16[512,2048]{1,0:T(8,128)(2,1)}) custom-call(f32[4,16,512]{2,1,0:T(8,128)S(1)} %get-tuple-element.50.table_ref, bf16[512,2048]{1,0:T(8,128)(2,1)S(1)} %get-tuple-element.52.k_ref, bf16[512,2048]{1,0:T(8,128)(2,1)S(1)} %get-tuple-element.53.v_ref, f32[512,512]{1,0:T(8,128)S(1)} %get-tuple-element.76.refs_5_.refs_0_, ...), custom_call_target="tpu_custom_call" | custom-call | flops 536870912 | bytes 1048576 | tf_op jit(solution)/shard_map/final/pallas_call | solution.py:527
  (15 shorter events, 0.9 us)
Async XLA Ops:
  4.8 8.1 %collective-permute-start = (bf16[528,128]{1,0:T(8,128)(2,1)S(1)}, bf16[528,128]{1,0:T(8,128)(2,1)S(1)}, u32[]{:S(2)}, u32[]{:S(2)}) collective-permute-start(bf16[528,128]{1,0:T(8,128)(2,1)S(1)} %get-tuple-element.57), channel_id=1, source_target_pairs={{0,4},{4,0},{8,12},{12,8},{16,20},{20,16},{24,28},{28,24},{1,5},{5... | collective-permute-start | bytes 405512 | tf_op jit(solution)/shard_map/ppermute | solution.py:375
  7.8 6.5 %collective-permute-start.1 = (bf16[528,128]{1,0:T(8,128)(2,1)S(1)}, bf16[528,128]{1,0:T(8,128)(2,1)S(1)}, u32[]{:S(2)}, u32[]{:S(2)}) collective-permute-start(bf16[528,128]{1,0:T(8,128)(2,1)S(1)} %get-tuple-element.58), channel_id=1, source_target_pairs={{0,8},{4,12},{8,0},{12,4},{16,24},{20,28},{24,16},{28,20},{1,9},{5... | collective-permute-start | bytes 405512 | tf_op jit(solution)/shard_map/ppermute | solution.py:375
  9.4 6.2 %collective-permute-start.2 = (bf16[528,128]{1,0:T(8,128)(2,1)S(1)}, bf16[528,128]{1,0:T(8,128)(2,1)S(1)}, u32[]{:S(2)}, u32[]{:S(2)}) collective-permute-start(bf16[528,128]{1,0:T(8,128)(2,1)S(1)} %get-tuple-element.59), channel_id=1, source_target_pairs={{0,12},{4,8},{8,4},{12,0},{16,28},{20,24},{24,20},{28,16},{1,13},{... | collective-permute-start | bytes 405512 | tf_op jit(solution)/shard_map/ppermute | solution.py:375
  15.7 8.1 %collective-permute-start.3 = (bf16[512,128]{1,0:T(8,128)(2,1)S(1)}, bf16[512,128]{1,0:T(8,128)(2,1)S(1)}, u32[]{:S(2)}, u32[]{:S(2)}) collective-permute-start(bf16[512,128]{1,0:T(8,128)(2,1)S(1)} %get-tuple-element.62), channel_id=1, source_target_pairs={{0,16},{4,20},{8,24},{12,28},{1,17},{5,21},{9,25},{13,29},{2,18},{... | collective-permute-start | bytes 393224 | tf_op jit(solution)/shard_map/ppermute | solution.py:430
  24.0 6.4 %collective-permute-start.4 = (bf16[512,128]{1,0:T(8,128)(2,1)S(1)}, bf16[512,128]{1,0:T(8,128)(2,1)S(1)}, u32[]{:S(2)}, u32[]{:S(2)}) collective-permute-start(bf16[512,128]{1,0:T(8,128)(2,1)S(1)} %get-tuple-element.64), channel_id=1, source_target_pairs={{0,4},{4,0},{8,12},{12,8},{16,20},{20,16},{24,28},{28,24},{1,5},{5... | collective-permute-start | bytes 393224 | tf_op jit(solution)/shard_map/ppermute | solution.py:375
  25.5 5.7 %collective-permute-start.5 = (bf16[512,128]{1,0:T(8,128)(2,1)S(1)}, bf16[512,128]{1,0:T(8,128)(2,1)S(1)}, u32[]{:S(2)}, u32[]{:S(2)}) collective-permute-start(bf16[512,128]{1,0:T(8,128)(2,1)S(1)} %get-tuple-element.65), channel_id=1, source_target_pairs={{0,8},{4,12},{8,0},{12,4},{16,24},{20,28},{24,16},{28,20},{1,9},{5... | collective-permute-start | bytes 393224 | tf_op jit(solution)/shard_map/ppermute | solution.py:375
  27.6 5.9 %collective-permute-start.6 = (bf16[512,128]{1,0:T(8,128)(2,1)S(1)}, bf16[512,128]{1,0:T(8,128)(2,1)S(1)}, u32[]{:S(2)}, u32[]{:S(2)}) collective-permute-start(bf16[512,128]{1,0:T(8,128)(2,1)S(1)} %get-tuple-element.66), channel_id=1, source_target_pairs={{0,12},{4,8},{8,4},{12,0},{16,28},{20,24},{24,20},{28,16},{1,13},{... | collective-permute-start | bytes 393224 | tf_op jit(solution)/shard_map/ppermute | solution.py:375
  36.6 1.8 %collective-permute-start.9 = (f32[8,128]{1,0:T(8,128)S(1)}, f32[8,128]{1,0:T(8,128)S(1)}, u32[]{:S(2)}, u32[]{:S(2)}) collective-permute-start(f32[8,128]{1,0:T(8,128)S(1)} %get-tuple-element.67.refs_0_), channel_id=1, source_target_pairs={{0,3},{1,0},{2,1},{3,2},{4,7},{5,4},{6,5},{7,6},{8,11},{9,8},{10,9... | collective-permute-start | bytes 12296 | tf_op jit(solution)/shard_map/ppermute | solution.py:492
  36.7 3.7 %collective-permute-start.8 = (f32[8,128]{1,0:T(8,128)S(1)}, f32[8,128]{1,0:T(8,128)S(1)}, u32[]{:S(2)}, u32[]{:S(2)}) collective-permute-start(f32[8,128]{1,0:T(8,128)S(1)} %get-tuple-element.67.refs_0_), channel_id=1, source_target_pairs={{0,2},{1,3},{2,0},{3,1},{4,6},{5,7},{6,4},{7,5},{8,10},{9,11},{10,... | collective-permute-start | bytes 12296 | tf_op jit(solution)/shard_map/ppermute | solution.py:492
  38.3 3.0 %collective-permute-start.7 = (f32[8,128]{1,0:T(8,128)S(1)}, f32[8,128]{1,0:T(8,128)S(1)}, u32[]{:S(2)}, u32[]{:S(2)}) collective-permute-start(f32[8,128]{1,0:T(8,128)S(1)} %get-tuple-element.67.refs_0_), channel_id=1, source_target_pairs={{0,1},{1,2},{2,3},{3,0},{4,5},{5,6},{6,7},{7,4},{8,9},{9,10},{10,1... | collective-permute-start | bytes 12296 | tf_op jit(solution)/shard_map/ppermute | solution.py:492
  45.1 7.7 %collective-permute-start.10 = (bf16[512,128]{1,0:T(8,128)(2,1)S(1)}, bf16[512,128]{1,0:T(8,128)(2,1)S(1)}, u32[]{:S(2)}, u32[]{:S(2)}) collective-permute-start(bf16[512,128]{1,0:T(8,128)(2,1)S(1)} %get-tuple-element.83), channel_id=1, source_target_pairs={{0,4},{4,0},{8,12},{12,8},{16,20},{20,16},{24,28},{28,24},{1,5},{5... | collective-permute-start | bytes 393224 | tf_op jit(solution)/shard_map/ppermute | solution.py:375
  46.0 6.9 %collective-permute-start.11 = (bf16[512,128]{1,0:T(8,128)(2,1)S(1)}, bf16[512,128]{1,0:T(8,128)(2,1)S(1)}, u32[]{:S(2)}, u32[]{:S(2)}) collective-permute-start(bf16[512,128]{1,0:T(8,128)(2,1)S(1)} %get-tuple-element.84), channel_id=1, source_target_pairs={{0,8},{4,12},{8,0},{12,4},{16,24},{20,28},{24,16},{28,20},{1,9},{5... | collective-permute-start | bytes 393224 | tf_op jit(solution)/shard_map/ppermute | solution.py:375
  47.2 5.9 %collective-permute-start.12 = (bf16[512,128]{1,0:T(8,128)(2,1)S(1)}, bf16[512,128]{1,0:T(8,128)(2,1)S(1)}, u32[]{:S(2)}, u32[]{:S(2)}) collective-permute-start(bf16[512,128]{1,0:T(8,128)(2,1)S(1)} %get-tuple-element.85), channel_id=1, source_target_pairs={{0,12},{4,8},{8,4},{12,0},{16,28},{20,24},{24,20},{28,16},{1,13},{... | collective-permute-start | bytes 393224 | tf_op jit(solution)/shard_map/ppermute | solution.py:375
  53.2 9.3 %collective-permute-start.13 = (bf16[512,128]{1,0:T(8,128)(2,1)S(1)}, bf16[512,128]{1,0:T(8,128)(2,1)S(1)}, u32[]{:S(2)}, u32[]{:S(2)}) collective-permute-start(bf16[512,128]{1,0:T(8,128)(2,1)S(1)} %get-tuple-element.89), channel_id=1, source_target_pairs={{16,0},{20,4},{24,8},{28,12},{17,1},{21,5},{25,9},{29,13},{18,2},{... | collective-permute-start | bytes 393224 | tf_op jit(solution)/shard_map/ppermute | solution.py:430
  62.6 7.7 %collective-permute-start.14 = (bf16[512,128]{1,0:T(8,128)(2,1)S(1)}, bf16[512,128]{1,0:T(8,128)(2,1)S(1)}, u32[]{:S(2)}, u32[]{:S(2)}) collective-permute-start(bf16[512,128]{1,0:T(8,128)(2,1)S(1)} %get-tuple-element.91), channel_id=1, source_target_pairs={{0,4},{4,0},{8,12},{12,8},{16,20},{20,16},{24,28},{28,24},{1,5},{5... | collective-permute-start | bytes 393224 | tf_op jit(solution)/shard_map/ppermute | solution.py:375
  63.6 6.7 %collective-permute-start.15 = (bf16[512,128]{1,0:T(8,128)(2,1)S(1)}, bf16[512,128]{1,0:T(8,128)(2,1)S(1)}, u32[]{:S(2)}, u32[]{:S(2)}) collective-permute-start(bf16[512,128]{1,0:T(8,128)(2,1)S(1)} %get-tuple-element.92), channel_id=1, source_target_pairs={{0,8},{4,12},{8,0},{12,4},{16,24},{20,28},{24,16},{28,20},{1,9},{5... | collective-permute-start | bytes 393224 | tf_op jit(solution)/shard_map/ppermute | solution.py:375
  64.5 6.0 %collective-permute-start.16 = (bf16[512,128]{1,0:T(8,128)(2,1)S(1)}, bf16[512,128]{1,0:T(8,128)(2,1)S(1)}, u32[]{:S(2)}, u32[]{:S(2)}) collective-permute-start(bf16[512,128]{1,0:T(8,128)(2,1)S(1)} %get-tuple-element.93), channel_id=1, source_target_pairs={{0,12},{4,8},{8,4},{12,0},{16,28},{20,24},{24,20},{28,16},{1,13},{... | collective-permute-start | bytes 393224 | tf_op jit(solution)/shard_map/ppermute | solution.py:375

commit v3 on v0

v3 whole, which is shorter than its diff:
```python
import functools

import jax
import jax.numpy as jnp
from jax import lax
from jax.experimental import pallas as pl
from jax.experimental.pallas import tpu as pltpu
from jax.sharding import PartitionSpec as P

HEAD_TOTAL = 64
HEAD_DIM = 128
EPS = 1e-05
LOG2E = 1.4426950408889634
MASKED = -1e30
ROWS = 16
HALF = 256
F32 = jnp.float32
BF16 = jnp.bfloat16


def dot(a, b, dims=((1,), (0,))):
    return lax.dot_general(a, b, (dims, ((), ())), preferred_element_type=F32)


def dot_nt(a, b):
    return dot(a, b, ((1,), (1,)))


def running_sum(x):
    width = x.shape[1]
    lane = lax.broadcasted_iota(jnp.int32, x.shape, 1)
    step = 1
    while step < width:
        x = x + jnp.where(lane >= step, pltpu.roll(x, step, 1), 0.0)
        step *= 2
    return x


def three_parts(x):
    high = x.astype(BF16).astype(F32)
    rest = x - high
    middle = rest.astype(BF16).astype(F32)
    return high, middle, rest - middle


def lanes_of(index, size):
    return pl.ds(index * size if isinstance(index, int) else pl.multiple_of(index * size, size), size)


def partner(place, slot, size):
    return place ^ slot if size & (size - 1) == 0 else (place + slot) % size


def inverse(place, slot, size):
    return place ^ slot if size & (size - 1) == 0 else (place + size - slot) % size


def my_place(size):
    return lax.rem(lax.axis_index("seq"), size)


def block_mask(table):
    length = table.shape[1]
    row = table[ROWS - 1 :, :]
    column = table.T[:, ROWS - 1 :]
    down = lax.broadcasted_iota(jnp.int32, (length, length), 0)
    across = lax.broadcasted_iota(jnp.int32, (length, length), 1)
    return jnp.where((across >= down) & (row == column), 0.0, MASKED)


class Plan:
    def __init__(self, heads, dim, length, size):
        self.heads, self.dim, self.length, self.size = heads, dim, length, size
        self.hpo = -(-heads // size)
        self.span = self.hpo * dim

    def lanes(self, slot):
        start = partner(my_place(self.size), slot, self.size) * self.span
        return pl.ds(pl.multiple_of(start, self.span), self.span)

    def head(self, i):
        return slice(i * self.dim, (i + 1) * self.dim)

    def guard(self, slot):
        if self.hpo * self.size == self.heads:
            return lambda body: body()
        return pl.when(partner(my_place(self.size), slot, self.size) * self.hpo < self.heads)


def order(size):
    return list(range(1, size)) + [0]


def update_kernel(plan, logs_hbm, starts_hbm, k_hbm, v_hbm, *refs):
    size, hpo, dim, heads = plan.size, plan.hpo, plan.dim, plan.heads
    sent_refs, k_refs, v_refs, turned_refs = (refs[i * size : (i + 1) * size] for i in range(4))
    table_ref, logs_ref, starts_ref, natural_ref, small_sems, sems = refs[4 * size :]
    length = plan.length
    copies = [
        pltpu.make_async_copy(logs_hbm, logs_ref, small_sems.at[0]),
        pltpu.make_async_copy(starts_hbm, starts_ref, small_sems.at[1]),
    ]
    for copy in copies:
        copy.start()

    def loads(slot):
        lanes = plan.lanes(slot)
        return (
            pltpu.make_async_copy(k_hbm.at[:, lanes], k_refs[slot], sems.at[0, slot]),
            pltpu.make_async_copy(v_hbm.at[:, lanes], v_refs[slot], sems.at[1, slot]),
        )

    for slot in order(size):

        @plan.guard(slot)
        def _():
            for copy in loads(slot):
                copy.start()

    for copy in copies:
        copy.wait()
    flags = jnp.broadcast_to(starts_ref[...].astype(F32), (8, length))
    sums = running_sum(jnp.concatenate([logs_ref[...], flags], axis=0))
    logs, count = sums[:heads] * LOG2E, sums[heads : heads + 1]
    last = slice(length - 1, length)
    enter = jnp.where(count == 0.0, jnp.exp2(logs), 0.0)
    leave = jnp.where(count == count[:, last], jnp.exp2(logs[:, last] - logs), 0.0)
    fill = jnp.broadcast_to(count, (ROWS - 3 * hpo, length))
    for owner in range(heads // hpo):
        rows = slice(owner * hpo, (owner + 1) * hpo)
        natural_ref[owner] = jnp.concatenate([logs[rows], enter[rows], leave[rows], fill], axis=0)
    line = lax.broadcasted_iota(jnp.int32, (ROWS, dim), 0)

    for slot in order(size):

        @plan.guard(slot)
        def _():
            table = natural_ref[partner(my_place(size), slot, size)]
            table_ref[slot] = table
            for copy in loads(slot):
                copy.wait()
            tile = jnp.zeros((ROWS, dim), F32)
            for i in range(hpo):
                lanes = plan.head(i)
                turned = k_refs[slot][:, lanes].T
                turned_refs[slot][lanes, :] = turned
                decayed = (turned.astype(F32) * table[2 * hpo + i : 2 * hpo + i + 1]).astype(BF16)
                sent_refs[slot][lanes, :] = dot(decayed, v_refs[slot][:, lanes]).astype(BF16)
                carry = jnp.broadcast_to(table[hpo + i : hpo + i + 1, last], (ROWS, dim))
                for j, part in enumerate(three_parts(carry)):
                    tile = jnp.where(line == 3 * i + j, part, tile)
            sent_refs[slot][hpo * dim :, :] = tile.astype(BF16)


def scan_kernel(plan, forward, *refs):
    size, hpo, dim = plan.size, plan.hpo, plan.dim
    in_refs, refs = refs[:size], refs[size:]
    if forward:
        local_ref, total_ref, factor_ref, carry_ref, ordered_ref = refs[-5:]
    else:
        carry_ref = refs[0]
        local_ref, total_ref, factor_ref, ordered_ref = refs[-4:]
    me = my_place(size)
    for slot, in_ref in enumerate(in_refs):
        ordered_ref[inverse(me, slot, size)] = in_ref[...]
    if forward:
        for b in range(size):
            tile = ordered_ref[b, hpo * dim :, :].astype(F32)
            for i in range(hpo):
                carry_ref[b, i : i + 1, :] = tile[3 * i : 3 * i + 1] + tile[3 * i + 1 : 3 * i + 2] + tile[3 * i + 2 : 3 * i + 3]
    for i in range(hpo):
        rows = plan.head(i)
        state = jnp.zeros((dim, dim), F32)
        factor = jnp.ones((1, dim), F32)
        for b in range(size) if forward else reversed(range(size)):
            carry = carry_ref[b, i : i + 1, :]
            local_ref[b, rows, :] = state
            factor_ref[b, i : i + 1, :] = factor
            state = carry * state + ordered_ref[b, rows, :].astype(F32)
            factor = factor * carry
        total_ref[rows, :] = state.astype(BF16)


def return_kernel(plan, local_ref, factor_ref, outer_ref, *refs):
    out_refs = refs[-plan.size :]
    me = my_place(plan.size)
    for i in range(plan.hpo):
        rows = plan.head(i)
        outer = outer_ref[rows, :].astype(F32)
        for slot, out_ref in enumerate(out_refs):
            b = inverse(me, slot, plan.size)
            out_ref[rows, :] = (local_ref[b, rows, :] + factor_ref[b, i : i + 1, :] * outer).astype(BF16)


def intra_kernel(plan, slot, first_part, table_ref, k_ref, v_ref, *refs):
    size, hpo, length = plan.size, plan.hpo, plan.length
    copies = None
    if first_part:
        q_hbm, cot_hbm = refs[:2]
        q_refs, cot_refs = refs[2 : 2 + size], refs[2 + size : 2 + 2 * size]
        mask_ref, out_ref, decayed_ref, probs_ref, weight_ref, sems = refs[2 + 2 * size :]
        q_ref = q_refs[slot]

        def loads(other):
            lanes = plan.lanes(other)
            return (
                pltpu.make_async_copy(q_hbm.at[:, lanes], q_refs[other], sems.at[0, other]),
                pltpu.make_async_copy(cot_hbm.at[:, lanes], cot_refs[other], sems.at[1, other]),
            )

        copies = [loads(other) for other in [slot] + [other for other in range(size) if other != slot]]
        others = [slot] + [other for other in range(size) if other != slot]
        for other, pair in zip(others, copies):

            @plan.guard(other)
            def _():
                for copy in pair:
                    copy.start()

        mask_ref[...] = block_mask(table_ref[0])
    else:
        q_ref, mask_ref, out_ref, decayed_ref, probs_ref, weight_ref = refs

    @plan.guard(slot)
    def _():
        if copies is not None:
            copies[0][0].wait()
        table = table_ref[slot]
        columns = table.T
        for i in range(hpo):
            lanes = plan.head(i)
            turned = q_ref[:, lanes].T
            decayed_ref[lanes, :] = (turned.astype(F32) * table[hpo + i : hpo + i + 1]).astype(BF16)
            outs = [None] * (length // HALF)
            at = 0
            for first in range(0, length, HALF):
                rows = slice(first, first + HALF)
                gap = table[i : i + 1, first:] - columns[rows, i : i + 1]
                weight = jnp.exp2(gap + mask_ref[rows, first:])
                probs = (dot(k_ref[rows, lanes], turned[:, first:]) * weight).astype(BF16)
                weight_ref[i, :, at : at + length - first] = weight.astype(BF16)
                probs_ref[i, :, at : at + length - first] = probs
                for j in range(first, length, HALF):
                    part = dot(probs[:, j - first : j - first + HALF], v_ref[rows, lanes], ((0,), (0,)))
                    outs[j // HALF] = part if outs[j // HALF] is None else outs[j // HALF] + part
                at += length - first
            for j, out in enumerate(outs):
                out_ref[j * HALF : (j + 1) * HALF, lanes] = out

    if copies is not None:
        for other, pair in zip(others, copies):

            @plan.guard(other)
            def _():
                for copy in pair if other != slot else pair[1:]:
                    copy.wait()


def token_rows(total):
    length = total.shape[0]
    return jnp.concatenate(
        [jnp.sum(total[i : i + 128].T, axis=0, keepdims=True) for i in range(0, length, 128)], axis=0
    )


def output_kernel(plan, slot, first_part, last_part, table_ref, q_ref, cot_ref, intra_ref, state_ref, *refs):
    hpo = plan.hpo
    if not first_part:
        old_ref, refs = refs[0], refs[1:]
    out_ref, total_ref = refs[:2]
    if first_part:
        total_ref[...] = jnp.zeros_like(total_ref)
    else:
        total_ref[...] = old_ref[...]

    @plan.guard(slot)
    def _():
        columns = table_ref[slot].T
        square, cross = total_ref[0], total_ref[1]
        for i in range(hpo):
            lanes = plan.head(i)
            carried = dot(q_ref[:, lanes], state_ref[lanes, :])
            out = intra_ref[:, lanes] + columns[:, hpo + i : hpo + i + 1] * carried
            out_ref[:, lanes] = out
            square = square + out * out
            cross = cross + cot_ref[:, lanes].astype(F32) * out
        total_ref[0] = square
        total_ref[1] = cross

    if last_part:
        refs[2][...] = jnp.concatenate([token_rows(total_ref[0]), token_rows(total_ref[1])], axis=0)


def factors(sums_refs, factor_ref):
    total = sums_refs[0][...]
    for ref in sums_refs[1:]:
        total = total + ref[...]
    lines = total.shape[0] // 2
    full = HEAD_TOTAL * HEAD_DIM
    scale = lax.rsqrt(total[:lines] / full + EPS)
    slope = scale * scale * scale * total[lines:] / full
    turned = jnp.concatenate([scale, slope], axis=0).T
    for j in range(2):
        for i in range(lines):
            column = turned[:, j * lines + i : j * lines + i + 1]
            factor_ref[j, i * 128 : (i + 1) * 128, :] = jnp.broadcast_to(column, (128, factor_ref.shape[2]))


def gout_kernel(plan, slot, count, *refs):
    if count:
        factor_ref = refs[count + 3]
        factors(refs[:count], factor_ref)
        out_ref, cot_ref, decayed_ref, _, gout_ref, sent_ref = refs[count:]
    else:
        factor_ref, out_ref, cot_ref, decayed_ref, gout_ref, sent_ref = refs

    @plan.guard(slot)
    def _():
        for i in range(plan.hpo):
            lanes = plan.head(i)
            gout = factor_ref[0] * cot_ref[:, lanes].astype(F32) - factor_ref[1] * out_ref[:, lanes]
            gout = gout.astype(BF16)
            gout_ref[:, lanes] = gout
            sent_ref[lanes, :] = dot(decayed_ref[lanes, :], gout).astype(BF16)


def attn_kernel(plan, factor_ref, *refs):
    size = plan.size
    for slot, (out_ref, attn_ref) in enumerate(zip(refs[:size], refs[size:])):

        @plan.guard(slot)
        def _():
            for i in range(plan.hpo):
                lanes = plan.head(i)
                attn_ref[:, lanes] = (factor_ref[0] * out_ref[:, lanes]).astype(BF16)


def stores(plan, slots, in_refs, hbms, sems):
    return [
        (slot, pltpu.make_async_copy(ref, hbm.at[:, plan.lanes(slot)], sems.at[n]))
        for n, (slot, ref, hbm) in enumerate(zip(slots, in_refs, hbms))
    ]


def start_all(plan, copies):
    for slot, copy in copies:
        plan.guard(slot)(copy.start)


def wait_all(plan, copies):
    for slot, copy in copies:
        plan.guard(slot)(copy.wait)


def gradient_kernel(plan, slot, finished, fresh, *refs):
    table_ref, k_ref, v_ref, q_ref, gout_ref, turned_ref, probs_ref, weight_ref, state_ref = refs[:9]
    refs = refs[9:]
    done_refs, refs = refs[: len(finished)], refs[len(finished) :]
    copies = []
    if finished:
        if not fresh:
            refs = refs[1:]
        copies = stores(plan, finished, done_refs, [refs[0]] * len(finished), refs[-1])
        refs = refs[1:-1]
    start_all(plan, copies)
    gq_ref, gk_ref, gv_ref = refs
    hpo, length = plan.hpo, plan.length

    @plan.guard(slot)
    def _():
        table = table_ref[slot]
        for i in range(hpo):
            lanes = plan.head(i)
            gout_turned = gout_ref[:, lanes].T
            totals = table[hpo + i : hpo + i + 1] * dot(state_ref[lanes, :], gout_turned)
            totals = [totals[:, j : j + HALF] for j in range(0, length, HALF)]
            at = 0
            for first in range(0, length, HALF):
                rows, later = slice(first, first + HALF), slice(first, length)
                size = length - first
                gv_ref[rows, lanes] = dot(probs_ref[i, :, at : at + size], gout_ref[later, lanes])
                grads = dot(v_ref[rows, lanes], gout_turned[:, later])
                grads = (grads * weight_ref[i, :, at : at + size].astype(F32)).astype(BF16)
                gk_ref[rows, lanes] = dot(grads, q_ref[later, lanes])
                piece = dot(turned_ref[lanes, rows], grads)
                for j in range(first, length, HALF):
                    totals[j // HALF] = totals[j // HALF] + piece[:, j - first : j - first + HALF]
                at += size
            for j, total in enumerate(totals):
                gq_ref[j * HALF : (j + 1) * HALF, lanes] = total.astype(BF16).T

    wait_all(plan, copies)


def final_kernel(plan, slot, finished, fresh, last_part, *refs):
    table_ref, k_ref, v_ref, gkp_ref, gvp_ref, back_ref = refs[:6]
    refs = refs[6:]
    done_refs, refs = refs[: len(finished)], refs[len(finished) :]
    if not all(fresh):
        refs = refs[fresh.count(False) :]
    gq_hbm, gk_hbm, gv_hbm, gk_ref, gv_ref, sems = refs
    hbm_of = {"gq": gq_hbm, "gk": gk_hbm, "gv": gv_hbm}
    copies = stores(plan, [s for _, s in finished], done_refs, [hbm_of[name] for name, _ in finished], sems)
    start_all(plan, copies)

    @plan.guard(slot)
    def _():
        columns = table_ref[slot].T
        for i in range(plan.hpo):
            lanes = plan.head(i)
            leave = columns[:, 2 * plan.hpo + i : 2 * plan.hpo + i + 1]
            back = back_ref[lanes, :]
            gk_ref[:, lanes] = (gkp_ref[:, lanes] + leave * dot_nt(v_ref[:, lanes], back)).astype(BF16)
            gv_ref[:, lanes] = (gvp_ref[:, lanes] + leave * dot(k_ref[:, lanes], back)).astype(BF16)

    if last_part:
        own = len(finished)
        lanes = plan.lanes(slot)
        tail = [
            (slot, pltpu.make_async_copy(gk_ref, gk_hbm.at[:, lanes], sems.at[own])),
            (slot, pltpu.make_async_copy(gv_ref, gv_hbm.at[:, lanes], sems.at[own + 1])),
        ]
        start_all(plan, tail)
        copies = copies + tail
    wait_all(plan, copies)


def exchange(arrays, size, halves, target):
    def pairs(slot):
        return [(base + i, base + target(i, slot, size)) for base in range(0, halves * size, size) for i in range(size)]

    return [arrays[0]] + [lax.ppermute(arrays[slot], "seq", pairs(slot)) for slot in range(1, size)]


def per_device(queries, keys, values, cotangent, log_decay, starts):
    length, width = queries.shape
    heads = log_decay.shape[0]
    dim = width // heads
    blocks = lax.axis_size("seq")
    shares = lax.axis_size("head")
    halves = 2 if blocks % 2 == 0 else 1
    size = blocks // halves
    plan = Plan(heads, dim, length, size)
    hpo, span = plan.hpo, plan.span
    params = pltpu.CompilerParams(vmem_limit_bytes=12 << 20)

    inside = pl.BlockSpec(memory_space=pltpu.VMEM)
    unused = pl.BlockSpec(memory_space=pl.ANY)
    hbm = pl.BlockSpec(memory_space=pltpu.HBM)
    dma = pltpu.SemaphoreType.DMA
    whole = pltpu.HBM((length, width), BF16)

    def outside(array):
        return pltpu.with_memory_space_constraint(array, pltpu.HBM)

    def held(dtype, columns=span):
        return pltpu.VMEM((length, columns), dtype)

    def cost(products, exps=0):
        return pl.CostEstimate(flops=2 * hpo * products, bytes_accessed=length * span, transcendentals=hpo * exps)

    def call(kernel, name, operands, results, work, extra=(), scratch=(), aliases=None):
        far = [isinstance(a, tuple) for a in operands]
        return pl.pallas_call(
            kernel,
            in_specs=[hbm if f else inside for f in far] + [unused] * len(extra),
            out_specs=[hbm if r is whole else inside for r in results],
            out_shape=list(results),
            scratch_shapes=list(scratch),
            input_output_aliases=aliases or {},
            compiler_params=params,
            cost_estimate=work,
            name=name,
        )(*[a[0] if f else a for a, f in zip(operands, far)], *extra)

    def scan(arrays, carries, after, later):
        forward = carries is None
        factor = pltpu.VMEM((size, 8, dim), F32)
        local, total, factor, *rest = call(
            functools.partial(scan_kernel, plan, forward),
            "scan",
            [*arrays] + ([] if forward else [carries]),
            [pltpu.VMEM((size, span, dim), F32), pltpu.VMEM((span, dim), BF16), factor] + ([factor] if forward else []),
            None,
            after,
            [pltpu.VMEM((size, *arrays[0].shape), BF16)],
        )
        if halves == 2:
            pairs = [(i, i + size) if forward else (i + size, i) for i in range(size)]
            outer = lax.ppermute(total, "seq", pairs)
        else:
            outer = jnp.zeros_like(total)
        back = call(
            functools.partial(return_kernel, plan),
            "return",
            [local, factor, outer],
            [pltpu.VMEM((span, dim), BF16)] * size,
            None,
            later,
        )
        return exchange(back, size, halves, inverse), (rest[0] if forward else None)

    big, small = length * length * dim, length * dim * dim
    queries, keys, values, cotangent = (outside(a) for a in (queries, keys, values, cotangent))
    results = call(
        functools.partial(update_kernel, plan),
        "update",
        [(outside(log_decay),), (outside(starts.reshape(1, length)),), (keys,), (values,)],
        [pltpu.VMEM((span + ROWS, dim), BF16)] * size
        + [held(BF16)] * (2 * size)
        + [pltpu.VMEM((span, length), BF16)] * size
        + [pltpu.VMEM((size, ROWS, length), F32)],
        cost(size * small),
        scratch=[
            pltpu.VMEM((heads, length), F32),
            pltpu.VMEM((1, length), jnp.int32),
            pltpu.VMEM((heads // hpo, ROWS, length), F32),
            dma((2,)),
            dma((2, size)),
        ],
    )
    sent, k, v, turned = (results[i * size : (i + 1) * size] for i in range(4))
    table = results[-1]
    received = exchange(sent, size, halves, partner)

    lower = length * (length + HALF) // 2 // HALF
    kept = pltpu.VMEM((hpo, HALF, lower), BF16)
    intra, decayed, probs, weights = [], [], [], []
    for slot in range(size):
        first = slot == 0
        results = call(
            functools.partial(intra_kernel, plan, slot, first),
            "intra",
            [table, k[slot], v[slot]] + ([(queries,), (cotangent,)] if first else [q[slot], mask]),
            ([held(BF16)] * (2 * size) + [pltpu.VMEM((length, length), F32)] if first else [])
            + [held(F32), pltpu.VMEM((span, length), BF16), kept, kept],
            cost(2 * big, length * length),
            scratch=[dma((2, size))] if first else [],
        )
        if first:
            q, cot, mask = results[:size], results[size : 2 * size], results[2 * size]
        for kind, result in zip((intra, decayed, probs, weights), results[-4:]):
            kind.append(result)

    middle = -(-size // 2)
    received, carries = scan(received, None, intra[:middle], intra[middle:])

    outputs = []
    total = sums = None
    for slot in range(size):
        first, last = slot == 0, slot == size - 1
        out, total, *rest = call(
            functools.partial(output_kernel, plan, slot, first, last),
            "output",
            [table, q[slot], cot[slot], intra[slot], received[slot]] + ([] if first else [total]),
            [held(F32), pltpu.VMEM((2, length, dim), F32)] + ([pltpu.VMEM((2 * length // 128, 128), F32)] if last else []),
            cost(small),
        )
        outputs.append(out)
        sums = rest[0] if last else sums
    states = received

    everyone = [sums] + [
        lax.ppermute(sums, "head", [(i, (i + k) % shares) for i in range(shares)]) for k in range(1, shares)
    ]

    gout, sent = [None] * size, [None] * size
    factor = None
    for slot in order(size):
        first = factor is None
        *rest, gout[slot], sent[slot] = call(
            functools.partial(gout_kernel, plan, slot, shares if first else 0),
            "gout",
            (everyone if first else [factor]) + [outputs[slot], cot[slot], decayed[slot]],
            ([pltpu.VMEM((2, length, dim), F32)] if first else []) + [held(BF16), pltpu.VMEM((span, dim), BF16)],
            cost(small),
        )
        factor = rest[0] if first else factor
    received = exchange(sent, size, halves, partner)
    attn = call(
        functools.partial(attn_kernel, plan),
        "attn",
        [factor, *outputs],
        [held(BF16)] * size,
        cost(small),
    )

    gq, gk_part, gv_part = [], [], []
    attn_whole = gq_whole = None
    for slot in range(size):
        fresh = slot < 2
        finished = list(range(size)) if slot == 0 else [slot - 1]
        done = list(attn) if slot == 0 else [gq[slot - 1]]
        operands = [table, k[slot], v[slot], q[slot], gout[slot], turned[slot], probs[slot], weights[slot], states[slot]]
        operands += done
        results = call(
            functools.partial(gradient_kernel, plan, slot, finished, fresh),
            "gradient",
            operands + ([] if fresh else [(gq_whole,)]),
            [whole, held(BF16), held(F32), held(F32)],
            cost(4 * big),
            scratch=[dma((len(finished),))],
            aliases={} if fresh else {len(operands): 0},
        )
        if slot == 0:
            attn_whole = results[0]
        else:
            gq_whole = results[0]
        for kind, result in zip((gq, gk_part, gv_part), results[1:]):
            kind.append(result)

    received, _ = scan(received, carries, gk_part[:1], gk_part[1:-1])

    gk_whole = gv_whole = None
    gk = gv = None
    for slot in range(size):
        first, last = slot == 0, slot == size - 1
        finished = [("gq", size - 1)] if first else [("gk", slot - 1), ("gv", slot - 1)]
        done = [gq[-1]] if first else [gk, gv]
        operands = [table, k[slot], v[slot], gk_part[slot], gv_part[slot], received[slot]] + done
        held_back = [gq_whole, gk_whole, gv_whole]
        fresh = [a is None for a in held_back]
        aliases = {}
        chained = []
        for n, array in enumerate(held_back):
            if array is not None:
                aliases[len(operands) + len(chained)] = n
                chained.append((array,))
        gq_whole, gk_whole, gv_whole, gk, gv = call(
            functools.partial(final_kernel, plan, slot, finished, fresh, last),
            "final",
            operands + chained,
            [whole] * 3 + [held(BF16)] * 2,
            cost(2 * small),
            scratch=[dma((len(finished) + 2,))],
            aliases=aliases,
        )
    return (attn_whole, gq_whole, gk_whole, gv_whole)


def solution(mesh):
    wide = P("seq", "head")
    return jax.shard_map(
        per_device,
        mesh=mesh,
        in_specs=(wide, wide, wide, wide, P("head", "seq"), P("seq")),
        out_specs=(wide, wide, wide, wide),
        check_vma=False,
    )
```

time: 720 us -> 71.3 us (0.10)
  matrix products: 272 us -> 0 us
  waiting for transfers between devices: 167 us -> 9.32 us
  local copies, waits for them, and re-layouts: 116 us -> 0 us
  other arithmetic: 73 us -> 0 us
  loops' own time: 41.5 us -> 0 us
  Pallas kernels: 0 us -> 37.7 us
  blocking collectives: 29.1 us -> 0 us
  starting transfers between devices: 0.08 us -> 23.1 us
  between operations: 14.8 us -> 1.07 us
    dot_general x162 -> x0, matrix products: 272 us -> none  [the longest x16 34.8 us: local_forward(): jnp.einsum('td,sd->ts', query_head, key_head, preferred_element_type=jnp....]
    all_gather x2 -> x0, waiting for transfers between devices: 167 us -> none  [the longest x1 120 us: prefix(): gathered = jax.tree.map(lambda a: lax.all_gather(a, axis), part)]
    slice x80 -> x0, local copies, waits for them, and re-layouts: 46.2 us -> none  [the longest x48 27.5 us: block_factors(): cum_log[:, -1:] - cum_log]
    another operation x3 -> x0, loops' own time: 41.5 us -> none  [the longest x1 21.3 us: per_device(): lax.map(local_forward, (query_heads, key_heads, value_heads, log_decay))]
    pallas_call x0 -> x26, Pallas kernels: none -> 37.7 us  [call(): pl.pallas_call(kernel, in_specs=[hbm if f else inside for f in far] + [un...]
    select_n x65 -> x0, other arithmetic: 31.4 us -> none  [the longest x32 31.1 us: block_factors(): jnp.where(doc_count[None, :] == doc_count[-1], jnp.exp(cum_log[:, -1:] -...]
    unnamed x1 -> x0, blocking collectives: 23.4 us -> none
    dynamic_slice x32 -> x0, local copies, waits for them, and re-layouts: 23.2 us -> none  [per_device(): lax.map(local_forward, (query_heads, key_heads, value_heads, log_decay))]
  transfers between devices with their start and end apart: 2 -> 17, of which waited for: 2 -> 6; matrix products, arithmetic and copies ran while one was open for 1% -> 0% of each run, Pallas kernels for 0% -> 41%
where the time goes in v3:
time: 71.3 us; the launch traced here: 71.1 us
  Pallas kernels  37.7 us (53%)
  starting transfers between devices  23.1 us (32%)
  waiting for transfers between devices  9.32 us (13%)
  between operations  1.07 us (2%)
    pallas_call x26, Pallas kernels, call(): pl.pallas_call(kernel, in_specs=[hbm if f else inside for f in far] + [un...  37.7 us
    ppermute x12, starting transfers between devices, exchange(): lax.ppermute(arrays[slot], 'seq', pairs(slot))  15.4 us
    ppermute x2, starting transfers between devices, scan(): outer = lax.ppermute(total, 'seq', pairs)  5.95 us
    ppermute x12, waiting for transfers between devices, exchange(): lax.ppermute(arrays[slot], 'seq', pairs(slot))  4.86 us
    ppermute x3, waiting for transfers between devices, per_device(): lax.ppermute(sums, 'head', [(i, (i + k) % shares) for i in range(shares)])  2.8 us
    ppermute x3, starting transfers between devices, per_device(): lax.ppermute(sums, 'head', [(i, (i + k) % shares) for i in range(shares)])  1.74 us
    ppermute x2, waiting for transfers between devices, scan(): outer = lax.ppermute(total, 'seq', pairs)  1.66 us
  transfers between devices with their start and end apart: 17, of which 6 were waited for; matrix products, arithmetic and copies ran while one was open for 0% of the time, Pallas kernels for 41%

profile of v3, /device:TPU:0, one launch (start us, length us, event | category | flops | bytes accessed | tf_op | source)
XLA Modules:
  0.0 71.1 jit_solution(4305540039618259081)
XLA Ops:
  0.6 2.9 %update.1 = (bf16[528,128]{1,0:T(8,128)(2,1)S(1)}, bf16[528,128]{1,0:T(8,128)(2,1)S(1)}, bf16[528,128]{1,0:T(8,128)(2,1)S(1)}, bf16[528,128]{1,0:T(8,128)(2,1)S(...) custom-call(f32[16,512]{1,0:T(8,128)} %logs_hbm.1, ...), custom_call_target="tpu_custom_call" | custom-call | flops 268435456 | bytes 262144 | tf_op jit(solution)/shard_map/update/pallas_call | solution.py:464
  3.6 3.0 %collective-permute-start = (bf16[528,128]{1,0:T(8,128)(2,1)S(1)}, bf16[528,128]{1,0:T(8,128)(2,1)S(1)}, u32[]{:S(2)}, u32[]{:S(2)}) collective-permute-start(bf16[528,128]{1,0:T(8,128)(2,1)S(1)} %get-tuple-element.127), channel_id=1, source_target_pairs={{0,4},{4,0},{8,12},{12,8},{16,20},{20,16},{24,28},{28,24},{1,5},{5... | collective-permute-start | bytes 405512 | tf_op jit(solution)/shard_map/ppermute | solution.py:432
  6.6 1.6 %collective-permute-start.1 = (bf16[528,128]{1,0:T(8,128)(2,1)S(1)}, bf16[528,128]{1,0:T(8,128)(2,1)S(1)}, u32[]{:S(2)}, u32[]{:S(2)}) collective-permute-start(bf16[528,128]{1,0:T(8,128)(2,1)S(1)} %get-tuple-element.128), channel_id=1, source_target_pairs={{0,8},{4,12},{8,0},{12,4},{16,24},{20,28},{24,16},{28,20},{1,9},{5... | collective-permute-start | bytes 405512 | tf_op jit(solution)/shard_map/ppermute | solution.py:432
  8.2 3.1 %intra.4 = (bf16[512,512]{1,0:T(8,128)(2,1)S(1)}, bf16[512,512]{1,0:T(8,128)(2,1)S(1)}, bf16[512,512]{1,0:T(8,128)(2,1)S(1)}, bf16[512,512]{1,0:T(8,128)(2,1)S(1...) custom-call(f32[4,16,512]{2,1,0:T(8,128)S(1)} %get-tuple-element.116, ...), custom_call_target="tpu_custom_call" | custom-call | flops 536870912 | bytes 262144 | tf_op jit(solution)/shard_map/intra/pallas_call | solution.py:464
  11.3 1.9 %intra.6 = (f32[512,512]{1,0:T(8,128)S(1)}, bf16[512,512]{1,0:T(8,128)(2,1)S(1)}, bf16[4,256,768]{2,1,0:T(8,128)(2,1)S(1)}, bf16[4,256,768]{2,1,0:T(8,128)(2,1)S(1)}) custom-call(f32[4,16,512]{2,1,0:T(8,128)S(1)} %get-tuple-element.116.table_ref.refs_0_, bf16[512,512]{1,0:T(8,128)(2,1)S(1)} %get-tuple-element.131.k_ref.refs_1_, ...), custom_call_target="tpu_custom_call" | custom-call | flops 536870912 | bytes 262144 | tf_op jit(solution)/shard_map/intra/pallas_call | solution.py:464
  13.3 1.1 %collective-permute-done.2.refs_3_ = bf16[528,128]{1,0:T(8,128)(2,1)S(1)} collective-permute-done((bf16[528,128]{1,0:T(8,128)(2,1)S(1)}, bf16[528,128]{1,0:T(8,128)(2,1)S(1)}, u32[]{:S(2)}, u32[]{:S(2)}) %collective-permute-start.2) | collective-permute-done | bytes 135200 | tf_op jit(solution)/shard_map/ppermute | solution.py:432
  14.5 4.7 %collective-permute-start.3 = (bf16[512,128]{1,0:T(8,128)(2,1)S(1)}, bf16[512,128]{1,0:T(8,128)(2,1)S(1)}, u32[]{:S(2)}, u32[]{:S(2)}) collective-permute-start(bf16[512,128]{1,0:T(8,128)(2,1)S(1)} %get-tuple-element.137), channel_id=1, source_target_pairs={{0,16},{4,20},{8,24},{12,28},{1,17},{5,21},{9,25},{13,29},{2,18},{... | collective-permute-start | bytes 393224 | tf_op jit(solution)/shard_map/ppermute | solution.py:490
  19.2 1.9 %intra.5 = (f32[512,512]{1,0:T(8,128)S(1)}, bf16[512,512]{1,0:T(8,128)(2,1)S(1)}, bf16[4,256,768]{2,1,0:T(8,128)(2,1)S(1)}, bf16[4,256,768]{2,1,0:T(8,128)(2,1)S(1)}) custom-call(f32[4,16,512]{2,1,0:T(8,128)S(1)} %get-tuple-element.116.table_ref.refs_0_, bf16[512,512]{1,0:T(8,128)(2,1)S(1)} %get-tuple-element.122.k_ref.refs_1_, ...), custom_call_target="tpu_custom_call" | custom-call | flops 536870912 | bytes 262144 | tf_op jit(solution)/shard_map/intra/pallas_call | solution.py:464
  21.1 1.9 %intra.7 = (f32[512,512]{1,0:T(8,128)S(1)}, bf16[512,512]{1,0:T(8,128)(2,1)S(1)}, bf16[4,256,768]{2,1,0:T(8,128)(2,1)S(1)}, bf16[4,256,768]{2,1,0:T(8,128)(2,1)S(1)}) custom-call(f32[4,16,512]{2,1,0:T(8,128)S(1)} %get-tuple-element.116.table_ref.refs_0_, bf16[512,512]{1,0:T(8,128)(2,1)S(1)} %get-tuple-element.138.k_ref.refs_1_, ...), custom_call_target="tpu_custom_call" | custom-call | flops 536870912 | bytes 262144 | tf_op jit(solution)/shard_map/intra/pallas_call | solution.py:464
  23.2 1.6 %collective-permute-start.6 = (bf16[512,128]{1,0:T(8,128)(2,1)S(1)}, bf16[512,128]{1,0:T(8,128)(2,1)S(1)}, u32[]{:S(2)}, u32[]{:S(2)}) collective-permute-start(bf16[512,128]{1,0:T(8,128)(2,1)S(1)} %get-tuple-element.146), channel_id=1, source_target_pairs={{0,4},{4,0},{8,12},{12,8},{16,20},{20,16},{24,28},{28,24},{1,5},{5... | collective-permute-start | bytes 393224 | tf_op jit(solution)/shard_map/ppermute | solution.py:432
  24.8 1.6 %collective-permute-start.5 = (bf16[512,128]{1,0:T(8,128)(2,1)S(1)}, bf16[512,128]{1,0:T(8,128)(2,1)S(1)}, u32[]{:S(2)}, u32[]{:S(2)}) collective-permute-start(bf16[512,128]{1,0:T(8,128)(2,1)S(1)} %get-tuple-element.144), channel_id=1, source_target_pairs={{0,8},{4,12},{8,0},{12,4},{16,24},{20,28},{24,16},{28,20},{1,9},{5... | collective-permute-start | bytes 393224 | tf_op jit(solution)/shard_map/ppermute | solution.py:432
  27.3 2.3 %collective-permute-done.6.state_ref.refs_8_ = bf16[512,128]{1,0:T(8,128)(2,1)S(1)} collective-permute-done((bf16[512,128]{1,0:T(8,128)(2,1)S(1)}, bf16[512,128]{1,0:T(8,128)(2,1)S(1)}, u32[]{:S(2)}, u32[]{:S(2)}) %collective-permute-start.6) | collective-permute-done | bytes 131104 | tf_op jit(solution)/shard_map/ppermute | solution.py:432
  30.8 1.4 %collective-permute-done.4.state_ref.refs_8_ = bf16[512,128]{1,0:T(8,128)(2,1)S(1)} collective-permute-done((bf16[512,128]{1,0:T(8,128)(2,1)S(1)}, bf16[512,128]{1,0:T(8,128)(2,1)S(1)}, u32[]{:S(2)}, u32[]{:S(2)}) %collective-permute-start.4) | collective-permute-done | bytes 131104 | tf_op jit(solution)/shard_map/ppermute | solution.py:432
  32.2 1.4 %output.7 = (f32[512,512]{1,0:T(8,128)S(1)}, f32[2,512,128]{2,1,0:T(8,128)}, f32[8,128]{1,0:T(8,128)S(1)}) custom-call(f32[4,16,512]{2,1,0:T(8,128)S(1)} %get-tuple-element.116.table_ref.refs_0_, bf16[512,512]{1,0:T(8,128)(2,1)S(1)} %get-tuple-element.120.refs_0_.q_ref.refs_3_, bf16[512,512]{1,0:T(8,128)(2,1)S(1)} %get-tuple-element.121.cot_ref.refs_2_, ...), custom_call_target="tpu_custom_call" | custom-call | flops 67108864 | bytes 262144 | tf_op jit(solution)/shard_map/output/pallas_call | solution.py:464
  33.6 1.5 %collective-permute-start.8 = (f32[8,128]{1,0:T(8,128)S(1)}, f32[8,128]{1,0:T(8,128)S(1)}, u32[]{:S(2)}, u32[]{:S(2)}) collective-permute-start(f32[8,128]{1,0:T(8,128)S(1)} %get-tuple-element.152.refs_0_), channel_id=1, source_target_pairs={{0,2},{1,3},{2,0},{3,1},{4,6},{5,7},{6,4},{7,5},{8,10},{9,11},{10,... | collective-permute-start | bytes 12296 | tf_op jit(solution)/shard_map/ppermute | solution.py:564
  35.4 1.9 %collective-permute-done.8.refs_2_ = f32[8,128]{1,0:T(8,128)S(1)} collective-permute-done((f32[8,128]{1,0:T(8,128)S(1)}, f32[8,128]{1,0:T(8,128)S(1)}, u32[]{:S(2)}, u32[]{:S(2)}) %collective-permute-start.8) | collective-permute-done | bytes 4128 | tf_op jit(solution)/shard_map/ppermute | solution.py:564
  37.2 0.9 %collective-permute-done.7.refs_1_ = f32[8,128]{1,0:T(8,128)S(1)} collective-permute-done((f32[8,128]{1,0:T(8,128)S(1)}, f32[8,128]{1,0:T(8,128)S(1)}, u32[]{:S(2)}, u32[]{:S(2)}) %collective-permute-start.7) | collective-permute-done | bytes 4128 | tf_op jit(solution)/shard_map/ppermute | solution.py:564
  38.9 0.9 %collective-permute-start.10 = (bf16[512,128]{1,0:T(8,128)(2,1)S(1)}, bf16[512,128]{1,0:T(8,128)(2,1)S(1)}, u32[]{:S(2)}, u32[]{:S(2)}) collective-permute-start(bf16[512,128]{1,0:T(8,128)(2,1)S(1)} %get-tuple-element.191), channel_id=1, source_target_pairs={{0,4},{4,0},{8,12},{12,8},{16,20},{20,16},{24,28},{28,24},{1,5},{5... | collective-permute-start | bytes 393224 | tf_op jit(solution)/shard_map/ppermute | solution.py:432
  40.2 1.2 %collective-permute-start.11 = (bf16[512,128]{1,0:T(8,128)(2,1)S(1)}, bf16[512,128]{1,0:T(8,128)(2,1)S(1)}, u32[]{:S(2)}, u32[]{:S(2)}) collective-permute-start(bf16[512,128]{1,0:T(8,128)(2,1)S(1)} %get-tuple-element.192), channel_id=1, source_target_pairs={{0,8},{4,12},{8,0},{12,4},{16,24},{20,28},{24,16},{28,20},{1,9},{5... | collective-permute-start | bytes 393224 | tf_op jit(solution)/shard_map/ppermute | solution.py:432
  41.9 1.6 %collective-permute-start.12 = (bf16[512,128]{1,0:T(8,128)(2,1)S(1)}, bf16[512,128]{1,0:T(8,128)(2,1)S(1)}, u32[]{:S(2)}, u32[]{:S(2)}) collective-permute-start(bf16[512,128]{1,0:T(8,128)(2,1)S(1)} %get-tuple-element.193), channel_id=1, source_target_pairs={{0,12},{4,8},{8,4},{12,0},{16,28},{20,24},{24,20},{28,16},{1,13},{... | collective-permute-start | bytes 393224 | tf_op jit(solution)/shard_map/ppermute | solution.py:432
  44.4 3.6 %gradient.4 = (bf16[512,2048]{1,0:T(8,128)(2,1)}, bf16[512,512]{1,0:T(8,128)(2,1)S(1)}, f32[512,512]{1,0:T(8,128)S(1)}, f32[512,512]{1,0:T(8,128)S(1)}) custom-call(f32[4,16,512]{2,1,0:T(8,128)S(1)} %get-tuple-element.116.table_ref.refs_0_, bf16[512,512]{1,0:T(8,128)(2,1)S(1)} %get-tuple-element.117.k_ref.refs_1_, ...), custom_call_target="tpu_custom_call" | custom-call | flops 1073741824 | bytes 262144 | tf_op jit(solution)/shard_map/gradient/pallas_call | solution.py:464
  48.3 1.3 %collective-permute-start.13 = (bf16[512,128]{1,0:T(8,128)(2,1)S(1)}, bf16[512,128]{1,0:T(8,128)(2,1)S(1)}, u32[]{:S(2)}, u32[]{:S(2)}) collective-permute-start(bf16[512,128]{1,0:T(8,128)(2,1)S(1)} %get-tuple-element.198), channel_id=1, source_target_pairs={{16,0},{20,4},{24,8},{28,12},{17,1},{21,5},{25,9},{29,13},{18,2},{... | collective-permute-start | bytes 393224 | tf_op jit(solution)/shard_map/ppermute | solution.py:490
  49.6 3.1 %gradient.5 = (bf16[512,2048]{1,0:T(8,128)(2,1)}, bf16[512,512]{1,0:T(8,128)(2,1)S(1)}, f32[512,512]{1,0:T(8,128)S(1)}, f32[512,512]{1,0:T(8,128)S(1)}) custom-call(f32[4,16,512]{2,1,0:T(8,128)S(1)} %get-tuple-element.116.table_ref.refs_0_, bf16[512,512]{1,0:T(8,128)(2,1)S(1)} %get-tuple-element.131.k_ref.refs_1_, ...), custom_call_target="tpu_custom_call" | custom-call | flops 1073741824 | bytes 262144 | tf_op jit(solution)/shard_map/gradient/pallas_call | solution.py:464
  52.7 3.1 %gradient.6 = (bf16[512,2048]{1,0:T(8,128)(2,1)}, bf16[512,512]{1,0:T(8,128)(2,1)S(1)}, f32[512,512]{1,0:T(8,128)S(1)}, f32[512,512]{1,0:T(8,128)S(1)}) custom-call(f32[4,16,512]{2,1,0:T(8,128)S(1)} %get-tuple-element.116.table_ref.refs_0_, bf16[512,512]{1,0:T(8,128)(2,1)S(1)} %get-tuple-element.138.k_ref.refs_1_, ...), custom_call_target="tpu_custom_call", output_to_operand_aliasing={{0}: (10, {})} | custom-call | flops 1073741824 | bytes 262144 | tf_op jit(solution)/shard_map/gradient/pallas_call | solution.py:464
  55.8 1.7 %collective-permute-done.13.outer_ref = bf16[512,128]{1,0:T(8,128)(2,1)S(1)} collective-permute-done((bf16[512,128]{1,0:T(8,128)(2,1)S(1)}, bf16[512,128]{1,0:T(8,128)(2,1)S(1)}, u32[]{:S(2)}, u32[]{:S(2)}) %collective-permute-start.13) | collective-permute-done | bytes 131104 | tf_op jit(solution)/shard_map/ppermute | solution.py:490
  57.6 0.8 %collective-permute-start.16 = (bf16[512,128]{1,0:T(8,128)(2,1)S(1)}, bf16[512,128]{1,0:T(8,128)(2,1)S(1)}, u32[]{:S(2)}, u32[]{:S(2)}) collective-permute-start(bf16[512,128]{1,0:T(8,128)(2,1)S(1)} %get-tuple-element.205), channel_id=1, source_target_pairs={{0,4},{4,0},{8,12},{12,8},{16,20},{20,16},{24,28},{28,24},{1,5},{5... | collective-permute-start | bytes 393224 | tf_op jit(solution)/shard_map/ppermute | solution.py:432
  58.5 2.7 %collective-permute-start.14 = (bf16[512,128]{1,0:T(8,128)(2,1)S(1)}, bf16[512,128]{1,0:T(8,128)(2,1)S(1)}, u32[]{:S(2)}, u32[]{:S(2)}) collective-permute-start(bf16[512,128]{1,0:T(8,128)(2,1)S(1)} %get-tuple-element.201), channel_id=1, source_target_pairs={{0,12},{4,8},{8,4},{12,0},{16,28},{20,24},{24,20},{28,16},{1,13},{... | collective-permute-start | bytes 393224 | tf_op jit(solution)/shard_map/ppermute | solution.py:432
  61.1 3.1 %gradient.7 = (bf16[512,2048]{1,0:T(8,128)(2,1)}, bf16[512,512]{1,0:T(8,128)(2,1)S(1)}, f32[512,512]{1,0:T(8,128)S(1)}, f32[512,512]{1,0:T(8,128)S(1)}) custom-call(f32[4,16,512]{2,1,0:T(8,128)S(1)} %get-tuple-element.116.table_ref.refs_0_, bf16[512,512]{1,0:T(8,128)(2,1)S(1)} %get-tuple-element.122.k_ref.refs_1_, ...), custom_call_target="tpu_custom_call", output_to_operand_aliasing={{0}: (10, {})} | custom-call | flops 1073741824 | bytes 262144 | tf_op jit(solution)/shard_map/gradient/pallas_call | solution.py:464
  64.2 1.2 %final.4 = (bf16[512,2048]{1,0:T(8,128)(2,1)}, bf16[512,2048]{1,0:T(8,128)(2,1)}, bf16[512,2048]{1,0:T(8,128)(2,1)}, bf16[512,512]{1,0:T(8,128)(2,1)S(1)}, bf16[512,512]{1,0:T(8,128)(2,1)S(1)}) custom-call(f32[4,16,512]{2,1,0:T(8,128)S(1)} %get-tuple-element.116.table_ref.refs_0_, ...), custom_call_target="tpu_custom_call", output_to_operand_aliasing={{0}: (7, {})} | custom-call | flops 134217728 | bytes 262144 | tf_op jit(solution)/shard_map/final/pallas_call | solution.py:464
  65.5 1.4 %final.5 = (bf16[512,2048]{1,0:T(8,128)(2,1)}, bf16[512,2048]{1,0:T(8,128)(2,1)}, bf16[512,2048]{1,0:T(8,128)(2,1)}, bf16[512,512]{1,0:T(8,128)(2,1)S(1)}, bf16[512,512]{1,0:T(8,128)(2,1)S(1)}) custom-call(f32[4,16,512]{2,1,0:T(8,128)S(1)} %get-tuple-element.116.table_ref.refs_0_, ...), custom_call_target="tpu_custom_call", output_to_operand_aliasing={{0}: (8, {}), {1}: (9, {}), {2}: (10, {})} | custom-call | flops 134217728 | bytes 262144 | tf_op jit(solution)/shard_map/final/pallas_call | solution.py:464
  66.9 1.4 %final.6 = (bf16[512,2048]{1,0:T(8,128)(2,1)}, bf16[512,2048]{1,0:T(8,128)(2,1)}, bf16[512,2048]{1,0:T(8,128)(2,1)}, bf16[512,512]{1,0:T(8,128)(2,1)S(1)}, bf16[512,512]{1,0:T(8,128)(2,1)S(1)}) custom-call(f32[4,16,512]{2,1,0:T(8,128)S(1)} %get-tuple-element.116.table_ref.refs_0_, ...), custom_call_target="tpu_custom_call", output_to_operand_aliasing={{0}: (8, {}), {1}: (9, {}), {2}: (10, {})} | custom-call | flops 134217728 | bytes 262144 | tf_op jit(solution)/shard_map/final/pallas_call | solution.py:464
  68.3 2.6 %final.7 = (bf16[512,2048]{1,0:T(8,128)(2,1)}, bf16[512,2048]{1,0:T(8,128)(2,1)}, bf16[512,2048]{1,0:T(8,128)(2,1)}, bf16[512,512]{1,0:T(8,128)(2,1)}, bf16[512,512]{1,0:T(8,128)(2,1)}) custom-call(f32[4,16,512]{2,1,0:T(8,128)S(1)} %get-tuple-element.116.table_ref.refs_0_, ...), custom_call_target="tpu_custom_call", output_to_operand_aliasing={{0}: (8, {}), {1}: (9, {}), {2}: (10, {})} | custom-call | flops 134217728 | bytes 262144 | tf_op jit(solution)/shard_map/final/pallas_call | solution.py:464
  (28 shorter events, 5.5 us)
Async XLA Ops:
  3.6 9.6 %collective-permute-start = (bf16[528,128]{1,0:T(8,128)(2,1)S(1)}, bf16[528,128]{1,0:T(8,128)(2,1)S(1)}, u32[]{:S(2)}, u32[]{:S(2)}) collective-permute-start(bf16[528,128]{1,0:T(8,128)(2,1)S(1)} %get-tuple-element.127), channel_id=1, source_target_pairs={{0,4},{4,0},{8,12},{12,8},{16,20},{20,16},{24,28},{28,24},{1,5},{5... | collective-permute-start | bytes 405512 | tf_op jit(solution)/shard_map/ppermute | solution.py:432
  6.6 6.7 %collective-permute-start.1 = (bf16[528,128]{1,0:T(8,128)(2,1)S(1)}, bf16[528,128]{1,0:T(8,128)(2,1)S(1)}, u32[]{:S(2)}, u32[]{:S(2)}) collective-permute-start(bf16[528,128]{1,0:T(8,128)(2,1)S(1)} %get-tuple-element.128), channel_id=1, source_target_pairs={{0,8},{4,12},{8,0},{12,4},{16,24},{20,28},{24,16},{28,20},{1,9},{5... | collective-permute-start | bytes 405512 | tf_op jit(solution)/shard_map/ppermute | solution.py:432
  8.2 6.2 %collective-permute-start.2 = (bf16[528,128]{1,0:T(8,128)(2,1)S(1)}, bf16[528,128]{1,0:T(8,128)(2,1)S(1)}, u32[]{:S(2)}, u32[]{:S(2)}) collective-permute-start(bf16[528,128]{1,0:T(8,128)(2,1)S(1)} %get-tuple-element.129), channel_id=1, source_target_pairs={{0,12},{4,8},{8,4},{12,0},{16,28},{20,24},{24,20},{28,16},{1,13},{... | collective-permute-start | bytes 405512 | tf_op jit(solution)/shard_map/ppermute | solution.py:432
  14.5 8.6 %collective-permute-start.3 = (bf16[512,128]{1,0:T(8,128)(2,1)S(1)}, bf16[512,128]{1,0:T(8,128)(2,1)S(1)}, u32[]{:S(2)}, u32[]{:S(2)}) collective-permute-start(bf16[512,128]{1,0:T(8,128)(2,1)S(1)} %get-tuple-element.137), channel_id=1, source_target_pairs={{0,16},{4,20},{8,24},{12,28},{1,17},{5,21},{9,25},{13,29},{2,18},{... | collective-permute-start | bytes 393224 | tf_op jit(solution)/shard_map/ppermute | solution.py:490
  23.2 6.4 %collective-permute-start.6 = (bf16[512,128]{1,0:T(8,128)(2,1)S(1)}, bf16[512,128]{1,0:T(8,128)(2,1)S(1)}, u32[]{:S(2)}, u32[]{:S(2)}) collective-permute-start(bf16[512,128]{1,0:T(8,128)(2,1)S(1)} %get-tuple-element.146), channel_id=1, source_target_pairs={{0,4},{4,0},{8,12},{12,8},{16,20},{20,16},{24,28},{28,24},{1,5},{5... | collective-permute-start | bytes 393224 | tf_op jit(solution)/shard_map/ppermute | solution.py:432
  24.8 5.5 %collective-permute-start.5 = (bf16[512,128]{1,0:T(8,128)(2,1)S(1)}, bf16[512,128]{1,0:T(8,128)(2,1)S(1)}, u32[]{:S(2)}, u32[]{:S(2)}) collective-permute-start(bf16[512,128]{1,0:T(8,128)(2,1)S(1)} %get-tuple-element.144), channel_id=1, source_target_pairs={{0,8},{4,12},{8,0},{12,4},{16,24},{20,28},{24,16},{28,20},{1,9},{5... | collective-permute-start | bytes 393224 | tf_op jit(solution)/shard_map/ppermute | solution.py:432
  26.4 5.9 %collective-permute-start.4 = (bf16[512,128]{1,0:T(8,128)(2,1)S(1)}, bf16[512,128]{1,0:T(8,128)(2,1)S(1)}, u32[]{:S(2)}, u32[]{:S(2)}) collective-permute-start(bf16[512,128]{1,0:T(8,128)(2,1)S(1)} %get-tuple-element.142), channel_id=1, source_target_pairs={{0,12},{4,8},{8,4},{12,0},{16,28},{20,24},{24,20},{28,16},{1,13},{... | collective-permute-start | bytes 393224 | tf_op jit(solution)/shard_map/ppermute | solution.py:432
  33.6 1.7 %collective-permute-start.9 = (f32[8,128]{1,0:T(8,128)S(1)}, f32[8,128]{1,0:T(8,128)S(1)}, u32[]{:S(2)}, u32[]{:S(2)}) collective-permute-start(f32[8,128]{1,0:T(8,128)S(1)} %get-tuple-element.152.refs_0_), channel_id=1, source_target_pairs={{0,3},{1,0},{2,1},{3,2},{4,7},{5,4},{6,5},{7,6},{8,11},{9,8},{10,9... | collective-permute-start | bytes 12296 | tf_op jit(solution)/shard_map/ppermute | solution.py:564
  33.6 3.6 %collective-permute-start.8 = (f32[8,128]{1,0:T(8,128)S(1)}, f32[8,128]{1,0:T(8,128)S(1)}, u32[]{:S(2)}, u32[]{:S(2)}) collective-permute-start(f32[8,128]{1,0:T(8,128)S(1)} %get-tuple-element.152.refs_0_), channel_id=1, source_target_pairs={{0,2},{1,3},{2,0},{3,1},{4,6},{5,7},{6,4},{7,5},{8,10},{9,11},{10,... | collective-permute-start | bytes 12296 | tf_op jit(solution)/shard_map/ppermute | solution.py:564
  35.1 3.0 %collective-permute-start.7 = (f32[8,128]{1,0:T(8,128)S(1)}, f32[8,128]{1,0:T(8,128)S(1)}, u32[]{:S(2)}, u32[]{:S(2)}) collective-permute-start(f32[8,128]{1,0:T(8,128)S(1)} %get-tuple-element.152.refs_0_), channel_id=1, source_target_pairs={{0,1},{1,2},{2,3},{3,0},{4,5},{5,6},{6,7},{7,4},{8,9},{9,10},{10,1... | collective-permute-start | bytes 12296 | tf_op jit(solution)/shard_map/ppermute | solution.py:564
  38.9 9.2 %collective-permute-start.10 = (bf16[512,128]{1,0:T(8,128)(2,1)S(1)}, bf16[512,128]{1,0:T(8,128)(2,1)S(1)}, u32[]{:S(2)}, u32[]{:S(2)}) collective-permute-start(bf16[512,128]{1,0:T(8,128)(2,1)S(1)} %get-tuple-element.191), channel_id=1, source_target_pairs={{0,4},{4,0},{8,12},{12,8},{16,20},{20,16},{24,28},{28,24},{1,5},{5... | collective-permute-start | bytes 393224 | tf_op jit(solution)/shard_map/ppermute | solution.py:432
  40.2 7.9 %collective-permute-start.11 = (bf16[512,128]{1,0:T(8,128)(2,1)S(1)}, bf16[512,128]{1,0:T(8,128)(2,1)S(1)}, u32[]{:S(2)}, u32[]{:S(2)}) collective-permute-start(bf16[512,128]{1,0:T(8,128)(2,1)S(1)} %get-tuple-element.192), channel_id=1, source_target_pairs={{0,8},{4,12},{8,0},{12,4},{16,24},{20,28},{24,16},{28,20},{1,9},{5... | collective-permute-start | bytes 393224 | tf_op jit(solution)/shard_map/ppermute | solution.py:432
  41.9 6.2 %collective-permute-start.12 = (bf16[512,128]{1,0:T(8,128)(2,1)S(1)}, bf16[512,128]{1,0:T(8,128)(2,1)S(1)}, u32[]{:S(2)}, u32[]{:S(2)}) collective-permute-start(bf16[512,128]{1,0:T(8,128)(2,1)S(1)} %get-tuple-element.193), channel_id=1, source_target_pairs={{0,12},{4,8},{8,4},{12,0},{16,28},{20,24},{24,20},{28,16},{1,13},{... | collective-permute-start | bytes 393224 | tf_op jit(solution)/shard_map/ppermute | solution.py:432
  48.3 9.2 %collective-permute-start.13 = (bf16[512,128]{1,0:T(8,128)(2,1)S(1)}, bf16[512,128]{1,0:T(8,128)(2,1)S(1)}, u32[]{:S(2)}, u32[]{:S(2)}) collective-permute-start(bf16[512,128]{1,0:T(8,128)(2,1)S(1)} %get-tuple-element.198), channel_id=1, source_target_pairs={{16,0},{20,4},{24,8},{28,12},{17,1},{21,5},{25,9},{29,13},{18,2},{... | collective-permute-start | bytes 393224 | tf_op jit(solution)/shard_map/ppermute | solution.py:490
  57.6 7.9 %collective-permute-start.16 = (bf16[512,128]{1,0:T(8,128)(2,1)S(1)}, bf16[512,128]{1,0:T(8,128)(2,1)S(1)}, u32[]{:S(2)}, u32[]{:S(2)}) collective-permute-start(bf16[512,128]{1,0:T(8,128)(2,1)S(1)} %get-tuple-element.205), channel_id=1, source_target_pairs={{0,4},{4,0},{8,12},{12,8},{16,20},{20,16},{24,28},{28,24},{1,5},{5... | collective-permute-start | bytes 393224 | tf_op jit(solution)/shard_map/ppermute | solution.py:432
  58.4 8.5 %collective-permute-start.15 = (bf16[512,128]{1,0:T(8,128)(2,1)S(1)}, bf16[512,128]{1,0:T(8,128)(2,1)S(1)}, u32[]{:S(2)}, u32[]{:S(2)}) collective-permute-start(bf16[512,128]{1,0:T(8,128)(2,1)S(1)} %get-tuple-element.203), channel_id=1, source_target_pairs={{0,8},{4,12},{8,0},{12,4},{16,24},{20,28},{24,16},{28,20},{1,9},{5... | collective-permute-start | bytes 393224 | tf_op jit(solution)/shard_map/ppermute | solution.py:432
  58.5 9.9 %collective-permute-start.14 = (bf16[512,128]{1,0:T(8,128)(2,1)S(1)}, bf16[512,128]{1,0:T(8,128)(2,1)S(1)}, u32[]{:S(2)}, u32[]{:S(2)}) collective-permute-start(bf16[512,128]{1,0:T(8,128)(2,1)S(1)} %get-tuple-element.201), channel_id=1, source_target_pairs={{0,12},{4,8},{8,4},{12,0},{16,28},{20,24},{24,20},{28,16},{1,13},{... | collective-permute-start | bytes 393224 | tf_op jit(solution)/shard_map/ppermute | solution.py:432

commit v4 on v3

--- a/solution.py
+++ b/solution.py
@@ -26,16 +26,6 @@
     return dot(a, b, ((1,), (1,)))
 
 
-def running_sum(x):
-    width = x.shape[1]
-    lane = lax.broadcasted_iota(jnp.int32, x.shape, 1)
-    step = 1
-    while step < width:
-        x = x + jnp.where(lane >= step, pltpu.roll(x, step, 1), 0.0)
-        step *= 2
-    return x
-
-
 def three_parts(x):
     high = x.astype(BF16).astype(F32)
     rest = x - high
@@ -48,15 +38,36 @@
 
 
 def partner(place, slot, size):
-    return place ^ slot if size & (size - 1) == 0 else (place + slot) % size
+    if size & (size - 1):
+        return (place + slot) % size
+    return place ^ (3 - slot if slot in (1, 2) and size > 2 else slot)
 
 
 def inverse(place, slot, size):
-    return place ^ slot if size & (size - 1) == 0 else (place + size - slot) % size
+    return partner(place, slot, size) if size & (size - 1) == 0 else (place + size - slot) % size
 
 
 def my_place(size):
     return lax.rem(lax.axis_index("seq"), size)
+
+
+def ones_where(keep):
+    return jnp.where(keep, 1.0, 0.0).astype(BF16)
+
+
+def running_sum(x, upper):
+    rows = x.shape[0]
+    parts = jnp.concatenate(three_parts(x), axis=0).astype(BF16)
+    sums = dot(parts, upper)
+    return sums[:rows] + sums[rows : 2 * rows] + sums[2 * rows :]
+
+
+def diagonal(blocks):
+    if len(blocks) == 1:
+        return blocks[0]
+    zero = jnp.zeros_like(blocks[0])
+    rows = [[block if i == j else zero for j in range(len(blocks))] for i, block in enumerate(blocks)]
+    return jnp.concatenate([jnp.concatenate(row, axis=1) for row in rows], axis=0)
 
 
 def block_mask(table):
@@ -81,9 +92,19 @@
     def head(self, i):
         return slice(i * self.dim, (i + 1) * self.dim)
 
+    def tiles(self):
+        for j in range(self.length // HALF):
+            start = HALF * (j * (j + 1) // 2)
+            yield slice(j * HALF, (j + 1) * HALF), slice(0, (j + 1) * HALF), slice(start, start + (j + 1) * HALF)
+
+    def pairs(self):
+        step = 2 if self.hpo % 2 == 0 else 1
+        return [list(range(i, i + step)) for i in range(0, self.hpo, step)]
+
+    def columns(self, pair):
+        return slice(pair[0] * self.dim, (pair[-1] + 1) * self.dim)
+
     def guard(self, slot):
-        if self.hpo * self.size == self.heads:
-            return lambda body: body()
         return pl.when(partner(my_place(self.size), slot, self.size) * self.hpo < self.heads)
 
 
@@ -117,10 +138,13 @@
             for copy in loads(slot):
                 copy.start()
 
+    down = lax.broadcasted_iota(jnp.int32, (length, length), 0)
+    across = lax.broadcasted_iota(jnp.int32, (length, length), 1)
+    upper = ones_where(down <= across)
     for copy in copies:
         copy.wait()
     flags = jnp.broadcast_to(starts_ref[...].astype(F32), (8, length))
-    sums = running_sum(jnp.concatenate([logs_ref[...], flags], axis=0))
+    sums = running_sum(jnp.concatenate([logs_ref[...], flags], axis=0), upper)
     logs, count = sums[:heads] * LOG2E, sums[heads : heads + 1]
     last = slice(length - 1, length)
     enter = jnp.where(count == 0.0, jnp.exp2(logs), 0.0)
@@ -181,12 +205,14 @@
         total_ref[rows, :] = state.astype(BF16)
 
 
-def return_kernel(plan, local_ref, factor_ref, outer_ref, *refs):
+def return_kernel(plan, forward, local_ref, factor_ref, outer_ref, *refs):
     out_refs = refs[-plan.size :]
     me = my_place(plan.size)
+    upper = lax.axis_index("seq") >= plan.size
+    takes = upper if forward else jnp.logical_not(upper)
     for i in range(plan.hpo):
         rows = plan.head(i)
-        outer = outer_ref[rows, :].astype(F32)
+        outer = jnp.where(takes, outer_ref[rows, :].astype(F32), 0.0)
         for slot, out_ref in enumerate(out_refs):
             b = inverse(me, slot, plan.size)
             out_ref[rows, :] = (local_ref[b, rows, :] + factor_ref[b, i : i + 1, :] * outer).astype(BF16)
@@ -231,21 +257,13 @@
             lanes = plan.head(i)
             turned = q_ref[:, lanes].T
             decayed_ref[lanes, :] = (turned.astype(F32) * table[hpo + i : hpo + i + 1]).astype(BF16)
-            outs = [None] * (length // HALF)
-            at = 0
-            for first in range(0, length, HALF):
-                rows = slice(first, first + HALF)
-                gap = table[i : i + 1, first:] - columns[rows, i : i + 1]
-                weight = jnp.exp2(gap + mask_ref[rows, first:])
-                probs = (dot(k_ref[rows, lanes], turned[:, first:]) * weight).astype(BF16)
-                weight_ref[i, :, at : at + length - first] = weight.astype(BF16)
-                probs_ref[i, :, at : at + length - first] = probs
-                for j in range(first, length, HALF):
-                    part = dot(probs[:, j - first : j - first + HALF], v_ref[rows, lanes], ((0,), (0,)))
-                    outs[j // HALF] = part if outs[j // HALF] is None else outs[j // HALF] + part
-                at += length - first
-            for j, out in enumerate(outs):
-                out_ref[j * HALF : (j + 1) * HALF, lanes] = out
+            for later, seen, kept in plan.tiles():
+                gap = table[i : i + 1, later] - columns[seen, i : i + 1]
+                weight = jnp.exp2(gap + mask_ref[seen, later])
+                probs = (dot(k_ref[seen, lanes], turned[:, later]) * weight).astype(BF16)
+                weight_ref[i, kept, :] = weight.astype(BF16)
+                probs_ref[i, kept, :] = probs
+                out_ref[later, lanes] = dot(probs, v_ref[seen, lanes], ((0,), (0,)))
 
     if copies is not None:
         for other, pair in zip(others, copies):
@@ -257,10 +275,9 @@
 
 
 def token_rows(total):
-    length = total.shape[0]
-    return jnp.concatenate(
-        [jnp.sum(total[i : i + 128].T, axis=0, keepdims=True) for i in range(0, length, 128)], axis=0
-    )
+    ones = jnp.ones((ROWS, total.shape[1]), BF16)
+    row = sum(dot_nt(ones, part.astype(BF16)) for part in three_parts(total))[:1]
+    return jnp.concatenate([row[:, i : i + 128] for i in range(0, total.shape[0], 128)], axis=0)
 
 
 def output_kernel(plan, slot, first_part, last_part, table_ref, q_ref, cot_ref, intra_ref, state_ref, *refs):
@@ -277,13 +294,15 @@
     def _():
         columns = table_ref[slot].T
         square, cross = total_ref[0], total_ref[1]
-        for i in range(hpo):
-            lanes = plan.head(i)
-            carried = dot(q_ref[:, lanes], state_ref[lanes, :])
-            out = intra_ref[:, lanes] + columns[:, hpo + i : hpo + i + 1] * carried
-            out_ref[:, lanes] = out
-            square = square + out * out
-            cross = cross + cot_ref[:, lanes].astype(F32) * out
+        for pair in plan.pairs():
+            states = diagonal([state_ref[plan.head(i), :] for i in pair])
+            both = dot(q_ref[:, plan.columns(pair)], states)
+            for j, i in enumerate(pair):
+                lanes = plan.head(i)
+                out = intra_ref[:, lanes] + columns[:, hpo + i : hpo + i + 1] * both[:, plan.head(j)]
+                out_ref[:, lanes] = out
+                square = square + out * out
+                cross = cross + cot_ref[:, lanes].astype(F32) * out
         total_ref[0] = square
         total_ref[1] = cross
 
@@ -372,22 +391,20 @@
         for i in range(hpo):
             lanes = plan.head(i)
             gout_turned = gout_ref[:, lanes].T
-            totals = table[hpo + i : hpo + i + 1] * dot(state_ref[lanes, :], gout_turned)
-            totals = [totals[:, j : j + HALF] for j in range(0, length, HALF)]
-            at = 0
-            for first in range(0, length, HALF):
-                rows, later = slice(first, first + HALF), slice(first, length)
-                size = length - first
-                gv_ref[rows, lanes] = dot(probs_ref[i, :, at : at + size], gout_ref[later, lanes])
-                grads = dot(v_ref[rows, lanes], gout_turned[:, later])
-                grads = (grads * weight_ref[i, :, at : at + size].astype(F32)).astype(BF16)
-                gk_ref[rows, lanes] = dot(grads, q_ref[later, lanes])
-                piece = dot(turned_ref[lanes, rows], grads)
-                for j in range(first, length, HALF):
-                    totals[j // HALF] = totals[j // HALF] + piece[:, j - first : j - first + HALF]
-                at += size
-            for j, total in enumerate(totals):
-                gq_ref[j * HALF : (j + 1) * HALF, lanes] = total.astype(BF16).T
+            carried = table[hpo + i : hpo + i + 1] * dot(state_ref[lanes, :], gout_turned)
+            for later, seen, kept in reversed(list(plan.tiles())):
+                grads = dot(v_ref[seen, lanes], gout_turned[:, later])
+                grads = (grads * weight_ref[i, kept, :].astype(F32)).astype(BF16)
+                from_probs = dot(probs_ref[i, kept, :], gout_ref[later, lanes])
+                from_grads = dot(grads, q_ref[later, lanes])
+                if seen.stop == length:
+                    gv_ref[:, lanes] = from_probs
+                    gk_ref[:, lanes] = from_grads
+                else:
+                    gv_ref[seen, lanes] += from_probs
+                    gk_ref[seen, lanes] += from_grads
+                total = carried[:, later] + dot(turned_ref[lanes, seen], grads)
+                gq_ref[later, lanes] = total.astype(BF16).T
 
     wait_all(plan, copies)
 
@@ -403,26 +420,33 @@
     copies = stores(plan, [s for _, s in finished], done_refs, [hbm_of[name] for name, _ in finished], sems)
     start_all(plan, copies)
 
+    tails = []
+    if last_part:
+        for n, pair in enumerate(plan.pairs()):
+            for m, (ref, target) in enumerate(((gk_ref, gk_hbm), (gv_ref, gv_hbm))):
+                start = partner(my_place(plan.size), slot, plan.size) * plan.span
+                width = len(pair) * plan.dim
+                lanes = pl.ds(pl.multiple_of(start + n * width, width), width)
+                sem = sems.at[len(finished) + 2 * n + m]
+                tails.append((slot, pltpu.make_async_copy(ref.at[:, plan.columns(pair)], target.at[:, lanes], sem)))
+
     @plan.guard(slot)
     def _():
         columns = table_ref[slot].T
-        for i in range(plan.hpo):
-            lanes = plan.head(i)
-            leave = columns[:, 2 * plan.hpo + i : 2 * plan.hpo + i + 1]
-            back = back_ref[lanes, :]
-            gk_ref[:, lanes] = (gkp_ref[:, lanes] + leave * dot_nt(v_ref[:, lanes], back)).astype(BF16)
-            gv_ref[:, lanes] = (gvp_ref[:, lanes] + leave * dot(k_ref[:, lanes], back)).astype(BF16)
-
-    if last_part:
-        own = len(finished)
-        lanes = plan.lanes(slot)
-        tail = [
-            (slot, pltpu.make_async_copy(gk_ref, gk_hbm.at[:, lanes], sems.at[own])),
-            (slot, pltpu.make_async_copy(gv_ref, gv_hbm.at[:, lanes], sems.at[own + 1])),
-        ]
-        start_all(plan, tail)
-        copies = copies + tail
-    wait_all(plan, copies)
+        for n, pair in enumerate(plan.pairs()):
+            back = diagonal([back_ref[plan.head(i), :] for i in pair])
+            both = plan.columns(pair)
+            from_values = dot_nt(v_ref[:, both], back)
+            from_keys = dot(k_ref[:, both], back)
+            for j, i in enumerate(pair):
+                lanes, part = plan.head(i), plan.head(j)
+                leave = columns[:, 2 * plan.hpo + i : 2 * plan.hpo + i + 1]
+                gk_ref[:, lanes] = (gkp_ref[:, lanes] + leave * from_values[:, part]).astype(BF16)
+                gv_ref[:, lanes] = (gvp_ref[:, lanes] + leave * from_keys[:, part]).astype(BF16)
+            for _, copy in tails[2 * n : 2 * n + 2]:
+                copy.start()
+
+    wait_all(plan, copies + tails)
 
 
 def exchange(arrays, size, halves, target):
@@ -486,12 +510,12 @@
             [pltpu.VMEM((size, *arrays[0].shape), BF16)],
         )
         if halves == 2:
-            pairs = [(i, i + size) if forward else (i + size, i) for i in range(size)]
+            pairs = [(i, (i + size) % (2 * size)) for i in range(2 * size)]
             outer = lax.ppermute(total, "seq", pairs)
         else:
             outer = jnp.zeros_like(total)
         back = call(
-            functools.partial(return_kernel, plan),
+            functools.partial(return_kernel, plan, forward),
             "return",
             [local, factor, outer],
             [pltpu.VMEM((span, dim), BF16)] * size,
@@ -523,8 +547,7 @@
     table = results[-1]
     received = exchange(sent, size, halves, partner)
 
-    lower = length * (length + HALF) // 2 // HALF
-    kept = pltpu.VMEM((hpo, HALF, lower), BF16)
+    kept = pltpu.VMEM((hpo, length * (length + HALF) // 2 // HALF, HALF), BF16)
     intra, decayed, probs, weights = [], [], [], []
     for slot in range(size):
         first = slot == 0
@@ -561,7 +584,7 @@
     states = received
 
     everyone = [sums] + [
-        lax.ppermute(sums, "head", [(i, (i + k) % shares) for i in range(shares)]) for k in range(1, shares)
+        lax.ppermute(sums, "head", [(i, partner(i, k, shares)) for i in range(shares)]) for k in range(1, shares)
     ]
 
     gout, sent = [None] * size, [None] * size
@@ -632,7 +655,7 @@
             operands + chained,
             [whole] * 3 + [held(BF16)] * 2,
             cost(2 * small),
-            scratch=[dma((len(finished) + 2,))],
+            scratch=[dma((len(finished) + 2 * len(plan.pairs()),))],
             aliases=aliases,
         )
     return (attn_whole, gq_whole, gk_whole, gv_whole)

time: 71.3 us -> 67.3 us (0.944)
  Pallas kernels: 37.7 us -> 32.2 us
  waiting for transfers between devices: 9.32 us -> 10.6 us
    pallas_call x26, Pallas kernels: 37.7 us -> 32.2 us  [call(): pl.pallas_call(kernel, in_specs=[hbm if f else inside for f in far] + [un...]
    ppermute x12, waiting for transfers between devices: 4.86 us -> 6.22 us  [exchange(): lax.ppermute(arrays[slot], 'seq', pairs(slot))]
  transfers between devices with their start and end apart: 17 -> 17, of which waited for: 6 -> 8; matrix products, arithmetic and copies ran while one was open for 0% -> 0% of each run, Pallas kernels for 41% -> 36%
where the time goes in v4:
time: 67.3 us; the launch traced here: 67.1 us
  Pallas kernels  32.2 us (48%)
  starting transfers between devices  23.3 us (35%)
  waiting for transfers between devices  10.6 us (16%)
  between operations  1.02 us (2%)
    pallas_call x26, Pallas kernels, call(): pl.pallas_call(kernel, in_specs=[hbm if f else inside for f in far] + [un...  32.2 us
    ppermute x12, starting transfers between devices, exchange(): lax.ppermute(arrays[slot], 'seq', pairs(slot))  15.4 us
    ppermute x12, waiting for transfers between devices, exchange(): lax.ppermute(arrays[slot], 'seq', pairs(slot))  6.22 us
    ppermute x2, starting transfers between devices, scan(): outer = lax.ppermute(total, 'seq', pairs)  5.77 us
    ppermute x3, waiting for transfers between devices, per_device(): lax.ppermute(sums, 'head', [(i, partner(i, k, shares)) for i in range(sha...  2.86 us
    ppermute x3, starting transfers between devices, per_device(): lax.ppermute(sums, 'head', [(i, partner(i, k, shares)) for i in range(sha...  2.14 us
    ppermute x2, waiting for transfers between devices, scan(): outer = lax.ppermute(total, 'seq', pairs)  1.53 us
  transfers between devices with their start and end apart: 17, of which 8 were waited for; matrix products, arithmetic and copies ran while one was open for 0% of the time, Pallas kernels for 36%

profile of v4, /device:TPU:0, one launch (start us, length us, event | category | flops | bytes accessed | tf_op | source)
XLA Modules:
  0.0 67.1 jit_solution(6380486674190956340)
XLA Ops:
  0.6 2.8 %update.1 = (bf16[528,128]{1,0:T(8,128)(2,1)S(1)}, bf16[528,128]{1,0:T(8,128)(2,1)S(1)}, bf16[528,128]{1,0:T(8,128)(2,1)S(1)}, bf16[528,128]{1,0:T(8,128)(2,1)S(...) custom-call(f32[16,512]{1,0:T(8,128)} %logs_hbm.1, ...), custom_call_target="tpu_custom_call" | custom-call | flops 268435456 | bytes 262144 | tf_op jit(solution)/shard_map/update/pallas_call | solution.py:488
  3.5 3.1 %collective-permute-start = (bf16[528,128]{1,0:T(8,128)(2,1)S(1)}, bf16[528,128]{1,0:T(8,128)(2,1)S(1)}, u32[]{:S(2)}, u32[]{:S(2)}) collective-permute-start(bf16[528,128]{1,0:T(8,128)(2,1)S(1)} %get-tuple-element.127), channel_id=1, source_target_pairs={{0,8},{4,12},{8,0},{12,4},{16,24},{20,28},{24,16},{28,20},{1,9},{5... | collective-permute-start | bytes 405512 | tf_op jit(solution)/shard_map/ppermute | solution.py:456
  6.6 1.5 %collective-permute-start.1 = (bf16[528,128]{1,0:T(8,128)(2,1)S(1)}, bf16[528,128]{1,0:T(8,128)(2,1)S(1)}, u32[]{:S(2)}, u32[]{:S(2)}) collective-permute-start(bf16[528,128]{1,0:T(8,128)(2,1)S(1)} %get-tuple-element.128), channel_id=1, source_target_pairs={{0,4},{4,0},{8,12},{12,8},{16,20},{20,16},{24,28},{28,24},{1,5},{5... | collective-permute-start | bytes 405512 | tf_op jit(solution)/shard_map/ppermute | solution.py:456
  8.1 2.9 %intra.4 = (bf16[512,512]{1,0:T(8,128)(2,1)S(1)}, bf16[512,512]{1,0:T(8,128)(2,1)S(1)}, bf16[512,512]{1,0:T(8,128)(2,1)S(1)}, bf16[512,512]{1,0:T(8,128)(2,1)S(1...) custom-call(f32[4,16,512]{2,1,0:T(8,128)S(1)} %get-tuple-element.116, ...), custom_call_target="tpu_custom_call" | custom-call | flops 536870912 | bytes 262144 | tf_op jit(solution)/shard_map/intra/pallas_call | solution.py:488
  11.0 1.7 %intra.6 = (f32[512,512]{1,0:T(8,128)S(1)}, bf16[512,512]{1,0:T(8,128)(2,1)S(1)}, bf16[4,768,256]{2,1,0:T(8,128)(2,1)S(1)}, bf16[4,768,256]{2,1,0:T(8,128)(2,1)S(1)}) custom-call(f32[4,16,512]{2,1,0:T(8,128)S(1)} %get-tuple-element.116.table_ref.refs_0_, bf16[512,512]{1,0:T(8,128)(2,1)S(1)} %get-tuple-element.131.k_ref.refs_1_, ...), custom_call_target="tpu_custom_call" | custom-call | flops 536870912 | bytes 262144 | tf_op jit(solution)/shard_map/intra/pallas_call | solution.py:488
  12.7 1.8 %collective-permute-done.1.refs_2_ = bf16[528,128]{1,0:T(8,128)(2,1)S(1)} collective-permute-done((bf16[528,128]{1,0:T(8,128)(2,1)S(1)}, bf16[528,128]{1,0:T(8,128)(2,1)S(1)}, u32[]{:S(2)}, u32[]{:S(2)}) %collective-permute-start.1) | collective-permute-done | bytes 135200 | tf_op jit(solution)/shard_map/ppermute | solution.py:456
  14.7 2.7 %collective-permute-start.3 = (bf16[512,128]{1,0:T(8,128)(2,1)S(1)}, bf16[512,128]{1,0:T(8,128)(2,1)S(1)}, u32[]{:S(2)}, u32[]{:S(2)}) collective-permute-start(bf16[512,128]{1,0:T(8,128)(2,1)S(1)} %get-tuple-element.137), channel_id=1, source_target_pairs={{0,16},{4,20},{8,24},{12,28},{16,0},{20,4},{24,8},{28,12},{1,17},{... | collective-permute-start | bytes 393224 | tf_op jit(solution)/shard_map/ppermute | solution.py:514
  17.3 1.7 %intra.5 = (f32[512,512]{1,0:T(8,128)S(1)}, bf16[512,512]{1,0:T(8,128)(2,1)S(1)}, bf16[4,768,256]{2,1,0:T(8,128)(2,1)S(1)}, bf16[4,768,256]{2,1,0:T(8,128)(2,1)S(1)}) custom-call(f32[4,16,512]{2,1,0:T(8,128)S(1)} %get-tuple-element.116.table_ref.refs_0_, bf16[512,512]{1,0:T(8,128)(2,1)S(1)} %get-tuple-element.122.k_ref.refs_1_, ...), custom_call_target="tpu_custom_call" | custom-call | flops 536870912 | bytes 262144 | tf_op jit(solution)/shard_map/intra/pallas_call | solution.py:488
  19.0 1.7 %intra.7 = (f32[512,512]{1,0:T(8,128)S(1)}, bf16[512,512]{1,0:T(8,128)(2,1)S(1)}, bf16[4,768,256]{2,1,0:T(8,128)(2,1)S(1)}, bf16[4,768,256]{2,1,0:T(8,128)(2,1)S(1)}) custom-call(f32[4,16,512]{2,1,0:T(8,128)S(1)} %get-tuple-element.116.table_ref.refs_0_, bf16[512,512]{1,0:T(8,128)(2,1)S(1)} %get-tuple-element.138.k_ref.refs_1_, ...), custom_call_target="tpu_custom_call" | custom-call | flops 536870912 | bytes 262144 | tf_op jit(solution)/shard_map/intra/pallas_call | solution.py:488
  20.8 1.5 %collective-permute-done.3.outer_ref = bf16[512,128]{1,0:T(8,128)(2,1)S(1)} collective-permute-done((bf16[512,128]{1,0:T(8,128)(2,1)S(1)}, bf16[512,128]{1,0:T(8,128)(2,1)S(1)}, u32[]{:S(2)}, u32[]{:S(2)}) %collective-permute-start.3) | collective-permute-done | bytes 131104 | tf_op jit(solution)/shard_map/ppermute | solution.py:514
  23.1 1.1 %collective-permute-start.5 = (bf16[512,128]{1,0:T(8,128)(2,1)S(1)}, bf16[512,128]{1,0:T(8,128)(2,1)S(1)}, u32[]{:S(2)}, u32[]{:S(2)}) collective-permute-start(bf16[512,128]{1,0:T(8,128)(2,1)S(1)} %get-tuple-element.144), channel_id=1, source_target_pairs={{0,4},{4,0},{8,12},{12,8},{16,20},{20,16},{24,28},{28,24},{1,5},{5... | collective-permute-start | bytes 393224 | tf_op jit(solution)/shard_map/ppermute | solution.py:456
  24.2 1.7 %collective-permute-start.4 = (bf16[512,128]{1,0:T(8,128)(2,1)S(1)}, bf16[512,128]{1,0:T(8,128)(2,1)S(1)}, u32[]{:S(2)}, u32[]{:S(2)}) collective-permute-start(bf16[512,128]{1,0:T(8,128)(2,1)S(1)} %get-tuple-element.142), channel_id=1, source_target_pairs={{0,12},{4,8},{8,4},{12,0},{16,28},{20,24},{24,20},{28,16},{1,13},{... | collective-permute-start | bytes 393224 | tf_op jit(solution)/shard_map/ppermute | solution.py:456
  26.5 2.0 %collective-permute-done.6.state_ref.refs_8_ = bf16[512,128]{1,0:T(8,128)(2,1)S(1)} collective-permute-done((bf16[512,128]{1,0:T(8,128)(2,1)S(1)}, bf16[512,128]{1,0:T(8,128)(2,1)S(1)}, u32[]{:S(2)}, u32[]{:S(2)}) %collective-permute-start.6) | collective-permute-done | bytes 131104 | tf_op jit(solution)/shard_map/ppermute | solution.py:456
  31.0 1.4 %output.7 = (f32[512,512]{1,0:T(8,128)S(1)}, f32[2,512,128]{2,1,0:T(8,128)}, f32[8,128]{1,0:T(8,128)S(1)}) custom-call(f32[4,16,512]{2,1,0:T(8,128)S(1)} %get-tuple-element.116.table_ref.refs_0_, bf16[512,512]{1,0:T(8,128)(2,1)S(1)} %get-tuple-element.120.refs_0_.q_ref.refs_3_, bf16[512,512]{1,0:T(8,128)(2,1)S(1)} %get-tuple-element.121.cot_ref.refs_2_, ...), custom_call_target="tpu_custom_call" | custom-call | flops 67108864 | bytes 262144 | tf_op jit(solution)/shard_map/output/pallas_call | solution.py:488
  32.4 1.4 %collective-permute-start.8 = (f32[8,128]{1,0:T(8,128)S(1)}, f32[8,128]{1,0:T(8,128)S(1)}, u32[]{:S(2)}, u32[]{:S(2)}) collective-permute-start(f32[8,128]{1,0:T(8,128)S(1)} %get-tuple-element.152.refs_0_), channel_id=1, source_target_pairs={{0,1},{1,0},{2,3},{3,2},{4,5},{5,4},{6,7},{7,6},{8,9},{9,8},{10,11... | collective-permute-start | bytes 12296 | tf_op jit(solution)/shard_map/ppermute | solution.py:587
  34.5 0.9 %collective-permute-done.9.refs_3_ = f32[8,128]{1,0:T(8,128)S(1)} collective-permute-done((f32[8,128]{1,0:T(8,128)S(1)}, f32[8,128]{1,0:T(8,128)S(1)}, u32[]{:S(2)}, u32[]{:S(2)}) %collective-permute-start.9) | collective-permute-done | bytes 4128 | tf_op jit(solution)/shard_map/ppermute | solution.py:587
  35.4 2.0 %collective-permute-done.7.refs_1_ = f32[8,128]{1,0:T(8,128)S(1)} collective-permute-done((f32[8,128]{1,0:T(8,128)S(1)}, f32[8,128]{1,0:T(8,128)S(1)}, u32[]{:S(2)}, u32[]{:S(2)}) %collective-permute-start.7) | collective-permute-done | bytes 4128 | tf_op jit(solution)/shard_map/ppermute | solution.py:587
  37.4 0.9 %gout.4 = (f32[2,512,128]{2,1,0:T(8,128)S(1)}, bf16[512,512]{1,0:T(8,128)(2,1)S(1)}, bf16[512,128]{1,0:T(8,128)(2,1)S(1)}) custom-call(f32[8,128]{1,0:T(8,128)S(1)} %get-tuple-element.152.refs_0_, f32[8,128]{1,0:T(8,128)S(1)} %collective-permute-done.7.refs_1_, f32[8,128]{1,0:T(8,128)S(1)} %collective-permute-done.8.refs_2_, ...), custom_call_target="tpu_custom_call" | custom-call | flops 67108864 | bytes 262144 | tf_op jit(solution)/shard_map/gout/pallas_call | solution.py:488
  38.3 0.9 %collective-permute-start.10 = (bf16[512,128]{1,0:T(8,128)(2,1)S(1)}, bf16[512,128]{1,0:T(8,128)(2,1)S(1)}, u32[]{:S(2)}, u32[]{:S(2)}) collective-permute-start(bf16[512,128]{1,0:T(8,128)(2,1)S(1)} %get-tuple-element.191), channel_id=1, source_target_pairs={{0,8},{4,12},{8,0},{12,4},{16,24},{20,28},{24,16},{28,20},{1,9},{5... | collective-permute-start | bytes 393224 | tf_op jit(solution)/shard_map/ppermute | solution.py:456
  39.6 1.0 %collective-permute-start.11 = (bf16[512,128]{1,0:T(8,128)(2,1)S(1)}, bf16[512,128]{1,0:T(8,128)(2,1)S(1)}, u32[]{:S(2)}, u32[]{:S(2)}) collective-permute-start(bf16[512,128]{1,0:T(8,128)(2,1)S(1)} %get-tuple-element.192), channel_id=1, source_target_pairs={{0,4},{4,0},{8,12},{12,8},{16,20},{20,16},{24,28},{28,24},{1,5},{5... | collective-permute-start | bytes 393224 | tf_op jit(solution)/shard_map/ppermute | solution.py:456
  41.0 1.9 %collective-permute-start.12 = (bf16[512,128]{1,0:T(8,128)(2,1)S(1)}, bf16[512,128]{1,0:T(8,128)(2,1)S(1)}, u32[]{:S(2)}, u32[]{:S(2)}) collective-permute-start(bf16[512,128]{1,0:T(8,128)(2,1)S(1)} %get-tuple-element.193), channel_id=1, source_target_pairs={{0,12},{4,8},{8,4},{12,0},{16,28},{20,24},{24,20},{28,16},{1,13},{... | collective-permute-start | bytes 393224 | tf_op jit(solution)/shard_map/ppermute | solution.py:456
  43.9 2.4 %gradient.4 = (bf16[512,2048]{1,0:T(8,128)(2,1)}, bf16[512,512]{1,0:T(8,128)(2,1)S(1)}, f32[512,512]{1,0:T(8,128)S(1)}, f32[512,512]{1,0:T(8,128)S(1)}) custom-call(f32[4,16,512]{2,1,0:T(8,128)S(1)} %get-tuple-element.116.table_ref.refs_0_, bf16[512,512]{1,0:T(8,128)(2,1)S(1)} %get-tuple-element.117.k_ref.refs_1_, ...), custom_call_target="tpu_custom_call" | custom-call | flops 1073741824 | bytes 262144 | tf_op jit(solution)/shard_map/gradient/pallas_call | solution.py:488
  46.3 1.2 %collective-permute-done.11.refs_2_ = bf16[512,128]{1,0:T(8,128)(2,1)S(1)} collective-permute-done((bf16[512,128]{1,0:T(8,128)(2,1)S(1)}, bf16[512,128]{1,0:T(8,128)(2,1)S(1)}, u32[]{:S(2)}, u32[]{:S(2)}) %collective-permute-start.11) | collective-permute-done | bytes 131104 | tf_op jit(solution)/shard_map/ppermute | solution.py:456
  47.6 3.1 %collective-permute-start.13 = (bf16[512,128]{1,0:T(8,128)(2,1)S(1)}, bf16[512,128]{1,0:T(8,128)(2,1)S(1)}, u32[]{:S(2)}, u32[]{:S(2)}) collective-permute-start(bf16[512,128]{1,0:T(8,128)(2,1)S(1)} %get-tuple-element.198), channel_id=1, source_target_pairs={{0,16},{4,20},{8,24},{12,28},{16,0},{20,4},{24,8},{28,12},{1,17},{... | collective-permute-start | bytes 393224 | tf_op jit(solution)/shard_map/ppermute | solution.py:514
  50.8 2.3 %gradient.5 = (bf16[512,2048]{1,0:T(8,128)(2,1)}, bf16[512,512]{1,0:T(8,128)(2,1)S(1)}, f32[512,512]{1,0:T(8,128)S(1)}, f32[512,512]{1,0:T(8,128)S(1)}) custom-call(f32[4,16,512]{2,1,0:T(8,128)S(1)} %get-tuple-element.116.table_ref.refs_0_, bf16[512,512]{1,0:T(8,128)(2,1)S(1)} %get-tuple-element.131.k_ref.refs_1_, ...), custom_call_target="tpu_custom_call" | custom-call | flops 1073741824 | bytes 262144 | tf_op jit(solution)/shard_map/gradient/pallas_call | solution.py:488
  53.1 2.4 %gradient.6 = (bf16[512,2048]{1,0:T(8,128)(2,1)}, bf16[512,512]{1,0:T(8,128)(2,1)S(1)}, f32[512,512]{1,0:T(8,128)S(1)}, f32[512,512]{1,0:T(8,128)S(1)}) custom-call(f32[4,16,512]{2,1,0:T(8,128)S(1)} %get-tuple-element.116.table_ref.refs_0_, bf16[512,512]{1,0:T(8,128)(2,1)S(1)} %get-tuple-element.138.k_ref.refs_1_, ...), custom_call_target="tpu_custom_call", output_to_operand_aliasing={{0}: (10, {})} | custom-call | flops 1073741824 | bytes 262144 | tf_op jit(solution)/shard_map/gradient/pallas_call | solution.py:488
  55.6 1.8 %collective-permute-start.16 = (bf16[512,128]{1,0:T(8,128)(2,1)S(1)}, bf16[512,128]{1,0:T(8,128)(2,1)S(1)}, u32[]{:S(2)}, u32[]{:S(2)}) collective-permute-start(bf16[512,128]{1,0:T(8,128)(2,1)S(1)} %get-tuple-element.205), channel_id=1, source_target_pairs={{0,8},{4,12},{8,0},{12,4},{16,24},{20,28},{24,16},{28,20},{1,9},{5... | collective-permute-start | bytes 393224 | tf_op jit(solution)/shard_map/ppermute | solution.py:456
  58.2 1.0 %collective-permute-start.14 = (bf16[512,128]{1,0:T(8,128)(2,1)S(1)}, bf16[512,128]{1,0:T(8,128)(2,1)S(1)}, u32[]{:S(2)}, u32[]{:S(2)}) collective-permute-start(bf16[512,128]{1,0:T(8,128)(2,1)S(1)} %get-tuple-element.201), channel_id=1, source_target_pairs={{0,12},{4,8},{8,4},{12,0},{16,28},{20,24},{24,20},{28,16},{1,13},{... | collective-permute-start | bytes 393224 | tf_op jit(solution)/shard_map/ppermute | solution.py:456
  59.2 2.3 %gradient.7 = (bf16[512,2048]{1,0:T(8,128)(2,1)}, bf16[512,512]{1,0:T(8,128)(2,1)S(1)}, f32[512,512]{1,0:T(8,128)S(1)}, f32[512,512]{1,0:T(8,128)S(1)}) custom-call(f32[4,16,512]{2,1,0:T(8,128)S(1)} %get-tuple-element.116.table_ref.refs_0_, bf16[512,512]{1,0:T(8,128)(2,1)S(1)} %get-tuple-element.122.k_ref.refs_1_, ...), custom_call_target="tpu_custom_call", output_to_operand_aliasing={{0}: (10, {})} | custom-call | flops 1073741824 | bytes 262144 | tf_op jit(solution)/shard_map/gradient/pallas_call | solution.py:488
  62.4 1.0 %final.5 = (bf16[512,2048]{1,0:T(8,128)(2,1)}, bf16[512,2048]{1,0:T(8,128)(2,1)}, bf16[512,2048]{1,0:T(8,128)(2,1)}, bf16[512,512]{1,0:T(8,128)(2,1)S(1)}, bf16[512,512]{1,0:T(8,128)(2,1)S(1)}) custom-call(f32[4,16,512]{2,1,0:T(8,128)S(1)} %get-tuple-element.116.table_ref.refs_0_, ...), custom_call_target="tpu_custom_call", output_to_operand_aliasing={{0}: (8, {}), {1}: (9, {}), {2}: (10, {})} | custom-call | flops 134217728 | bytes 262144 | tf_op jit(solution)/shard_map/final/pallas_call | solution.py:488
  63.5 1.0 %final.6 = (bf16[512,2048]{1,0:T(8,128)(2,1)}, bf16[512,2048]{1,0:T(8,128)(2,1)}, bf16[512,2048]{1,0:T(8,128)(2,1)}, bf16[512,512]{1,0:T(8,128)(2,1)S(1)}, bf16[512,512]{1,0:T(8,128)(2,1)S(1)}) custom-call(f32[4,16,512]{2,1,0:T(8,128)S(1)} %get-tuple-element.116.table_ref.refs_0_, ...), custom_call_target="tpu_custom_call", output_to_operand_aliasing={{0}: (8, {}), {1}: (9, {}), {2}: (10, {})} | custom-call | flops 134217728 | bytes 262144 | tf_op jit(solution)/shard_map/final/pallas_call | solution.py:488
  64.5 2.4 %final.7 = (bf16[512,2048]{1,0:T(8,128)(2,1)}, bf16[512,2048]{1,0:T(8,128)(2,1)}, bf16[512,2048]{1,0:T(8,128)(2,1)}, bf16[512,512]{1,0:T(8,128)(2,1)}, bf16[512,512]{1,0:T(8,128)(2,1)}) custom-call(f32[4,16,512]{2,1,0:T(8,128)S(1)} %get-tuple-element.116.table_ref.refs_0_, ...), custom_call_target="tpu_custom_call", output_to_operand_aliasing={{0}: (8, {}), {1}: (9, {}), {2}: (10, {})} | custom-call | flops 134217728 | bytes 262144 | tf_op jit(solution)/shard_map/final/pallas_call | solution.py:488
  (28 shorter events, 8.7 us)
Async XLA Ops:
  3.5 9.2 %collective-permute-start = (bf16[528,128]{1,0:T(8,128)(2,1)S(1)}, bf16[528,128]{1,0:T(8,128)(2,1)S(1)}, u32[]{:S(2)}, u32[]{:S(2)}) collective-permute-start(bf16[528,128]{1,0:T(8,128)(2,1)S(1)} %get-tuple-element.127), channel_id=1, source_target_pairs={{0,8},{4,12},{8,0},{12,4},{16,24},{20,28},{24,16},{28,20},{1,9},{5... | collective-permute-start | bytes 405512 | tf_op jit(solution)/shard_map/ppermute | solution.py:456
  6.6 7.9 %collective-permute-start.1 = (bf16[528,128]{1,0:T(8,128)(2,1)S(1)}, bf16[528,128]{1,0:T(8,128)(2,1)S(1)}, u32[]{:S(2)}, u32[]{:S(2)}) collective-permute-start(bf16[528,128]{1,0:T(8,128)(2,1)S(1)} %get-tuple-element.128), channel_id=1, source_target_pairs={{0,4},{4,0},{8,12},{12,8},{16,20},{20,16},{24,28},{28,24},{1,5},{5... | collective-permute-start | bytes 405512 | tf_op jit(solution)/shard_map/ppermute | solution.py:456
  8.0 6.5 %collective-permute-start.2 = (bf16[528,128]{1,0:T(8,128)(2,1)S(1)}, bf16[528,128]{1,0:T(8,128)(2,1)S(1)}, u32[]{:S(2)}, u32[]{:S(2)}) collective-permute-start(bf16[528,128]{1,0:T(8,128)(2,1)S(1)} %get-tuple-element.129), channel_id=1, source_target_pairs={{0,12},{4,8},{8,4},{12,0},{16,28},{20,24},{24,20},{28,16},{1,13},{... | collective-permute-start | bytes 405512 | tf_op jit(solution)/shard_map/ppermute | solution.py:456
  14.7 7.6 %collective-permute-start.3 = (bf16[512,128]{1,0:T(8,128)(2,1)S(1)}, bf16[512,128]{1,0:T(8,128)(2,1)S(1)}, u32[]{:S(2)}, u32[]{:S(2)}) collective-permute-start(bf16[512,128]{1,0:T(8,128)(2,1)S(1)} %get-tuple-element.137), channel_id=1, source_target_pairs={{0,16},{4,20},{8,24},{12,28},{16,0},{20,4},{24,8},{28,12},{1,17},{... | collective-permute-start | bytes 393224 | tf_op jit(solution)/shard_map/ppermute | solution.py:514
  22.4 6.1 %collective-permute-start.6 = (bf16[512,128]{1,0:T(8,128)(2,1)S(1)}, bf16[512,128]{1,0:T(8,128)(2,1)S(1)}, u32[]{:S(2)}, u32[]{:S(2)}) collective-permute-start(bf16[512,128]{1,0:T(8,128)(2,1)S(1)} %get-tuple-element.146), channel_id=1, source_target_pairs={{0,8},{4,12},{8,0},{12,4},{16,24},{20,28},{24,16},{28,20},{1,9},{5... | collective-permute-start | bytes 393224 | tf_op jit(solution)/shard_map/ppermute | solution.py:456
  23.1 6.4 %collective-permute-start.5 = (bf16[512,128]{1,0:T(8,128)(2,1)S(1)}, bf16[512,128]{1,0:T(8,128)(2,1)S(1)}, u32[]{:S(2)}, u32[]{:S(2)}) collective-permute-start(bf16[512,128]{1,0:T(8,128)(2,1)S(1)} %get-tuple-element.144), channel_id=1, source_target_pairs={{0,4},{4,0},{8,12},{12,8},{16,20},{20,16},{24,28},{28,24},{1,5},{5... | collective-permute-start | bytes 393224 | tf_op jit(solution)/shard_map/ppermute | solution.py:456
  24.2 6.7 %collective-permute-start.4 = (bf16[512,128]{1,0:T(8,128)(2,1)S(1)}, bf16[512,128]{1,0:T(8,128)(2,1)S(1)}, u32[]{:S(2)}, u32[]{:S(2)}) collective-permute-start(bf16[512,128]{1,0:T(8,128)(2,1)S(1)} %get-tuple-element.142), channel_id=1, source_target_pairs={{0,12},{4,8},{8,4},{12,0},{16,28},{20,24},{24,20},{28,16},{1,13},{... | collective-permute-start | bytes 393224 | tf_op jit(solution)/shard_map/ppermute | solution.py:456
  32.4 3.0 %collective-permute-start.9 = (f32[8,128]{1,0:T(8,128)S(1)}, f32[8,128]{1,0:T(8,128)S(1)}, u32[]{:S(2)}, u32[]{:S(2)}) collective-permute-start(f32[8,128]{1,0:T(8,128)S(1)} %get-tuple-element.152.refs_0_), channel_id=1, source_target_pairs={{0,3},{1,2},{2,1},{3,0},{4,7},{5,6},{6,5},{7,4},{8,11},{9,10},{10,... | collective-permute-start | bytes 12296 | tf_op jit(solution)/shard_map/ppermute | solution.py:587
  32.4 3.0 %collective-permute-start.8 = (f32[8,128]{1,0:T(8,128)S(1)}, f32[8,128]{1,0:T(8,128)S(1)}, u32[]{:S(2)}, u32[]{:S(2)}) collective-permute-start(f32[8,128]{1,0:T(8,128)S(1)} %get-tuple-element.152.refs_0_), channel_id=1, source_target_pairs={{0,1},{1,0},{2,3},{3,2},{4,5},{5,4},{6,7},{7,6},{8,9},{9,8},{10,11... | collective-permute-start | bytes 12296 | tf_op jit(solution)/shard_map/ppermute | solution.py:587
  33.8 3.6 %collective-permute-start.7 = (f32[8,128]{1,0:T(8,128)S(1)}, f32[8,128]{1,0:T(8,128)S(1)}, u32[]{:S(2)}, u32[]{:S(2)}) collective-permute-start(f32[8,128]{1,0:T(8,128)S(1)} %get-tuple-element.152.refs_0_), channel_id=1, source_target_pairs={{0,2},{1,3},{2,0},{3,1},{4,6},{5,7},{6,4},{7,5},{8,10},{9,11},{10,... | collective-permute-start | bytes 12296 | tf_op jit(solution)/shard_map/ppermute | solution.py:587
  38.3 8.0 %collective-permute-start.10 = (bf16[512,128]{1,0:T(8,128)(2,1)S(1)}, bf16[512,128]{1,0:T(8,128)(2,1)S(1)}, u32[]{:S(2)}, u32[]{:S(2)}) collective-permute-start(bf16[512,128]{1,0:T(8,128)(2,1)S(1)} %get-tuple-element.191), channel_id=1, source_target_pairs={{0,8},{4,12},{8,0},{12,4},{16,24},{20,28},{24,16},{28,20},{1,9},{5... | collective-permute-start | bytes 393224 | tf_op jit(solution)/shard_map/ppermute | solution.py:456
  39.6 7.8 %collective-permute-start.11 = (bf16[512,128]{1,0:T(8,128)(2,1)S(1)}, bf16[512,128]{1,0:T(8,128)(2,1)S(1)}, u32[]{:S(2)}, u32[]{:S(2)}) collective-permute-start(bf16[512,128]{1,0:T(8,128)(2,1)S(1)} %get-tuple-element.192), channel_id=1, source_target_pairs={{0,4},{4,0},{8,12},{12,8},{16,20},{20,16},{24,28},{28,24},{1,5},{5... | collective-permute-start | bytes 393224 | tf_op jit(solution)/shard_map/ppermute | solution.py:456
  41.0 6.5 %collective-permute-start.12 = (bf16[512,128]{1,0:T(8,128)(2,1)S(1)}, bf16[512,128]{1,0:T(8,128)(2,1)S(1)}, u32[]{:S(2)}, u32[]{:S(2)}) collective-permute-start(bf16[512,128]{1,0:T(8,128)(2,1)S(1)} %get-tuple-element.193), channel_id=1, source_target_pairs={{0,12},{4,8},{8,4},{12,0},{16,28},{20,24},{24,20},{28,16},{1,13},{... | collective-permute-start | bytes 393224 | tf_op jit(solution)/shard_map/ppermute | solution.py:456
  47.6 7.8 %collective-permute-start.13 = (bf16[512,128]{1,0:T(8,128)(2,1)S(1)}, bf16[512,128]{1,0:T(8,128)(2,1)S(1)}, u32[]{:S(2)}, u32[]{:S(2)}) collective-permute-start(bf16[512,128]{1,0:T(8,128)(2,1)S(1)} %get-tuple-element.198), channel_id=1, source_target_pairs={{0,16},{4,20},{8,24},{12,28},{16,0},{20,4},{24,8},{28,12},{1,17},{... | collective-permute-start | bytes 393224 | tf_op jit(solution)/shard_map/ppermute | solution.py:514
  55.6 6.8 %collective-permute-start.16 = (bf16[512,128]{1,0:T(8,128)(2,1)S(1)}, bf16[512,128]{1,0:T(8,128)(2,1)S(1)}, u32[]{:S(2)}, u32[]{:S(2)}) collective-permute-start(bf16[512,128]{1,0:T(8,128)(2,1)S(1)} %get-tuple-element.205), channel_id=1, source_target_pairs={{0,8},{4,12},{8,0},{12,4},{16,24},{20,28},{24,16},{28,20},{1,9},{5... | collective-permute-start | bytes 393224 | tf_op jit(solution)/shard_map/ppermute | solution.py:456
  57.4 6.1 %collective-permute-start.15 = (bf16[512,128]{1,0:T(8,128)(2,1)S(1)}, bf16[512,128]{1,0:T(8,128)(2,1)S(1)}, u32[]{:S(2)}, u32[]{:S(2)}) collective-permute-start(bf16[512,128]{1,0:T(8,128)(2,1)S(1)} %get-tuple-element.203), channel_id=1, source_target_pairs={{0,4},{4,0},{8,12},{12,8},{16,20},{20,16},{24,28},{28,24},{1,5},{5... | collective-permute-start | bytes 393224 | tf_op jit(solution)/shard_map/ppermute | solution.py:456
  58.2 6.3 %collective-permute-start.14 = (bf16[512,128]{1,0:T(8,128)(2,1)S(1)}, bf16[512,128]{1,0:T(8,128)(2,1)S(1)}, u32[]{:S(2)}, u32[]{:S(2)}) collective-permute-start(bf16[512,128]{1,0:T(8,128)(2,1)S(1)} %get-tuple-element.201), channel_id=1, source_target_pairs={{0,12},{4,8},{8,4},{12,0},{16,28},{20,24},{24,20},{28,16},{1,13},{... | collective-permute-start | bytes 393224 | tf_op jit(solution)/shard_map/ppermute | solution.py:456

commit v5 on v4

--- a/solution.py
+++ b/solution.py
@@ -112,11 +112,30 @@
     return list(range(1, size)) + [0]
 
 
+def arrival(size):
+    return list(range(size))
+
+
+def update_slot(plan, table, k_ref, v_ref, turned_ref, sent_ref):
+    hpo, dim = plan.hpo, plan.dim
+    line = lax.broadcasted_iota(jnp.int32, (ROWS, dim), 0)
+    tile = jnp.zeros((ROWS, dim), F32)
+    for i in range(hpo):
+        lanes = plan.head(i)
+        turned = k_ref[:, lanes].T
+        turned_ref[lanes, :] = turned
+        decayed = (turned.astype(F32) * table[2 * hpo + i : 2 * hpo + i + 1]).astype(BF16)
+        sent_ref[lanes, :] = dot(decayed, v_ref[:, lanes]).astype(BF16)
+        carry = jnp.broadcast_to(table[hpo + i : hpo + i + 1, plan.length - 1 :], (ROWS, dim))
+        for j, part in enumerate(three_parts(carry)):
+            tile = jnp.where(line == 3 * i + j, part, tile)
+    sent_ref[hpo * dim :, :] = tile.astype(BF16)
+
+
 def update_kernel(plan, logs_hbm, starts_hbm, k_hbm, v_hbm, *refs):
-    size, hpo, dim, heads = plan.size, plan.hpo, plan.dim, plan.heads
-    sent_refs, k_refs, v_refs, turned_refs = (refs[i * size : (i + 1) * size] for i in range(4))
-    table_ref, logs_ref, starts_ref, natural_ref, small_sems, sems = refs[4 * size :]
-    length = plan.length
+    size, hpo, heads, length = plan.size, plan.hpo, plan.heads, plan.length
+    sent_refs, k_refs, v_refs, turned_refs = (refs[i * (size - 1) : (i + 1) * (size - 1)] for i in range(4))
+    table_ref, logs_ref, starts_ref, natural_ref, small_sems, sems = refs[4 * (size - 1) :]
     copies = [
         pltpu.make_async_copy(logs_hbm, logs_ref, small_sems.at[0]),
         pltpu.make_async_copy(starts_hbm, starts_ref, small_sems.at[1]),
@@ -127,11 +146,11 @@
     def loads(slot):
         lanes = plan.lanes(slot)
         return (
-            pltpu.make_async_copy(k_hbm.at[:, lanes], k_refs[slot], sems.at[0, slot]),
-            pltpu.make_async_copy(v_hbm.at[:, lanes], v_refs[slot], sems.at[1, slot]),
-        )
-
-    for slot in order(size):
+            pltpu.make_async_copy(k_hbm.at[:, lanes], k_refs[slot - 1], sems.at[0, slot]),
+            pltpu.make_async_copy(v_hbm.at[:, lanes], v_refs[slot - 1], sems.at[1, slot]),
+        )
+
+    for slot in range(1, size):
 
         @plan.guard(slot)
         def _():
@@ -153,9 +172,9 @@
     for owner in range(heads // hpo):
         rows = slice(owner * hpo, (owner + 1) * hpo)
         natural_ref[owner] = jnp.concatenate([logs[rows], enter[rows], leave[rows], fill], axis=0)
-    line = lax.broadcasted_iota(jnp.int32, (ROWS, dim), 0)
-
-    for slot in order(size):
+    table_ref[0] = natural_ref[jnp.minimum(my_place(size), heads // hpo - 1)]
+
+    for slot in range(1, size):
 
         @plan.guard(slot)
         def _():
@@ -163,17 +182,8 @@
             table_ref[slot] = table
             for copy in loads(slot):
                 copy.wait()
-            tile = jnp.zeros((ROWS, dim), F32)
-            for i in range(hpo):
-                lanes = plan.head(i)
-                turned = k_refs[slot][:, lanes].T
-                turned_refs[slot][lanes, :] = turned
-                decayed = (turned.astype(F32) * table[2 * hpo + i : 2 * hpo + i + 1]).astype(BF16)
-                sent_refs[slot][lanes, :] = dot(decayed, v_refs[slot][:, lanes]).astype(BF16)
-                carry = jnp.broadcast_to(table[hpo + i : hpo + i + 1, last], (ROWS, dim))
-                for j, part in enumerate(three_parts(carry)):
-                    tile = jnp.where(line == 3 * i + j, part, tile)
-            sent_refs[slot][hpo * dim :, :] = tile.astype(BF16)
+            n = slot - 1
+            update_slot(plan, table, k_refs[n], v_refs[n], turned_refs[n], sent_refs[n])
 
 
 def scan_kernel(plan, forward, *refs):
@@ -218,41 +228,33 @@
             out_ref[rows, :] = (local_ref[b, rows, :] + factor_ref[b, i : i + 1, :] * outer).astype(BF16)
 
 
-def intra_kernel(plan, slot, first_part, table_ref, k_ref, v_ref, *refs):
+def intra_kernel(plan, slot, first_part, table_ref, *refs):
     size, hpo, length = plan.size, plan.hpo, plan.length
-    copies = None
+    copies = []
     if first_part:
-        q_hbm, cot_hbm = refs[:2]
-        q_refs, cot_refs = refs[2 : 2 + size], refs[2 + size : 2 + 2 * size]
-        mask_ref, out_ref, decayed_ref, probs_ref, weight_ref, sems = refs[2 + 2 * size :]
+        q_hbm, cot_hbm, k_hbm, v_hbm, k_ref, v_ref, turned_ref, sent_ref = refs[:8]
+        q_refs, cot_refs = refs[8 : 8 + size], refs[8 + size : 8 + 2 * size]
+        mask_ref, out_ref, decayed_ref, probs_ref, weight_ref, sems = refs[8 + 2 * size :]
         q_ref = q_refs[slot]
-
-        def loads(other):
-            lanes = plan.lanes(other)
-            return (
-                pltpu.make_async_copy(q_hbm.at[:, lanes], q_refs[other], sems.at[0, other]),
-                pltpu.make_async_copy(cot_hbm.at[:, lanes], cot_refs[other], sems.at[1, other]),
-            )
-
-        copies = [loads(other) for other in [slot] + [other for other in range(size) if other != slot]]
-        others = [slot] + [other for other in range(size) if other != slot]
-        for other, pair in zip(others, copies):
-
-            @plan.guard(other)
-            def _():
-                for copy in pair:
-                    copy.start()
-
+        first = [(slot, k_hbm, k_ref), (slot, v_hbm, v_ref), (slot, q_hbm, q_ref)]
+        rest = [(other, q_hbm, q_refs[other]) for other in range(size) if other != slot]
+        rest += [(other, cot_hbm, cot_refs[other]) for other in range(size)]
+        copies = [
+            (other, pltpu.make_async_copy(source.at[:, plan.lanes(other)], target, sems.at[n]))
+            for n, (other, source, target) in enumerate(first + rest)
+        ]
+        start_all(plan, copies)
         mask_ref[...] = block_mask(table_ref[0])
+        wait_all(plan, copies[:3])
     else:
-        q_ref, mask_ref, out_ref, decayed_ref, probs_ref, weight_ref = refs
+        k_ref, v_ref, q_ref, mask_ref, out_ref, decayed_ref, probs_ref, weight_ref = refs
 
     @plan.guard(slot)
     def _():
-        if copies is not None:
-            copies[0][0].wait()
         table = table_ref[slot]
         columns = table.T
+        if first_part:
+            update_slot(plan, table, k_ref, v_ref, turned_ref, sent_ref)
         for i in range(hpo):
             lanes = plan.head(i)
             turned = q_ref[:, lanes].T
@@ -265,22 +267,19 @@
                 probs_ref[i, kept, :] = probs
                 out_ref[later, lanes] = dot(probs, v_ref[seen, lanes], ((0,), (0,)))
 
-    if copies is not None:
-        for other, pair in zip(others, copies):
-
-            @plan.guard(other)
-            def _():
-                for copy in pair if other != slot else pair[1:]:
-                    copy.wait()
+    wait_all(plan, copies[3:])
 
 
 def token_rows(total):
-    ones = jnp.ones((ROWS, total.shape[1]), BF16)
-    row = sum(dot_nt(ones, part.astype(BF16)) for part in three_parts(total))[:1]
-    return jnp.concatenate([row[:, i : i + 128] for i in range(0, total.shape[0], 128)], axis=0)
-
-
-def output_kernel(plan, slot, first_part, last_part, table_ref, q_ref, cot_ref, intra_ref, state_ref, *refs):
+    rows = [jnp.sum(total[i : i + 128].T, axis=0, keepdims=True) for i in range(0, total.shape[0], 128)]
+    return jnp.concatenate(rows, axis=0)
+
+
+def sums_kernel(total_ref, sums_ref):
+    sums_ref[...] = jnp.concatenate([token_rows(total_ref[0]), token_rows(total_ref[1])], axis=0)
+
+
+def output_kernel(plan, slot, first_part, table_ref, q_ref, cot_ref, intra_ref, state_ref, *refs):
     hpo = plan.hpo
     if not first_part:
         old_ref, refs = refs[0], refs[1:]
@@ -306,9 +305,6 @@
         total_ref[0] = square
         total_ref[1] = cross
 
-    if last_part:
-        refs[2][...] = jnp.concatenate([token_rows(total_ref[0]), token_rows(total_ref[1])], axis=0)
-
 
 def factors(sums_refs, factor_ref):
     total = sums_refs[0][...]
@@ -392,18 +388,18 @@
             lanes = plan.head(i)
             gout_turned = gout_ref[:, lanes].T
             carried = table[hpo + i : hpo + i + 1] * dot(state_ref[lanes, :], gout_turned)
-            for later, seen, kept in reversed(list(plan.tiles())):
-                grads = dot(v_ref[seen, lanes], gout_turned[:, later])
-                grads = (grads * weight_ref[i, kept, :].astype(F32)).astype(BF16)
-                from_probs = dot(probs_ref[i, kept, :], gout_ref[later, lanes])
-                from_grads = dot(grads, q_ref[later, lanes])
-                if seen.stop == length:
-                    gv_ref[:, lanes] = from_probs
-                    gk_ref[:, lanes] = from_grads
-                else:
-                    gv_ref[seen, lanes] += from_probs
-                    gk_ref[seen, lanes] += from_grads
-                total = carried[:, later] + dot(turned_ref[lanes, seen], grads)
+            tiles = list(plan.tiles())
+            grads = [None] * len(tiles)
+            for j, (later, seen, kept) in reversed(list(enumerate(tiles))):
+                product = dot(v_ref[seen, lanes], gout_turned[:, later])
+                grads[j] = (product * weight_ref[i, kept, :].astype(F32)).astype(BF16)
+            probs = [probs_ref[i, kept, :] for _, _, kept in tiles]
+            for target, lefts, right_ref in ((gv_ref, probs, gout_ref), (gk_ref, grads, q_ref)):
+                parts = [dot(left, right_ref[later, lanes]) for left, (later, _, _) in zip(lefts, tiles)]
+                for j, (rows, _, _) in enumerate(tiles):
+                    target[rows, lanes] = functools.reduce(jnp.add, [part[rows] for part in reversed(parts[j:])])
+            for grad, (later, seen, _) in zip(grads, tiles):
+                total = carried[:, later] + dot(turned_ref[lanes, seen], grad)
                 gq_ref[later, lanes] = total.astype(BF16).T
 
     wait_all(plan, copies)
@@ -526,13 +522,14 @@
 
     big, small = length * length * dim, length * dim * dim
     queries, keys, values, cotangent = (outside(a) for a in (queries, keys, values, cotangent))
+    others = size - 1
     results = call(
         functools.partial(update_kernel, plan),
         "update",
         [(outside(log_decay),), (outside(starts.reshape(1, length)),), (keys,), (values,)],
-        [pltpu.VMEM((span + ROWS, dim), BF16)] * size
-        + [held(BF16)] * (2 * size)
-        + [pltpu.VMEM((span, length), BF16)] * size
+        [pltpu.VMEM((span + ROWS, dim), BF16)] * others
+        + [held(BF16)] * (2 * others)
+        + [pltpu.VMEM((span, length), BF16)] * others
         + [pltpu.VMEM((size, ROWS, length), F32)],
         cost(size * small),
         scratch=[
@@ -543,9 +540,10 @@
             dma((2, size)),
         ],
     )
-    sent, k, v, turned = (results[i * size : (i + 1) * size] for i in range(4))
+    sent, k, v, turned = ([None, *results[i * others : (i + 1) * others]] for i in range(4))
     table = results[-1]
     received = exchange(sent, size, halves, partner)
+    own = [held(BF16)] * 2 + [pltpu.VMEM((span, length), BF16), pltpu.VMEM((span + ROWS, dim), BF16)]
 
     kept = pltpu.VMEM((hpo, length * (length + HALF) // 2 // HALF, HALF), BF16)
     intra, decayed, probs, weights = [], [], [], []
@@ -554,37 +552,38 @@
         results = call(
             functools.partial(intra_kernel, plan, slot, first),
             "intra",
-            [table, k[slot], v[slot]] + ([(queries,), (cotangent,)] if first else [q[slot], mask]),
-            ([held(BF16)] * (2 * size) + [pltpu.VMEM((length, length), F32)] if first else [])
+            [table] + ([(a,) for a in (queries, cotangent, keys, values)] if first else [k[slot], v[slot], q[slot], mask]),
+            (own + [held(BF16)] * (2 * size) + [pltpu.VMEM((length, length), F32)] if first else [])
             + [held(F32), pltpu.VMEM((span, length), BF16), kept, kept],
             cost(2 * big, length * length),
-            scratch=[dma((2, size))] if first else [],
+            scratch=[dma((2 + 2 * size,))] if first else [],
         )
         if first:
+            k[0], v[0], turned[0], sent[0], *results = results
             q, cot, mask = results[:size], results[size : 2 * size], results[2 * size]
         for kind, result in zip((intra, decayed, probs, weights), results[-4:]):
             kind.append(result)
 
     middle = -(-size // 2)
+    received[0] = sent[0]
     received, carries = scan(received, None, intra[:middle], intra[middle:])
 
-    outputs = []
-    total = sums = None
-    for slot in range(size):
-        first, last = slot == 0, slot == size - 1
-        out, total, *rest = call(
-            functools.partial(output_kernel, plan, slot, first, last),
+    outputs = [None] * size
+    total = None
+    for slot in arrival(size):
+        first = slot == 0
+        outputs[slot], total = call(
+            functools.partial(output_kernel, plan, slot, first),
             "output",
             [table, q[slot], cot[slot], intra[slot], received[slot]] + ([] if first else [total]),
-            [held(F32), pltpu.VMEM((2, length, dim), F32)] + ([pltpu.VMEM((2 * length // 128, 128), F32)] if last else []),
+            [held(F32), pltpu.VMEM((2, length, dim), F32)],
             cost(small),
         )
-        outputs.append(out)
-        sums = rest[0] if last else sums
+    (sums,) = call(sums_kernel, "sums", [total], [pltpu.VMEM((2 * length // 128, 128), F32)], cost(length))
     states = received
 
     everyone = [sums] + [
-        lax.ppermute(sums, "head", [(i, partner(i, k, shares)) for i in range(shares)]) for k in range(1, shares)
+        lax.ppermute(sums, "head", [(i, partner(i, k, shares)) for i in range(shares)]) for k in [*range(2, shares), 1]
     ]
 
     gout, sent = [None] * size, [None] * size
@@ -636,18 +635,19 @@
 
     gk_whole = gv_whole = None
     gk = gv = None
-    for slot in range(size):
-        first, last = slot == 0, slot == size - 1
-        finished = [("gq", size - 1)] if first else [("gk", slot - 1), ("gv", slot - 1)]
+    slots = arrival(size)
+    for n, slot in enumerate(slots):
+        first, last = n == 0, n == size - 1
+        finished = [("gq", size - 1)] if first else [("gk", slots[n - 1]), ("gv", slots[n - 1])]
         done = [gq[-1]] if first else [gk, gv]
         operands = [table, k[slot], v[slot], gk_part[slot], gv_part[slot], received[slot]] + done
         held_back = [gq_whole, gk_whole, gv_whole]
         fresh = [a is None for a in held_back]
         aliases = {}
         chained = []
-        for n, array in enumerate(held_back):
+        for m, array in enumerate(held_back):
             if array is not None:
-                aliases[len(operands) + len(chained)] = n
+                aliases[len(operands) + len(chained)] = m
                 chained.append((array,))
         gq_whole, gk_whole, gv_whole, gk, gv = call(
             functools.partial(final_kernel, plan, slot, finished, fresh, last),

time: 67.3 us -> 65.4 us (0.972)
  Pallas kernels: 32.2 us -> 30.1 us
    pallas_call x26 -> x27, Pallas kernels: 32.2 us -> 30.1 us  [call(): pl.pallas_call(kernel, in_specs=[hbm if f else inside for f in far] + [un...]
    ppermute x3, waiting for transfers between devices: 2.86 us -> 2.09 us  [per_device(): lax.ppermute(sums, 'head', [(i, partner(i, k, shares)) for i in range(sha...]
  transfers between devices with their start and end apart: 17 -> 17, of which waited for: 8 -> 9; matrix products, arithmetic and copies ran while one was open for 0% -> 0% of each run, Pallas kernels for 36% -> 35%
where the time goes in v5:
time: 65.4 us; the launch traced here: 65.3 us
  Pallas kernels  30.1 us (46%)
  starting transfers between devices  23.3 us (36%)
  waiting for transfers between devices  10.9 us (17%)
  between operations  1.03 us (2%)
    pallas_call x27, Pallas kernels, call(): pl.pallas_call(kernel, in_specs=[hbm if f else inside for f in far] + [un...  30.1 us
    ppermute x12, starting transfers between devices, exchange(): lax.ppermute(arrays[slot], 'seq', pairs(slot))  15.4 us
    ppermute x12, waiting for transfers between devices, exchange(): lax.ppermute(arrays[slot], 'seq', pairs(slot))  6.62 us
    ppermute x2, starting transfers between devices, scan(): outer = lax.ppermute(total, 'seq', pairs)  5.63 us
    ppermute x3, starting transfers between devices, per_device(): lax.ppermute(sums, 'head', [(i, partner(i, k, shares)) for i in range(sha...  2.21 us
    ppermute x2, waiting for transfers between devices, scan(): outer = lax.ppermute(total, 'seq', pairs)  2.17 us
    ppermute x3, waiting for transfers between devices, per_device(): lax.ppermute(sums, 'head', [(i, partner(i, k, shares)) for i in range(sha...  2.09 us
  transfers between devices with their start and end apart: 17, of which 9 were waited for; matrix products, arithmetic and copies ran while one was open for 0% of the time, Pallas kernels for 35%

profile of v5, /device:TPU:0, one launch (start us, length us, event | category | flops | bytes accessed | tf_op | source)
XLA Modules:
  0.0 65.3 jit_solution(15844200637048506983)
XLA Ops:
  0.6 2.4 %update.1 = (bf16[528,128]{1,0:T(8,128)(2,1)S(1)}, bf16[528,128]{1,0:T(8,128)(2,1)S(1)}, bf16[528,128]{1,0:T(8,128)(2,1)S(1)}, bf16[512,512]{1,0:T(8,128)(2,1)S(...) custom-call(f32[16,512]{1,0:T(8,128)} %logs_hbm.1, ...), custom_call_target="tpu_custom_call" | custom-call | flops 268435456 | bytes 262144 | tf_op jit(solution)/shard_map/update/pallas_call | solution.py:484
  3.1 3.1 %collective-permute-start = (bf16[528,128]{1,0:T(8,128)(2,1)S(1)}, bf16[528,128]{1,0:T(8,128)(2,1)S(1)}, u32[]{:S(2)}, u32[]{:S(2)}) collective-permute-start(bf16[528,128]{1,0:T(8,128)(2,1)S(1)} %get-tuple-element.127), channel_id=1, source_target_pairs={{0,8},{4,12},{8,0},{12,4},{16,24},{20,28},{24,16},{28,20},{1,9},{5... | collective-permute-start | bytes 405512 | tf_op jit(solution)/shard_map/ppermute | solution.py:452
  6.2 1.5 %collective-permute-start.1 = (bf16[528,128]{1,0:T(8,128)(2,1)S(1)}, bf16[528,128]{1,0:T(8,128)(2,1)S(1)}, u32[]{:S(2)}, u32[]{:S(2)}) collective-permute-start(bf16[528,128]{1,0:T(8,128)(2,1)S(1)} %get-tuple-element.128), channel_id=1, source_target_pairs={{0,4},{4,0},{8,12},{12,8},{16,20},{20,16},{24,28},{28,24},{1,5},{5... | collective-permute-start | bytes 405512 | tf_op jit(solution)/shard_map/ppermute | solution.py:452
  7.7 3.5 %intra.4 = (bf16[512,512]{1,0:T(8,128)(2,1)S(1)}, bf16[512,512]{1,0:T(8,128)(2,1)S(1)}, bf16[512,512]{1,0:T(8,128)(2,1)S(1)}, bf16[528,128]{1,0:T(8,128)(2,1)S(1...) custom-call(f32[4,16,512]{2,1,0:T(8,128)S(1)} %get-tuple-element.116, ...), custom_call_target="tpu_custom_call" | custom-call | flops 536870912 | bytes 262144 | tf_op jit(solution)/shard_map/intra/pallas_call | solution.py:484
  11.2 1.8 %intra.6 = (f32[512,512]{1,0:T(8,128)S(1)}, bf16[512,512]{1,0:T(8,128)(2,1)S(1)}, bf16[4,768,256]{2,1,0:T(8,128)(2,1)S(1)}, bf16[4,768,256]{2,1,0:T(8,128)(2,1)S(1)}) custom-call(f32[4,16,512]{2,1,0:T(8,128)S(1)} %get-tuple-element.116.table_ref.refs_0_, bf16[512,512]{1,0:T(8,128)(2,1)S(1)} %get-tuple-element.131.refs_0_.refs_1_, ...), custom_call_target="tpu_custom_call" | custom-call | flops 536870912 | bytes 262144 | tf_op jit(solution)/shard_map/intra/pallas_call | solution.py:484
  13.0 1.1 %collective-permute-done.1.refs_2_ = bf16[528,128]{1,0:T(8,128)(2,1)S(1)} collective-permute-done((bf16[528,128]{1,0:T(8,128)(2,1)S(1)}, bf16[528,128]{1,0:T(8,128)(2,1)S(1)}, u32[]{:S(2)}, u32[]{:S(2)}) %collective-permute-start.1) | collective-permute-done | bytes 135200 | tf_op jit(solution)/shard_map/ppermute | solution.py:452
  14.3 2.7 %collective-permute-start.3 = (bf16[512,128]{1,0:T(8,128)(2,1)S(1)}, bf16[512,128]{1,0:T(8,128)(2,1)S(1)}, u32[]{:S(2)}, u32[]{:S(2)}) collective-permute-start(bf16[512,128]{1,0:T(8,128)(2,1)S(1)} %get-tuple-element.137), channel_id=1, source_target_pairs={{0,16},{4,20},{8,24},{12,28},{16,0},{20,4},{24,8},{28,12},{1,17},{... | collective-permute-start | bytes 393224 | tf_op jit(solution)/shard_map/ppermute | solution.py:510
  17.0 1.8 %intra.5 = (f32[512,512]{1,0:T(8,128)S(1)}, bf16[512,512]{1,0:T(8,128)(2,1)S(1)}, bf16[4,768,256]{2,1,0:T(8,128)(2,1)S(1)}, bf16[4,768,256]{2,1,0:T(8,128)(2,1)S(1)}) custom-call(f32[4,16,512]{2,1,0:T(8,128)S(1)} %get-tuple-element.116.table_ref.refs_0_, bf16[512,512]{1,0:T(8,128)(2,1)S(1)} %get-tuple-element.122.refs_0_.refs_1_, ...), custom_call_target="tpu_custom_call" | custom-call | flops 536870912 | bytes 262144 | tf_op jit(solution)/shard_map/intra/pallas_call | solution.py:484
  18.7 1.8 %intra.7 = (f32[512,512]{1,0:T(8,128)S(1)}, bf16[512,512]{1,0:T(8,128)(2,1)S(1)}, bf16[4,768,256]{2,1,0:T(8,128)(2,1)S(1)}, bf16[4,768,256]{2,1,0:T(8,128)(2,1)S(1)}) custom-call(f32[4,16,512]{2,1,0:T(8,128)S(1)} %get-tuple-element.116.table_ref.refs_0_, bf16[512,512]{1,0:T(8,128)(2,1)S(1)} %get-tuple-element.138.refs_0_.refs_1_, ...), custom_call_target="tpu_custom_call" | custom-call | flops 536870912 | bytes 262144 | tf_op jit(solution)/shard_map/intra/pallas_call | solution.py:484
  20.5 1.4 %collective-permute-done.3.outer_ref = bf16[512,128]{1,0:T(8,128)(2,1)S(1)} collective-permute-done((bf16[512,128]{1,0:T(8,128)(2,1)S(1)}, bf16[512,128]{1,0:T(8,128)(2,1)S(1)}, u32[]{:S(2)}, u32[]{:S(2)}) %collective-permute-start.3) | collective-permute-done | bytes 131104 | tf_op jit(solution)/shard_map/ppermute | solution.py:510
  22.8 1.3 %collective-permute-start.5 = (bf16[512,128]{1,0:T(8,128)(2,1)S(1)}, bf16[512,128]{1,0:T(8,128)(2,1)S(1)}, u32[]{:S(2)}, u32[]{:S(2)}) collective-permute-start(bf16[512,128]{1,0:T(8,128)(2,1)S(1)} %get-tuple-element.144), channel_id=1, source_target_pairs={{0,4},{4,0},{8,12},{12,8},{16,20},{20,16},{24,28},{28,24},{1,5},{5... | collective-permute-start | bytes 393224 | tf_op jit(solution)/shard_map/ppermute | solution.py:452
  24.1 1.5 %collective-permute-start.4 = (bf16[512,128]{1,0:T(8,128)(2,1)S(1)}, bf16[512,128]{1,0:T(8,128)(2,1)S(1)}, u32[]{:S(2)}, u32[]{:S(2)}) collective-permute-start(bf16[512,128]{1,0:T(8,128)(2,1)S(1)} %get-tuple-element.142), channel_id=1, source_target_pairs={{0,12},{4,8},{8,4},{12,0},{16,28},{20,24},{24,20},{28,16},{1,13},{... | collective-permute-start | bytes 393224 | tf_op jit(solution)/shard_map/ppermute | solution.py:452
  26.2 2.0 %collective-permute-done.6.state_ref.refs_8_ = bf16[512,128]{1,0:T(8,128)(2,1)S(1)} collective-permute-done((bf16[512,128]{1,0:T(8,128)(2,1)S(1)}, bf16[512,128]{1,0:T(8,128)(2,1)S(1)}, u32[]{:S(2)}, u32[]{:S(2)}) %collective-permute-start.6) | collective-permute-done | bytes 131104 | tf_op jit(solution)/shard_map/ppermute | solution.py:452
  29.8 1.0 %collective-permute-done.4.state_ref.refs_8_ = bf16[512,128]{1,0:T(8,128)(2,1)S(1)} collective-permute-done((bf16[512,128]{1,0:T(8,128)(2,1)S(1)}, bf16[512,128]{1,0:T(8,128)(2,1)S(1)}, u32[]{:S(2)}, u32[]{:S(2)}) %collective-permute-start.4) | collective-permute-done | bytes 131104 | tf_op jit(solution)/shard_map/ppermute | solution.py:452
  31.6 1.3 %collective-permute-start.9 = (f32[8,128]{1,0:T(8,128)S(1)}, f32[8,128]{1,0:T(8,128)S(1)}, u32[]{:S(2)}, u32[]{:S(2)}) collective-permute-start(f32[8,128]{1,0:T(8,128)S(1)} %sums.1.refs_0_), channel_id=1, source_target_pairs={{0,2},{1,3},{2,0},{3,1},{4,6},{5,7},{6,4},{7,5},{8,10},{9,11},{10,... | collective-permute-start | bytes 12296 | tf_op jit(solution)/shard_map/ppermute | solution.py:586
  32.9 0.9 %collective-permute-start.7 = (f32[8,128]{1,0:T(8,128)S(1)}, f32[8,128]{1,0:T(8,128)S(1)}, u32[]{:S(2)}, u32[]{:S(2)}) collective-permute-start(f32[8,128]{1,0:T(8,128)S(1)} %sums.1.refs_0_), channel_id=1, source_target_pairs={{0,1},{1,0},{2,3},{3,2},{4,5},{5,4},{6,7},{7,6},{8,9},{9,8},{10,11... | collective-permute-start | bytes 12296 | tf_op jit(solution)/shard_map/ppermute | solution.py:586
  33.8 1.5 %collective-permute-done.9.refs_3_ = f32[8,128]{1,0:T(8,128)S(1)} collective-permute-done((f32[8,128]{1,0:T(8,128)S(1)}, f32[8,128]{1,0:T(8,128)S(1)}, u32[]{:S(2)}, u32[]{:S(2)}) %collective-permute-start.9) | collective-permute-done | bytes 4128 | tf_op jit(solution)/shard_map/ppermute | solution.py:586
  36.7 1.2 %collective-permute-start.10 = (bf16[512,128]{1,0:T(8,128)(2,1)S(1)}, bf16[512,128]{1,0:T(8,128)(2,1)S(1)}, u32[]{:S(2)}, u32[]{:S(2)}) collective-permute-start(bf16[512,128]{1,0:T(8,128)(2,1)S(1)} %get-tuple-element.191), channel_id=1, source_target_pairs={{0,8},{4,12},{8,0},{12,4},{16,24},{20,28},{24,16},{28,20},{1,9},{5... | collective-permute-start | bytes 393224 | tf_op jit(solution)/shard_map/ppermute | solution.py:452
  38.4 1.3 %collective-permute-start.11 = (bf16[512,128]{1,0:T(8,128)(2,1)S(1)}, bf16[512,128]{1,0:T(8,128)(2,1)S(1)}, u32[]{:S(2)}, u32[]{:S(2)}) collective-permute-start(bf16[512,128]{1,0:T(8,128)(2,1)S(1)} %get-tuple-element.192), channel_id=1, source_target_pairs={{0,4},{4,0},{8,12},{12,8},{16,20},{20,16},{24,28},{28,24},{1,5},{5... | collective-permute-start | bytes 393224 | tf_op jit(solution)/shard_map/ppermute | solution.py:452
  40.2 1.2 %collective-permute-start.12 = (bf16[512,128]{1,0:T(8,128)(2,1)S(1)}, bf16[512,128]{1,0:T(8,128)(2,1)S(1)}, u32[]{:S(2)}, u32[]{:S(2)}) collective-permute-start(bf16[512,128]{1,0:T(8,128)(2,1)S(1)} %get-tuple-element.193), channel_id=1, source_target_pairs={{0,12},{4,8},{8,4},{12,0},{16,28},{20,24},{24,20},{28,16},{1,13},{... | collective-permute-start | bytes 393224 | tf_op jit(solution)/shard_map/ppermute | solution.py:452
  42.5 1.9 %gradient.4 = (bf16[512,2048]{1,0:T(8,128)(2,1)}, bf16[512,512]{1,0:T(8,128)(2,1)S(1)}, f32[512,512]{1,0:T(8,128)S(1)}, f32[512,512]{1,0:T(8,128)S(1)}) custom-call(f32[4,16,512]{2,1,0:T(8,128)S(1)} %get-tuple-element.116.table_ref.refs_0_, bf16[512,512]{1,0:T(8,128)(2,1)S(1)} %get-tuple-element.117.refs_1_, ...), custom_call_target="tpu_custom_call" | custom-call | flops 1073741824 | bytes 262144 | tf_op jit(solution)/shard_map/gradient/pallas_call | solution.py:484
  44.3 2.2 %collective-permute-done.11.refs_2_ = bf16[512,128]{1,0:T(8,128)(2,1)S(1)} collective-permute-done((bf16[512,128]{1,0:T(8,128)(2,1)S(1)}, bf16[512,128]{1,0:T(8,128)(2,1)S(1)}, u32[]{:S(2)}, u32[]{:S(2)}) %collective-permute-start.11) | collective-permute-done | bytes 131104 | tf_op jit(solution)/shard_map/ppermute | solution.py:452
  46.7 3.0 %collective-permute-start.13 = (bf16[512,128]{1,0:T(8,128)(2,1)S(1)}, bf16[512,128]{1,0:T(8,128)(2,1)S(1)}, u32[]{:S(2)}, u32[]{:S(2)}) collective-permute-start(bf16[512,128]{1,0:T(8,128)(2,1)S(1)} %get-tuple-element.198), channel_id=1, source_target_pairs={{0,16},{4,20},{8,24},{12,28},{16,0},{20,4},{24,8},{28,12},{1,17},{... | collective-permute-start | bytes 393224 | tf_op jit(solution)/shard_map/ppermute | solution.py:510
  49.7 1.8 %gradient.5 = (bf16[512,2048]{1,0:T(8,128)(2,1)}, bf16[512,512]{1,0:T(8,128)(2,1)S(1)}, f32[512,512]{1,0:T(8,128)S(1)}, f32[512,512]{1,0:T(8,128)S(1)}) custom-call(f32[4,16,512]{2,1,0:T(8,128)S(1)} %get-tuple-element.116.table_ref.refs_0_, bf16[512,512]{1,0:T(8,128)(2,1)S(1)} %get-tuple-element.131.refs_0_.refs_1_, ...), custom_call_target="tpu_custom_call" | custom-call | flops 1073741824 | bytes 262144 | tf_op jit(solution)/shard_map/gradient/pallas_call | solution.py:484
  51.5 1.9 %gradient.6 = (bf16[512,2048]{1,0:T(8,128)(2,1)}, bf16[512,512]{1,0:T(8,128)(2,1)S(1)}, f32[512,512]{1,0:T(8,128)S(1)}, f32[512,512]{1,0:T(8,128)S(1)}) custom-call(f32[4,16,512]{2,1,0:T(8,128)S(1)} %get-tuple-element.116.table_ref.refs_0_, bf16[512,512]{1,0:T(8,128)(2,1)S(1)} %get-tuple-element.138.refs_0_.refs_1_, ...), custom_call_target="tpu_custom_call", output_to_operand_aliasing={{0}: (10, {})} | custom-call | flops 1073741824 | bytes 262144 | tf_op jit(solution)/shard_map/gradient/pallas_call | solution.py:484
  54.3 1.1 %collective-permute-start.16 = (bf16[512,128]{1,0:T(8,128)(2,1)S(1)}, bf16[512,128]{1,0:T(8,128)(2,1)S(1)}, u32[]{:S(2)}, u32[]{:S(2)}) collective-permute-start(bf16[512,128]{1,0:T(8,128)(2,1)S(1)} %get-tuple-element.205), channel_id=1, source_target_pairs={{0,8},{4,12},{8,0},{12,4},{16,24},{20,28},{24,16},{28,20},{1,9},{5... | collective-permute-start | bytes 393224 | tf_op jit(solution)/shard_map/ppermute | solution.py:452
  55.3 0.9 %collective-permute-start.15 = (bf16[512,128]{1,0:T(8,128)(2,1)S(1)}, bf16[512,128]{1,0:T(8,128)(2,1)S(1)}, u32[]{:S(2)}, u32[]{:S(2)}) collective-permute-start(bf16[512,128]{1,0:T(8,128)(2,1)S(1)} %get-tuple-element.203), channel_id=1, source_target_pairs={{0,4},{4,0},{8,12},{12,8},{16,20},{20,16},{24,28},{28,24},{1,5},{5... | collective-permute-start | bytes 393224 | tf_op jit(solution)/shard_map/ppermute | solution.py:452
  56.2 1.6 %collective-permute-start.14 = (bf16[512,128]{1,0:T(8,128)(2,1)S(1)}, bf16[512,128]{1,0:T(8,128)(2,1)S(1)}, u32[]{:S(2)}, u32[]{:S(2)}) collective-permute-start(bf16[512,128]{1,0:T(8,128)(2,1)S(1)} %get-tuple-element.201), channel_id=1, source_target_pairs={{0,12},{4,8},{8,4},{12,0},{16,28},{20,24},{24,20},{28,16},{1,13},{... | collective-permute-start | bytes 393224 | tf_op jit(solution)/shard_map/ppermute | solution.py:452
  57.8 1.8 %gradient.7 = (bf16[512,2048]{1,0:T(8,128)(2,1)}, bf16[512,512]{1,0:T(8,128)(2,1)S(1)}, f32[512,512]{1,0:T(8,128)S(1)}, f32[512,512]{1,0:T(8,128)S(1)}) custom-call(f32[4,16,512]{2,1,0:T(8,128)S(1)} %get-tuple-element.116.table_ref.refs_0_, bf16[512,512]{1,0:T(8,128)(2,1)S(1)} %get-tuple-element.122.refs_0_.refs_1_, ...), custom_call_target="tpu_custom_call", output_to_operand_aliasing={{0}: (10, {})} | custom-call | flops 1073741824 | bytes 262144 | tf_op jit(solution)/shard_map/gradient/pallas_call | solution.py:484
  60.5 1.0 %final.5 = (bf16[512,2048]{1,0:T(8,128)(2,1)}, bf16[512,2048]{1,0:T(8,128)(2,1)}, bf16[512,2048]{1,0:T(8,128)(2,1)}, bf16[512,512]{1,0:T(8,128)(2,1)S(1)}, bf16[512,512]{1,0:T(8,128)(2,1)S(1)}) custom-call(f32[4,16,512]{2,1,0:T(8,128)S(1)} %get-tuple-element.116.table_ref.refs_0_, ...), custom_call_target="tpu_custom_call", output_to_operand_aliasing={{0}: (8, {}), {1}: (9, {}), {2}: (10, {})} | custom-call | flops 134217728 | bytes 262144 | tf_op jit(solution)/shard_map/final/pallas_call | solution.py:484
  61.6 1.0 %final.6 = (bf16[512,2048]{1,0:T(8,128)(2,1)}, bf16[512,2048]{1,0:T(8,128)(2,1)}, bf16[512,2048]{1,0:T(8,128)(2,1)}, bf16[512,512]{1,0:T(8,128)(2,1)S(1)}, bf16[512,512]{1,0:T(8,128)(2,1)S(1)}) custom-call(f32[4,16,512]{2,1,0:T(8,128)S(1)} %get-tuple-element.116.table_ref.refs_0_, ...), custom_call_target="tpu_custom_call", output_to_operand_aliasing={{0}: (8, {}), {1}: (9, {}), {2}: (10, {})} | custom-call | flops 134217728 | bytes 262144 | tf_op jit(solution)/shard_map/final/pallas_call | solution.py:484
  62.6 2.5 %final.7 = (bf16[512,2048]{1,0:T(8,128)(2,1)}, bf16[512,2048]{1,0:T(8,128)(2,1)}, bf16[512,2048]{1,0:T(8,128)(2,1)}, bf16[512,512]{1,0:T(8,128)(2,1)}, bf16[512,512]{1,0:T(8,128)(2,1)}) custom-call(f32[4,16,512]{2,1,0:T(8,128)S(1)} %get-tuple-element.116.table_ref.refs_0_, ...), custom_call_target="tpu_custom_call", output_to_operand_aliasing={{0}: (8, {}), {1}: (9, {}), {2}: (10, {})} | custom-call | flops 134217728 | bytes 262144 | tf_op jit(solution)/shard_map/final/pallas_call | solution.py:484
  (29 shorter events, 9.4 us)
Async XLA Ops:
  3.1 9.9 %collective-permute-start = (bf16[528,128]{1,0:T(8,128)(2,1)S(1)}, bf16[528,128]{1,0:T(8,128)(2,1)S(1)}, u32[]{:S(2)}, u32[]{:S(2)}) collective-permute-start(bf16[528,128]{1,0:T(8,128)(2,1)S(1)} %get-tuple-element.127), channel_id=1, source_target_pairs={{0,8},{4,12},{8,0},{12,4},{16,24},{20,28},{24,16},{28,20},{1,9},{5... | collective-permute-start | bytes 405512 | tf_op jit(solution)/shard_map/ppermute | solution.py:452
  6.2 7.9 %collective-permute-start.1 = (bf16[528,128]{1,0:T(8,128)(2,1)S(1)}, bf16[528,128]{1,0:T(8,128)(2,1)S(1)}, u32[]{:S(2)}, u32[]{:S(2)}) collective-permute-start(bf16[528,128]{1,0:T(8,128)(2,1)S(1)} %get-tuple-element.128), channel_id=1, source_target_pairs={{0,4},{4,0},{8,12},{12,8},{16,20},{20,16},{24,28},{28,24},{1,5},{5... | collective-permute-start | bytes 405512 | tf_op jit(solution)/shard_map/ppermute | solution.py:452
  7.7 6.5 %collective-permute-start.2 = (bf16[528,128]{1,0:T(8,128)(2,1)S(1)}, bf16[528,128]{1,0:T(8,128)(2,1)S(1)}, u32[]{:S(2)}, u32[]{:S(2)}) collective-permute-start(bf16[528,128]{1,0:T(8,128)(2,1)S(1)} %get-tuple-element.129), channel_id=1, source_target_pairs={{0,12},{4,8},{8,4},{12,0},{16,28},{20,24},{24,20},{28,16},{1,13},{... | collective-permute-start | bytes 405512 | tf_op jit(solution)/shard_map/ppermute | solution.py:452
  14.3 7.6 %collective-permute-start.3 = (bf16[512,128]{1,0:T(8,128)(2,1)S(1)}, bf16[512,128]{1,0:T(8,128)(2,1)S(1)}, u32[]{:S(2)}, u32[]{:S(2)}) collective-permute-start(bf16[512,128]{1,0:T(8,128)(2,1)S(1)} %get-tuple-element.137), channel_id=1, source_target_pairs={{0,16},{4,20},{8,24},{12,28},{16,0},{20,4},{24,8},{28,12},{1,17},{... | collective-permute-start | bytes 393224 | tf_op jit(solution)/shard_map/ppermute | solution.py:510
  22.0 6.2 %collective-permute-start.6 = (bf16[512,128]{1,0:T(8,128)(2,1)S(1)}, bf16[512,128]{1,0:T(8,128)(2,1)S(1)}, u32[]{:S(2)}, u32[]{:S(2)}) collective-permute-start(bf16[512,128]{1,0:T(8,128)(2,1)S(1)} %get-tuple-element.146), channel_id=1, source_target_pairs={{0,8},{4,12},{8,0},{12,4},{16,24},{20,28},{24,16},{28,20},{1,9},{5... | collective-permute-start | bytes 393224 | tf_op jit(solution)/shard_map/ppermute | solution.py:452
  22.8 6.4 %collective-permute-start.5 = (bf16[512,128]{1,0:T(8,128)(2,1)S(1)}, bf16[512,128]{1,0:T(8,128)(2,1)S(1)}, u32[]{:S(2)}, u32[]{:S(2)}) collective-permute-start(bf16[512,128]{1,0:T(8,128)(2,1)S(1)} %get-tuple-element.144), channel_id=1, source_target_pairs={{0,4},{4,0},{8,12},{12,8},{16,20},{20,16},{24,28},{28,24},{1,5},{5... | collective-permute-start | bytes 393224 | tf_op jit(solution)/shard_map/ppermute | solution.py:452
  24.1 6.7 %collective-permute-start.4 = (bf16[512,128]{1,0:T(8,128)(2,1)S(1)}, bf16[512,128]{1,0:T(8,128)(2,1)S(1)}, u32[]{:S(2)}, u32[]{:S(2)}) collective-permute-start(bf16[512,128]{1,0:T(8,128)(2,1)S(1)} %get-tuple-element.142), channel_id=1, source_target_pairs={{0,12},{4,8},{8,4},{12,0},{16,28},{20,24},{24,20},{28,16},{1,13},{... | collective-permute-start | bytes 393224 | tf_op jit(solution)/shard_map/ppermute | solution.py:452
  31.6 3.7 %collective-permute-start.9 = (f32[8,128]{1,0:T(8,128)S(1)}, f32[8,128]{1,0:T(8,128)S(1)}, u32[]{:S(2)}, u32[]{:S(2)}) collective-permute-start(f32[8,128]{1,0:T(8,128)S(1)} %sums.1.refs_0_), channel_id=1, source_target_pairs={{0,2},{1,3},{2,0},{3,1},{4,6},{5,7},{6,4},{7,5},{8,10},{9,11},{10,... | collective-permute-start | bytes 12296 | tf_op jit(solution)/shard_map/ppermute | solution.py:586
  32.9 3.0 %collective-permute-start.8 = (f32[8,128]{1,0:T(8,128)S(1)}, f32[8,128]{1,0:T(8,128)S(1)}, u32[]{:S(2)}, u32[]{:S(2)}) collective-permute-start(f32[8,128]{1,0:T(8,128)S(1)} %sums.1.refs_0_), channel_id=1, source_target_pairs={{0,3},{1,2},{2,1},{3,0},{4,7},{5,6},{6,5},{7,4},{8,11},{9,10},{10,... | collective-permute-start | bytes 12296 | tf_op jit(solution)/shard_map/ppermute | solution.py:586
  32.9 3.0 %collective-permute-start.7 = (f32[8,128]{1,0:T(8,128)S(1)}, f32[8,128]{1,0:T(8,128)S(1)}, u32[]{:S(2)}, u32[]{:S(2)}) collective-permute-start(f32[8,128]{1,0:T(8,128)S(1)} %sums.1.refs_0_), channel_id=1, source_target_pairs={{0,1},{1,0},{2,3},{3,2},{4,5},{5,4},{6,7},{7,6},{8,9},{9,8},{10,11... | collective-permute-start | bytes 12296 | tf_op jit(solution)/shard_map/ppermute | solution.py:586
  36.7 7.6 %collective-permute-start.10 = (bf16[512,128]{1,0:T(8,128)(2,1)S(1)}, bf16[512,128]{1,0:T(8,128)(2,1)S(1)}, u32[]{:S(2)}, u32[]{:S(2)}) collective-permute-start(bf16[512,128]{1,0:T(8,128)(2,1)S(1)} %get-tuple-element.191), channel_id=1, source_target_pairs={{0,8},{4,12},{8,0},{12,4},{16,24},{20,28},{24,16},{28,20},{1,9},{5... | collective-permute-start | bytes 393224 | tf_op jit(solution)/shard_map/ppermute | solution.py:452
  38.4 8.1 %collective-permute-start.11 = (bf16[512,128]{1,0:T(8,128)(2,1)S(1)}, bf16[512,128]{1,0:T(8,128)(2,1)S(1)}, u32[]{:S(2)}, u32[]{:S(2)}) collective-permute-start(bf16[512,128]{1,0:T(8,128)(2,1)S(1)} %get-tuple-element.192), channel_id=1, source_target_pairs={{0,4},{4,0},{8,12},{12,8},{16,20},{20,16},{24,28},{28,24},{1,5},{5... | collective-permute-start | bytes 393224 | tf_op jit(solution)/shard_map/ppermute | solution.py:452
  40.2 6.4 %collective-permute-start.12 = (bf16[512,128]{1,0:T(8,128)(2,1)S(1)}, bf16[512,128]{1,0:T(8,128)(2,1)S(1)}, u32[]{:S(2)}, u32[]{:S(2)}) collective-permute-start(bf16[512,128]{1,0:T(8,128)(2,1)S(1)} %get-tuple-element.193), channel_id=1, source_target_pairs={{0,12},{4,8},{8,4},{12,0},{16,28},{20,24},{24,20},{28,16},{1,13},{... | collective-permute-start | bytes 393224 | tf_op jit(solution)/shard_map/ppermute | solution.py:452
  46.7 7.5 %collective-permute-start.13 = (bf16[512,128]{1,0:T(8,128)(2,1)S(1)}, bf16[512,128]{1,0:T(8,128)(2,1)S(1)}, u32[]{:S(2)}, u32[]{:S(2)}) collective-permute-start(bf16[512,128]{1,0:T(8,128)(2,1)S(1)} %get-tuple-element.198), channel_id=1, source_target_pairs={{0,16},{4,20},{8,24},{12,28},{16,0},{20,4},{24,8},{28,12},{1,17},{... | collective-permute-start | bytes 393224 | tf_op jit(solution)/shard_map/ppermute | solution.py:510
  54.3 6.3 %collective-permute-start.16 = (bf16[512,128]{1,0:T(8,128)(2,1)S(1)}, bf16[512,128]{1,0:T(8,128)(2,1)S(1)}, u32[]{:S(2)}, u32[]{:S(2)}) collective-permute-start(bf16[512,128]{1,0:T(8,128)(2,1)S(1)} %get-tuple-element.205), channel_id=1, source_target_pairs={{0,8},{4,12},{8,0},{12,4},{16,24},{20,28},{24,16},{28,20},{1,9},{5... | collective-permute-start | bytes 393224 | tf_op jit(solution)/shard_map/ppermute | solution.py:452
  55.3 6.2 %collective-permute-start.15 = (bf16[512,128]{1,0:T(8,128)(2,1)S(1)}, bf16[512,128]{1,0:T(8,128)(2,1)S(1)}, u32[]{:S(2)}, u32[]{:S(2)}) collective-permute-start(bf16[512,128]{1,0:T(8,128)(2,1)S(1)} %get-tuple-element.203), channel_id=1, source_target_pairs={{0,4},{4,0},{8,12},{12,8},{16,20},{20,16},{24,28},{28,24},{1,5},{5... | collective-permute-start | bytes 393224 | tf_op jit(solution)/shard_map/ppermute | solution.py:452
  56.2 6.4 %collective-permute-start.14 = (bf16[512,128]{1,0:T(8,128)(2,1)S(1)}, bf16[512,128]{1,0:T(8,128)(2,1)S(1)}, u32[]{:S(2)}, u32[]{:S(2)}) collective-permute-start(bf16[512,128]{1,0:T(8,128)(2,1)S(1)} %get-tuple-element.201), channel_id=1, source_target_pairs={{0,12},{4,8},{8,4},{12,0},{16,28},{20,24},{24,20},{28,16},{1,13},{... | collective-permute-start | bytes 393224 | tf_op jit(solution)/shard_map/ppermute | solution.py:452

commit v6 on v5

--- a/solution.py
+++ b/solution.py
@@ -47,6 +47,10 @@
     return partner(place, slot, size) if size & (size - 1) == 0 else (place + size - slot) % size
 
 
+def mirrored(place, half, size):
+    return place ^ (2 * half) if size == 4 else place
+
+
 def my_place(size):
     return lax.rem(lax.axis_index("seq"), size)
 
@@ -85,8 +89,11 @@
         self.hpo = -(-heads // size)
         self.span = self.hpo * dim
 
+    def owner(self, slot):
+        return mirrored(partner(my_place(self.size), slot, self.size), lax.axis_index("seq") // self.size, self.size)
+
     def lanes(self, slot):
-        start = partner(my_place(self.size), slot, self.size) * self.span
+        start = self.owner(slot) * self.span
         return pl.ds(pl.multiple_of(start, self.span), self.span)
 
     def head(self, i):
@@ -105,7 +112,7 @@
         return slice(pair[0] * self.dim, (pair[-1] + 1) * self.dim)
 
     def guard(self, slot):
-        return pl.when(partner(my_place(self.size), slot, self.size) * self.hpo < self.heads)
+        return pl.when(self.owner(slot) * self.hpo < self.heads)
 
 
 def order(size):
@@ -172,13 +179,13 @@
     for owner in range(heads // hpo):
         rows = slice(owner * hpo, (owner + 1) * hpo)
         natural_ref[owner] = jnp.concatenate([logs[rows], enter[rows], leave[rows], fill], axis=0)
-    table_ref[0] = natural_ref[jnp.minimum(my_place(size), heads // hpo - 1)]
+    table_ref[0] = natural_ref[jnp.minimum(plan.owner(0), heads // hpo - 1)]
 
     for slot in range(1, size):
 
         @plan.guard(slot)
         def _():
-            table = natural_ref[partner(my_place(size), slot, size)]
+            table = natural_ref[plan.owner(slot)]
             table_ref[slot] = table
             for copy in loads(slot):
                 copy.wait()
@@ -420,7 +427,7 @@
     if last_part:
         for n, pair in enumerate(plan.pairs()):
             for m, (ref, target) in enumerate(((gk_ref, gk_hbm), (gv_ref, gv_hbm))):
-                start = partner(my_place(plan.size), slot, plan.size) * plan.span
+                start = plan.owner(slot) * plan.span
                 width = len(pair) * plan.dim
                 lanes = pl.ds(pl.multiple_of(start + n * width, width), width)
                 sem = sems.at[len(finished) + 2 * n + m]
@@ -506,7 +513,7 @@
             [pltpu.VMEM((size, *arrays[0].shape), BF16)],
         )
         if halves == 2:
-            pairs = [(i, (i + size) % (2 * size)) for i in range(2 * size)]
+            pairs = [(i, (1 - i // size) * size + mirrored(i % size, 1, size)) for i in range(2 * size)]
             outer = lax.ppermute(total, "seq", pairs)
         else:
             outer = jnp.zeros_like(total)

time: 65.4 us -> 63.9 us (0.977)
  waiting for transfers between devices: 10.9 us -> 8.65 us
    ppermute x2, waiting for transfers between devices: 2.17 us -> 0.41 us  [scan(): outer = lax.ppermute(total, 'seq', pairs)]
    ppermute x12, waiting for transfers between devices: 6.62 us -> 5.82 us  [exchange(): lax.ppermute(arrays[slot], 'seq', pairs(slot))]
  transfers between devices with their start and end apart: 17 -> 17, of which waited for: 9 -> 10; matrix products, arithmetic and copies ran while one was open for 0% -> 0% of each run, Pallas kernels for 35% -> 36%
where the time goes in v6:
time: 63.9 us; the launch traced here: 63.7 us
  Pallas kernels  30.2 us (47%)
  starting transfers between devices  23.8 us (37%)
  waiting for transfers between devices  8.65 us (14%)
  between operations  1.03 us (2%)
    pallas_call x27, Pallas kernels, call(): pl.pallas_call(kernel, in_specs=[hbm if f else inside for f in far] + [un...  30.2 us
    ppermute x12, starting transfers between devices, exchange(): lax.ppermute(arrays[slot], 'seq', pairs(slot))  15.4 us
    ppermute x2, starting transfers between devices, scan(): outer = lax.ppermute(total, 'seq', pairs)  6.21 us
    ppermute x12, waiting for transfers between devices, exchange(): lax.ppermute(arrays[slot], 'seq', pairs(slot))  5.82 us
    ppermute x3, waiting for transfers between devices, per_device(): lax.ppermute(sums, 'head', [(i, partner(i, k, shares)) for i in range(sha...  2.42 us
    ppermute x3, starting transfers between devices, per_device(): lax.ppermute(sums, 'head', [(i, partner(i, k, shares)) for i in range(sha...  2.21 us
  transfers between devices with their start and end apart: 17, of which 10 were waited for; matrix products, arithmetic and copies ran while one was open for 0% of the time, Pallas kernels for 36%

profile of v6, /device:TPU:0, one launch (start us, length us, event | category | flops | bytes accessed | tf_op | source)
XLA Modules:
  0.0 63.7 jit_solution(10127316064955921045)
XLA Ops:
  0.6 2.4 %update.1 = (bf16[528,128]{1,0:T(8,128)(2,1)S(1)}, bf16[528,128]{1,0:T(8,128)(2,1)S(1)}, bf16[528,128]{1,0:T(8,128)(2,1)S(1)}, bf16[512,512]{1,0:T(8,128)(2,1)S(...) custom-call(f32[16,512]{1,0:T(8,128)} %logs_hbm.1, ...), custom_call_target="tpu_custom_call" | custom-call | flops 268435456 | bytes 262144 | tf_op jit(solution)/shard_map/update/pallas_call | solution.py:491
  3.1 3.1 %collective-permute-start = (bf16[528,128]{1,0:T(8,128)(2,1)S(1)}, bf16[528,128]{1,0:T(8,128)(2,1)S(1)}, u32[]{:S(2)}, u32[]{:S(2)}) collective-permute-start(bf16[528,128]{1,0:T(8,128)(2,1)S(1)} %get-tuple-element.127), channel_id=1, source_target_pairs={{0,8},{4,12},{8,0},{12,4},{16,24},{20,28},{24,16},{28,20},{1,9},{5... | collective-permute-start | bytes 405512 | tf_op jit(solution)/shard_map/ppermute | solution.py:459
  6.2 1.5 %collective-permute-start.1 = (bf16[528,128]{1,0:T(8,128)(2,1)S(1)}, bf16[528,128]{1,0:T(8,128)(2,1)S(1)}, u32[]{:S(2)}, u32[]{:S(2)}) collective-permute-start(bf16[528,128]{1,0:T(8,128)(2,1)S(1)} %get-tuple-element.128), channel_id=1, source_target_pairs={{0,4},{4,0},{8,12},{12,8},{16,20},{20,16},{24,28},{28,24},{1,5},{5... | collective-permute-start | bytes 405512 | tf_op jit(solution)/shard_map/ppermute | solution.py:459
  7.7 3.5 %intra.4 = (bf16[512,512]{1,0:T(8,128)(2,1)S(1)}, bf16[512,512]{1,0:T(8,128)(2,1)S(1)}, bf16[512,512]{1,0:T(8,128)(2,1)S(1)}, bf16[528,128]{1,0:T(8,128)(2,1)S(1...) custom-call(f32[4,16,512]{2,1,0:T(8,128)S(1)} %get-tuple-element.116, ...), custom_call_target="tpu_custom_call" | custom-call | flops 536870912 | bytes 262144 | tf_op jit(solution)/shard_map/intra/pallas_call | solution.py:491
  11.2 1.8 %intra.6 = (f32[512,512]{1,0:T(8,128)S(1)}, bf16[512,512]{1,0:T(8,128)(2,1)S(1)}, bf16[4,768,256]{2,1,0:T(8,128)(2,1)S(1)}, bf16[4,768,256]{2,1,0:T(8,128)(2,1)S(1)}) custom-call(f32[4,16,512]{2,1,0:T(8,128)S(1)} %get-tuple-element.116.table_ref.refs_0_, bf16[512,512]{1,0:T(8,128)(2,1)S(1)} %get-tuple-element.131.refs_0_.refs_1_, ...), custom_call_target="tpu_custom_call" | custom-call | flops 536870912 | bytes 262144 | tf_op jit(solution)/shard_map/intra/pallas_call | solution.py:491
  13.0 1.1 %collective-permute-done.1.refs_2_ = bf16[528,128]{1,0:T(8,128)(2,1)S(1)} collective-permute-done((bf16[528,128]{1,0:T(8,128)(2,1)S(1)}, bf16[528,128]{1,0:T(8,128)(2,1)S(1)}, u32[]{:S(2)}, u32[]{:S(2)}) %collective-permute-start.1) | collective-permute-done | bytes 135200 | tf_op jit(solution)/shard_map/ppermute | solution.py:459
  14.3 3.3 %collective-permute-start.3 = (bf16[512,128]{1,0:T(8,128)(2,1)S(1)}, bf16[512,128]{1,0:T(8,128)(2,1)S(1)}, u32[]{:S(2)}, u32[]{:S(2)}) collective-permute-start(bf16[512,128]{1,0:T(8,128)(2,1)S(1)} %get-tuple-element.137), channel_id=1, source_target_pairs={{0,24},{4,28},{8,16},{12,20},{16,8},{20,12},{24,0},{28,4},{1,25},{... | collective-permute-start | bytes 393224 | tf_op jit(solution)/shard_map/ppermute | solution.py:517
  17.6 1.8 %intra.5 = (f32[512,512]{1,0:T(8,128)S(1)}, bf16[512,512]{1,0:T(8,128)(2,1)S(1)}, bf16[4,768,256]{2,1,0:T(8,128)(2,1)S(1)}, bf16[4,768,256]{2,1,0:T(8,128)(2,1)S(1)}) custom-call(f32[4,16,512]{2,1,0:T(8,128)S(1)} %get-tuple-element.116.table_ref.refs_0_, bf16[512,512]{1,0:T(8,128)(2,1)S(1)} %get-tuple-element.122.refs_0_.refs_1_, ...), custom_call_target="tpu_custom_call" | custom-call | flops 536870912 | bytes 262144 | tf_op jit(solution)/shard_map/intra/pallas_call | solution.py:491
  19.4 1.8 %intra.7 = (f32[512,512]{1,0:T(8,128)S(1)}, bf16[512,512]{1,0:T(8,128)(2,1)S(1)}, bf16[4,768,256]{2,1,0:T(8,128)(2,1)S(1)}, bf16[4,768,256]{2,1,0:T(8,128)(2,1)S(1)}) custom-call(f32[4,16,512]{2,1,0:T(8,128)S(1)} %get-tuple-element.116.table_ref.refs_0_, bf16[512,512]{1,0:T(8,128)(2,1)S(1)} %get-tuple-element.138.refs_0_.refs_1_, ...), custom_call_target="tpu_custom_call" | custom-call | flops 536870912 | bytes 262144 | tf_op jit(solution)/shard_map/intra/pallas_call | solution.py:491
  21.3 1.6 %collective-permute-start.6 = (bf16[512,128]{1,0:T(8,128)(2,1)S(1)}, bf16[512,128]{1,0:T(8,128)(2,1)S(1)}, u32[]{:S(2)}, u32[]{:S(2)}) collective-permute-start(bf16[512,128]{1,0:T(8,128)(2,1)S(1)} %get-tuple-element.146), channel_id=1, source_target_pairs={{0,8},{4,12},{8,0},{12,4},{16,24},{20,28},{24,16},{28,20},{1,9},{5... | collective-permute-start | bytes 393224 | tf_op jit(solution)/shard_map/ppermute | solution.py:459
  22.9 1.2 %collective-permute-start.5 = (bf16[512,128]{1,0:T(8,128)(2,1)S(1)}, bf16[512,128]{1,0:T(8,128)(2,1)S(1)}, u32[]{:S(2)}, u32[]{:S(2)}) collective-permute-start(bf16[512,128]{1,0:T(8,128)(2,1)S(1)} %get-tuple-element.144), channel_id=1, source_target_pairs={{0,4},{4,0},{8,12},{12,8},{16,20},{20,16},{24,28},{28,24},{1,5},{5... | collective-permute-start | bytes 393224 | tf_op jit(solution)/shard_map/ppermute | solution.py:459
  24.1 0.8 %collective-permute-start.4 = (bf16[512,128]{1,0:T(8,128)(2,1)S(1)}, bf16[512,128]{1,0:T(8,128)(2,1)S(1)}, u32[]{:S(2)}, u32[]{:S(2)}) collective-permute-start(bf16[512,128]{1,0:T(8,128)(2,1)S(1)} %get-tuple-element.142), channel_id=1, source_target_pairs={{0,12},{4,8},{8,4},{12,0},{16,28},{20,24},{24,20},{28,16},{1,13},{... | collective-permute-start | bytes 393224 | tf_op jit(solution)/shard_map/ppermute | solution.py:459
  25.6 1.4 %collective-permute-done.6.state_ref.refs_8_ = bf16[512,128]{1,0:T(8,128)(2,1)S(1)} collective-permute-done((bf16[512,128]{1,0:T(8,128)(2,1)S(1)}, bf16[512,128]{1,0:T(8,128)(2,1)S(1)}, u32[]{:S(2)}, u32[]{:S(2)}) %collective-permute-start.6) | collective-permute-done | bytes 131104 | tf_op jit(solution)/shard_map/ppermute | solution.py:459
  28.5 1.4 %collective-permute-done.4.state_ref.refs_8_ = bf16[512,128]{1,0:T(8,128)(2,1)S(1)} collective-permute-done((bf16[512,128]{1,0:T(8,128)(2,1)S(1)}, bf16[512,128]{1,0:T(8,128)(2,1)S(1)}, u32[]{:S(2)}, u32[]{:S(2)}) %collective-permute-start.4) | collective-permute-done | bytes 131104 | tf_op jit(solution)/shard_map/ppermute | solution.py:459
  30.8 1.6 %collective-permute-start.9 = (f32[8,128]{1,0:T(8,128)S(1)}, f32[8,128]{1,0:T(8,128)S(1)}, u32[]{:S(2)}, u32[]{:S(2)}) collective-permute-start(f32[8,128]{1,0:T(8,128)S(1)} %sums.1.refs_0_), channel_id=1, source_target_pairs={{0,2},{1,3},{2,0},{3,1},{4,6},{5,7},{6,4},{7,5},{8,10},{9,11},{10,... | collective-permute-start | bytes 12296 | tf_op jit(solution)/shard_map/ppermute | solution.py:593
  33.0 1.5 %collective-permute-done.9.refs_3_ = f32[8,128]{1,0:T(8,128)S(1)} collective-permute-done((f32[8,128]{1,0:T(8,128)S(1)}, f32[8,128]{1,0:T(8,128)S(1)}, u32[]{:S(2)}, u32[]{:S(2)}) %collective-permute-start.9) | collective-permute-done | bytes 4128 | tf_op jit(solution)/shard_map/ppermute | solution.py:593
  34.5 1.0 %collective-permute-done.8.refs_2_ = f32[8,128]{1,0:T(8,128)S(1)} collective-permute-done((f32[8,128]{1,0:T(8,128)S(1)}, f32[8,128]{1,0:T(8,128)S(1)}, u32[]{:S(2)}, u32[]{:S(2)}) %collective-permute-start.8) | collective-permute-done | bytes 4128 | tf_op jit(solution)/shard_map/ppermute | solution.py:593
  35.4 0.8 %gout.4 = (f32[2,512,128]{2,1,0:T(8,128)S(1)}, bf16[512,512]{1,0:T(8,128)(2,1)S(1)}, bf16[512,128]{1,0:T(8,128)(2,1)S(1)}) custom-call(f32[8,128]{1,0:T(8,128)S(1)} %sums.1.refs_0_, f32[8,128]{1,0:T(8,128)S(1)} %collective-permute-done.7.refs_1_, f32[8,128]{1,0:T(8,128)S(1)} %collective-permute-done.8.refs_2_, f32[8,128]{1,0:T(8,128)S(1)} %collective-permute-done.9.refs_3_, ...), custom_call_target="tpu_custom_call" | custom-call | flops 67108864 | bytes 262144 | tf_op jit(solution)/shard_map/gout/pallas_call | solution.py:491
  36.2 0.9 %collective-permute-start.10 = (bf16[512,128]{1,0:T(8,128)(2,1)S(1)}, bf16[512,128]{1,0:T(8,128)(2,1)S(1)}, u32[]{:S(2)}, u32[]{:S(2)}) collective-permute-start(bf16[512,128]{1,0:T(8,128)(2,1)S(1)} %get-tuple-element.191), channel_id=1, source_target_pairs={{0,8},{4,12},{8,0},{12,4},{16,24},{20,28},{24,16},{28,20},{1,9},{5... | collective-permute-start | bytes 393224 | tf_op jit(solution)/shard_map/ppermute | solution.py:459
  37.6 1.4 %collective-permute-start.11 = (bf16[512,128]{1,0:T(8,128)(2,1)S(1)}, bf16[512,128]{1,0:T(8,128)(2,1)S(1)}, u32[]{:S(2)}, u32[]{:S(2)}) collective-permute-start(bf16[512,128]{1,0:T(8,128)(2,1)S(1)} %get-tuple-element.192), channel_id=1, source_target_pairs={{0,4},{4,0},{8,12},{12,8},{16,20},{20,16},{24,28},{28,24},{1,5},{5... | collective-permute-start | bytes 393224 | tf_op jit(solution)/shard_map/ppermute | solution.py:459
  39.5 1.3 %collective-permute-start.12 = (bf16[512,128]{1,0:T(8,128)(2,1)S(1)}, bf16[512,128]{1,0:T(8,128)(2,1)S(1)}, u32[]{:S(2)}, u32[]{:S(2)}) collective-permute-start(bf16[512,128]{1,0:T(8,128)(2,1)S(1)} %get-tuple-element.193), channel_id=1, source_target_pairs={{0,12},{4,8},{8,4},{12,0},{16,28},{20,24},{24,20},{28,16},{1,13},{... | collective-permute-start | bytes 393224 | tf_op jit(solution)/shard_map/ppermute | solution.py:459
  42.0 1.9 %gradient.4 = (bf16[512,2048]{1,0:T(8,128)(2,1)}, bf16[512,512]{1,0:T(8,128)(2,1)S(1)}, f32[512,512]{1,0:T(8,128)S(1)}, f32[512,512]{1,0:T(8,128)S(1)}) custom-call(f32[4,16,512]{2,1,0:T(8,128)S(1)} %get-tuple-element.116.table_ref.refs_0_, bf16[512,512]{1,0:T(8,128)(2,1)S(1)} %get-tuple-element.117.refs_1_, ...), custom_call_target="tpu_custom_call" | custom-call | flops 1073741824 | bytes 262144 | tf_op jit(solution)/shard_map/gradient/pallas_call | solution.py:491
  44.3 1.2 %collective-permute-done.12.refs_3_ = bf16[512,128]{1,0:T(8,128)(2,1)S(1)} collective-permute-done((bf16[512,128]{1,0:T(8,128)(2,1)S(1)}, bf16[512,128]{1,0:T(8,128)(2,1)S(1)}, u32[]{:S(2)}, u32[]{:S(2)}) %collective-permute-start.12) | collective-permute-done | bytes 131104 | tf_op jit(solution)/shard_map/ppermute | solution.py:459
  45.6 2.9 %collective-permute-start.13 = (bf16[512,128]{1,0:T(8,128)(2,1)S(1)}, bf16[512,128]{1,0:T(8,128)(2,1)S(1)}, u32[]{:S(2)}, u32[]{:S(2)}) collective-permute-start(bf16[512,128]{1,0:T(8,128)(2,1)S(1)} %get-tuple-element.198), channel_id=1, source_target_pairs={{0,24},{4,28},{8,16},{12,20},{16,8},{20,12},{24,0},{28,4},{1,25},{... | collective-permute-start | bytes 393224 | tf_op jit(solution)/shard_map/ppermute | solution.py:517
  48.6 1.8 %gradient.5 = (bf16[512,2048]{1,0:T(8,128)(2,1)}, bf16[512,512]{1,0:T(8,128)(2,1)S(1)}, f32[512,512]{1,0:T(8,128)S(1)}, f32[512,512]{1,0:T(8,128)S(1)}) custom-call(f32[4,16,512]{2,1,0:T(8,128)S(1)} %get-tuple-element.116.table_ref.refs_0_, bf16[512,512]{1,0:T(8,128)(2,1)S(1)} %get-tuple-element.131.refs_0_.refs_1_, ...), custom_call_target="tpu_custom_call" | custom-call | flops 1073741824 | bytes 262144 | tf_op jit(solution)/shard_map/gradient/pallas_call | solution.py:491
  50.4 1.9 %gradient.6 = (bf16[512,2048]{1,0:T(8,128)(2,1)}, bf16[512,512]{1,0:T(8,128)(2,1)S(1)}, f32[512,512]{1,0:T(8,128)S(1)}, f32[512,512]{1,0:T(8,128)S(1)}) custom-call(f32[4,16,512]{2,1,0:T(8,128)S(1)} %get-tuple-element.116.table_ref.refs_0_, bf16[512,512]{1,0:T(8,128)(2,1)S(1)} %get-tuple-element.138.refs_0_.refs_1_, ...), custom_call_target="tpu_custom_call", output_to_operand_aliasing={{0}: (10, {})} | custom-call | flops 1073741824 | bytes 262144 | tf_op jit(solution)/shard_map/gradient/pallas_call | solution.py:491
  54.0 2.3 %collective-permute-start.14 = (bf16[512,128]{1,0:T(8,128)(2,1)S(1)}, bf16[512,128]{1,0:T(8,128)(2,1)S(1)}, u32[]{:S(2)}, u32[]{:S(2)}) collective-permute-start(bf16[512,128]{1,0:T(8,128)(2,1)S(1)} %get-tuple-element.201), channel_id=1, source_target_pairs={{0,12},{4,8},{8,4},{12,0},{16,28},{20,24},{24,20},{28,16},{1,13},{... | collective-permute-start | bytes 393224 | tf_op jit(solution)/shard_map/ppermute | solution.py:459
  56.3 1.8 %gradient.7 = (bf16[512,2048]{1,0:T(8,128)(2,1)}, bf16[512,512]{1,0:T(8,128)(2,1)S(1)}, f32[512,512]{1,0:T(8,128)S(1)}, f32[512,512]{1,0:T(8,128)S(1)}) custom-call(f32[4,16,512]{2,1,0:T(8,128)S(1)} %get-tuple-element.116.table_ref.refs_0_, bf16[512,512]{1,0:T(8,128)(2,1)S(1)} %get-tuple-element.122.refs_0_.refs_1_, ...), custom_call_target="tpu_custom_call", output_to_operand_aliasing={{0}: (10, {})} | custom-call | flops 1073741824 | bytes 262144 | tf_op jit(solution)/shard_map/gradient/pallas_call | solution.py:491
  58.1 0.9 %final.4 = (bf16[512,2048]{1,0:T(8,128)(2,1)}, bf16[512,2048]{1,0:T(8,128)(2,1)}, bf16[512,2048]{1,0:T(8,128)(2,1)}, bf16[512,512]{1,0:T(8,128)(2,1)S(1)}, bf16[512,512]{1,0:T(8,128)(2,1)S(1)}) custom-call(f32[4,16,512]{2,1,0:T(8,128)S(1)} %get-tuple-element.116.table_ref.refs_0_, ...), custom_call_target="tpu_custom_call", output_to_operand_aliasing={{0}: (7, {})} | custom-call | flops 134217728 | bytes 262144 | tf_op jit(solution)/shard_map/final/pallas_call | solution.py:491
  59.0 1.0 %final.5 = (bf16[512,2048]{1,0:T(8,128)(2,1)}, bf16[512,2048]{1,0:T(8,128)(2,1)}, bf16[512,2048]{1,0:T(8,128)(2,1)}, bf16[512,512]{1,0:T(8,128)(2,1)S(1)}, bf16[512,512]{1,0:T(8,128)(2,1)S(1)}) custom-call(f32[4,16,512]{2,1,0:T(8,128)S(1)} %get-tuple-element.116.table_ref.refs_0_, ...), custom_call_target="tpu_custom_call", output_to_operand_aliasing={{0}: (8, {}), {1}: (9, {}), {2}: (10, {})} | custom-call | flops 134217728 | bytes 262144 | tf_op jit(solution)/shard_map/final/pallas_call | solution.py:491
  60.0 1.0 %final.6 = (bf16[512,2048]{1,0:T(8,128)(2,1)}, bf16[512,2048]{1,0:T(8,128)(2,1)}, bf16[512,2048]{1,0:T(8,128)(2,1)}, bf16[512,512]{1,0:T(8,128)(2,1)S(1)}, bf16[512,512]{1,0:T(8,128)(2,1)S(1)}) custom-call(f32[4,16,512]{2,1,0:T(8,128)S(1)} %get-tuple-element.116.table_ref.refs_0_, ...), custom_call_target="tpu_custom_call", output_to_operand_aliasing={{0}: (8, {}), {1}: (9, {}), {2}: (10, {})} | custom-call | flops 134217728 | bytes 262144 | tf_op jit(solution)/shard_map/final/pallas_call | solution.py:491
  61.1 2.5 %final.7 = (bf16[512,2048]{1,0:T(8,128)(2,1)}, bf16[512,2048]{1,0:T(8,128)(2,1)}, bf16[512,2048]{1,0:T(8,128)(2,1)}, bf16[512,512]{1,0:T(8,128)(2,1)}, bf16[512,512]{1,0:T(8,128)(2,1)}) custom-call(f32[4,16,512]{2,1,0:T(8,128)S(1)} %get-tuple-element.116.table_ref.refs_0_, ...), custom_call_target="tpu_custom_call", output_to_operand_aliasing={{0}: (8, {}), {1}: (9, {}), {2}: (10, {})} | custom-call | flops 134217728 | bytes 262144 | tf_op jit(solution)/shard_map/final/pallas_call | solution.py:491
  (29 shorter events, 8.4 us)
Async XLA Ops:
  3.1 9.9 %collective-permute-start = (bf16[528,128]{1,0:T(8,128)(2,1)S(1)}, bf16[528,128]{1,0:T(8,128)(2,1)S(1)}, u32[]{:S(2)}, u32[]{:S(2)}) collective-permute-start(bf16[528,128]{1,0:T(8,128)(2,1)S(1)} %get-tuple-element.127), channel_id=1, source_target_pairs={{0,8},{4,12},{8,0},{12,4},{16,24},{20,28},{24,16},{28,20},{1,9},{5... | collective-permute-start | bytes 405512 | tf_op jit(solution)/shard_map/ppermute | solution.py:459
  6.2 7.9 %collective-permute-start.1 = (bf16[528,128]{1,0:T(8,128)(2,1)S(1)}, bf16[528,128]{1,0:T(8,128)(2,1)S(1)}, u32[]{:S(2)}, u32[]{:S(2)}) collective-permute-start(bf16[528,128]{1,0:T(8,128)(2,1)S(1)} %get-tuple-element.128), channel_id=1, source_target_pairs={{0,4},{4,0},{8,12},{12,8},{16,20},{20,16},{24,28},{28,24},{1,5},{5... | collective-permute-start | bytes 405512 | tf_op jit(solution)/shard_map/ppermute | solution.py:459
  7.7 6.5 %collective-permute-start.2 = (bf16[528,128]{1,0:T(8,128)(2,1)S(1)}, bf16[528,128]{1,0:T(8,128)(2,1)S(1)}, u32[]{:S(2)}, u32[]{:S(2)}) collective-permute-start(bf16[528,128]{1,0:T(8,128)(2,1)S(1)} %get-tuple-element.129), channel_id=1, source_target_pairs={{0,12},{4,8},{8,4},{12,0},{16,28},{20,24},{24,20},{28,16},{1,13},{... | collective-permute-start | bytes 405512 | tf_op jit(solution)/shard_map/ppermute | solution.py:459
  14.3 6.9 %collective-permute-start.3 = (bf16[512,128]{1,0:T(8,128)(2,1)S(1)}, bf16[512,128]{1,0:T(8,128)(2,1)S(1)}, u32[]{:S(2)}, u32[]{:S(2)}) collective-permute-start(bf16[512,128]{1,0:T(8,128)(2,1)S(1)} %get-tuple-element.137), channel_id=1, source_target_pairs={{0,24},{4,28},{8,16},{12,20},{16,8},{20,12},{24,0},{28,4},{1,25},{... | collective-permute-start | bytes 393224 | tf_op jit(solution)/shard_map/ppermute | solution.py:517
  21.3 5.6 %collective-permute-start.6 = (bf16[512,128]{1,0:T(8,128)(2,1)S(1)}, bf16[512,128]{1,0:T(8,128)(2,1)S(1)}, u32[]{:S(2)}, u32[]{:S(2)}) collective-permute-start(bf16[512,128]{1,0:T(8,128)(2,1)S(1)} %get-tuple-element.146), channel_id=1, source_target_pairs={{0,8},{4,12},{8,0},{12,4},{16,24},{20,28},{24,16},{28,20},{1,9},{5... | collective-permute-start | bytes 393224 | tf_op jit(solution)/shard_map/ppermute | solution.py:459
  22.9 5.0 %collective-permute-start.5 = (bf16[512,128]{1,0:T(8,128)(2,1)S(1)}, bf16[512,128]{1,0:T(8,128)(2,1)S(1)}, u32[]{:S(2)}, u32[]{:S(2)}) collective-permute-start(bf16[512,128]{1,0:T(8,128)(2,1)S(1)} %get-tuple-element.144), channel_id=1, source_target_pairs={{0,4},{4,0},{8,12},{12,8},{16,20},{20,16},{24,28},{28,24},{1,5},{5... | collective-permute-start | bytes 393224 | tf_op jit(solution)/shard_map/ppermute | solution.py:459
  24.1 5.9 %collective-permute-start.4 = (bf16[512,128]{1,0:T(8,128)(2,1)S(1)}, bf16[512,128]{1,0:T(8,128)(2,1)S(1)}, u32[]{:S(2)}, u32[]{:S(2)}) collective-permute-start(bf16[512,128]{1,0:T(8,128)(2,1)S(1)} %get-tuple-element.142), channel_id=1, source_target_pairs={{0,12},{4,8},{8,4},{12,0},{16,28},{20,24},{24,20},{28,16},{1,13},{... | collective-permute-start | bytes 393224 | tf_op jit(solution)/shard_map/ppermute | solution.py:459
  30.8 3.7 %collective-permute-start.9 = (f32[8,128]{1,0:T(8,128)S(1)}, f32[8,128]{1,0:T(8,128)S(1)}, u32[]{:S(2)}, u32[]{:S(2)}) collective-permute-start(f32[8,128]{1,0:T(8,128)S(1)} %sums.1.refs_0_), channel_id=1, source_target_pairs={{0,2},{1,3},{2,0},{3,1},{4,6},{5,7},{6,4},{7,5},{8,10},{9,11},{10,... | collective-permute-start | bytes 12296 | tf_op jit(solution)/shard_map/ppermute | solution.py:593
  32.4 3.0 %collective-permute-start.8 = (f32[8,128]{1,0:T(8,128)S(1)}, f32[8,128]{1,0:T(8,128)S(1)}, u32[]{:S(2)}, u32[]{:S(2)}) collective-permute-start(f32[8,128]{1,0:T(8,128)S(1)} %sums.1.refs_0_), channel_id=1, source_target_pairs={{0,3},{1,2},{2,1},{3,0},{4,7},{5,6},{6,5},{7,4},{8,11},{9,10},{10,... | collective-permute-start | bytes 12296 | tf_op jit(solution)/shard_map/ppermute | solution.py:593
  32.4 3.0 %collective-permute-start.7 = (f32[8,128]{1,0:T(8,128)S(1)}, f32[8,128]{1,0:T(8,128)S(1)}, u32[]{:S(2)}, u32[]{:S(2)}) collective-permute-start(f32[8,128]{1,0:T(8,128)S(1)} %sums.1.refs_0_), channel_id=1, source_target_pairs={{0,1},{1,0},{2,3},{3,2},{4,5},{5,4},{6,7},{7,6},{8,9},{9,8},{10,11... | collective-permute-start | bytes 12296 | tf_op jit(solution)/shard_map/ppermute | solution.py:593
  36.2 7.7 %collective-permute-start.10 = (bf16[512,128]{1,0:T(8,128)(2,1)S(1)}, bf16[512,128]{1,0:T(8,128)(2,1)S(1)}, u32[]{:S(2)}, u32[]{:S(2)}) collective-permute-start(bf16[512,128]{1,0:T(8,128)(2,1)S(1)} %get-tuple-element.191), channel_id=1, source_target_pairs={{0,8},{4,12},{8,0},{12,4},{16,24},{20,28},{24,16},{28,20},{1,9},{5... | collective-permute-start | bytes 393224 | tf_op jit(solution)/shard_map/ppermute | solution.py:459
  37.6 6.6 %collective-permute-start.11 = (bf16[512,128]{1,0:T(8,128)(2,1)S(1)}, bf16[512,128]{1,0:T(8,128)(2,1)S(1)}, u32[]{:S(2)}, u32[]{:S(2)}) collective-permute-start(bf16[512,128]{1,0:T(8,128)(2,1)S(1)} %get-tuple-element.192), channel_id=1, source_target_pairs={{0,4},{4,0},{8,12},{12,8},{16,20},{20,16},{24,28},{28,24},{1,5},{5... | collective-permute-start | bytes 393224 | tf_op jit(solution)/shard_map/ppermute | solution.py:459
  39.5 5.9 %collective-permute-start.12 = (bf16[512,128]{1,0:T(8,128)(2,1)S(1)}, bf16[512,128]{1,0:T(8,128)(2,1)S(1)}, u32[]{:S(2)}, u32[]{:S(2)}) collective-permute-start(bf16[512,128]{1,0:T(8,128)(2,1)S(1)} %get-tuple-element.193), channel_id=1, source_target_pairs={{0,12},{4,8},{8,4},{12,0},{16,28},{20,24},{24,20},{28,16},{1,13},{... | collective-permute-start | bytes 393224 | tf_op jit(solution)/shard_map/ppermute | solution.py:459
  45.6 7.0 %collective-permute-start.13 = (bf16[512,128]{1,0:T(8,128)(2,1)S(1)}, bf16[512,128]{1,0:T(8,128)(2,1)S(1)}, u32[]{:S(2)}, u32[]{:S(2)}) collective-permute-start(bf16[512,128]{1,0:T(8,128)(2,1)S(1)} %get-tuple-element.198), channel_id=1, source_target_pairs={{0,24},{4,28},{8,16},{12,20},{16,8},{20,12},{24,0},{28,4},{1,25},{... | collective-permute-start | bytes 393224 | tf_op jit(solution)/shard_map/ppermute | solution.py:517
  52.7 6.3 %collective-permute-start.16 = (bf16[512,128]{1,0:T(8,128)(2,1)S(1)}, bf16[512,128]{1,0:T(8,128)(2,1)S(1)}, u32[]{:S(2)}, u32[]{:S(2)}) collective-permute-start(bf16[512,128]{1,0:T(8,128)(2,1)S(1)} %get-tuple-element.205), channel_id=1, source_target_pairs={{0,8},{4,12},{8,0},{12,4},{16,24},{20,28},{24,16},{28,20},{1,9},{5... | collective-permute-start | bytes 393224 | tf_op jit(solution)/shard_map/ppermute | solution.py:459
  53.4 6.6 %collective-permute-start.15 = (bf16[512,128]{1,0:T(8,128)(2,1)S(1)}, bf16[512,128]{1,0:T(8,128)(2,1)S(1)}, u32[]{:S(2)}, u32[]{:S(2)}) collective-permute-start(bf16[512,128]{1,0:T(8,128)(2,1)S(1)} %get-tuple-element.203), channel_id=1, source_target_pairs={{0,4},{4,0},{8,12},{12,8},{16,20},{20,16},{24,28},{28,24},{1,5},{5... | collective-permute-start | bytes 393224 | tf_op jit(solution)/shard_map/ppermute | solution.py:459
  54.0 7.1 %collective-permute-start.14 = (bf16[512,128]{1,0:T(8,128)(2,1)S(1)}, bf16[512,128]{1,0:T(8,128)(2,1)S(1)}, u32[]{:S(2)}, u32[]{:S(2)}) collective-permute-start(bf16[512,128]{1,0:T(8,128)(2,1)S(1)} %get-tuple-element.201), channel_id=1, source_target_pairs={{0,12},{4,8},{8,4},{12,0},{16,28},{20,24},{24,20},{28,16},{1,13},{... | collective-permute-start | bytes 393224 | tf_op jit(solution)/shard_map/ppermute | solution.py:459

commit v7 on v6

--- a/solution.py
+++ b/solution.py
@@ -252,7 +252,7 @@
         ]
         start_all(plan, copies)
         mask_ref[...] = block_mask(table_ref[0])
-        wait_all(plan, copies[:3])
+        wait_all(plan, copies[:2])
     else:
         k_ref, v_ref, q_ref, mask_ref, out_ref, decayed_ref, probs_ref, weight_ref = refs
 
@@ -262,6 +262,7 @@
         columns = table.T
         if first_part:
             update_slot(plan, table, k_ref, v_ref, turned_ref, sent_ref)
+            copies[2][1].wait()
         for i in range(hpo):
             lanes = plan.head(i)
             turned = q_ref[:, lanes].T

time: 63.9 us -> 63.9 us (level)
  no operation moved by 1% of the time
where the time goes in v7:
time: 63.9 us; the launch traced here: 63.7 us
  Pallas kernels  30 us (47%)
  starting transfers between devices  23.7 us (37%)
  waiting for transfers between devices  9 us (14%)
  between operations  1.03 us (2%)
    pallas_call x27, Pallas kernels, call(): pl.pallas_call(kernel, in_specs=[hbm if f else inside for f in far] + [un...  30 us
    ppermute x12, starting transfers between devices, exchange(): lax.ppermute(arrays[slot], 'seq', pairs(slot))  15.4 us
    ppermute x12, waiting for transfers between devices, exchange(): lax.ppermute(arrays[slot], 'seq', pairs(slot))  6.07 us
    ppermute x2, starting transfers between devices, scan(): outer = lax.ppermute(total, 'seq', pairs)  6.06 us
    ppermute x3, waiting for transfers between devices, per_device(): lax.ppermute(sums, 'head', [(i, partner(i, k, shares)) for i in range(sha...  2.36 us
    ppermute x3, starting transfers between devices, per_device(): lax.ppermute(sums, 'head', [(i, partner(i, k, shares)) for i in range(sha...  2.21 us
  transfers between devices with their start and end apart: 17, of which 10 were waited for; matrix products, arithmetic and copies ran while one was open for 0% of the time, Pallas kernels for 36%

profile of v7, /device:TPU:0, one launch (start us, length us, event | category | flops | bytes accessed | tf_op | source)
XLA Modules:
  0.0 63.7 jit_solution(995395074129945138)
XLA Ops:
  0.6 2.4 %update.1 = (bf16[528,128]{1,0:T(8,128)(2,1)S(1)}, bf16[528,128]{1,0:T(8,128)(2,1)S(1)}, bf16[528,128]{1,0:T(8,128)(2,1)S(1)}, bf16[512,512]{1,0:T(8,128)(2,1)S(...) custom-call(f32[16,512]{1,0:T(8,128)} %logs_hbm.1, ...), custom_call_target="tpu_custom_call" | custom-call | flops 268435456 | bytes 262144 | tf_op jit(solution)/shard_map/update/pallas_call | solution.py:492
  3.1 3.1 %collective-permute-start = (bf16[528,128]{1,0:T(8,128)(2,1)S(1)}, bf16[528,128]{1,0:T(8,128)(2,1)S(1)}, u32[]{:S(2)}, u32[]{:S(2)}) collective-permute-start(bf16[528,128]{1,0:T(8,128)(2,1)S(1)} %get-tuple-element.127), channel_id=1, source_target_pairs={{0,8},{4,12},{8,0},{12,4},{16,24},{20,28},{24,16},{28,20},{1,9},{5... | collective-permute-start | bytes 405512 | tf_op jit(solution)/shard_map/ppermute | solution.py:460
  6.2 1.5 %collective-permute-start.1 = (bf16[528,128]{1,0:T(8,128)(2,1)S(1)}, bf16[528,128]{1,0:T(8,128)(2,1)S(1)}, u32[]{:S(2)}, u32[]{:S(2)}) collective-permute-start(bf16[528,128]{1,0:T(8,128)(2,1)S(1)} %get-tuple-element.128), channel_id=1, source_target_pairs={{0,4},{4,0},{8,12},{12,8},{16,20},{20,16},{24,28},{28,24},{1,5},{5... | collective-permute-start | bytes 405512 | tf_op jit(solution)/shard_map/ppermute | solution.py:460
  7.7 3.3 %intra.4 = (bf16[512,512]{1,0:T(8,128)(2,1)S(1)}, bf16[512,512]{1,0:T(8,128)(2,1)S(1)}, bf16[512,512]{1,0:T(8,128)(2,1)S(1)}, bf16[528,128]{1,0:T(8,128)(2,1)S(1...) custom-call(f32[4,16,512]{2,1,0:T(8,128)S(1)} %get-tuple-element.116, ...), custom_call_target="tpu_custom_call" | custom-call | flops 536870912 | bytes 262144 | tf_op jit(solution)/shard_map/intra/pallas_call | solution.py:492
  11.0 1.8 %intra.6 = (f32[512,512]{1,0:T(8,128)S(1)}, bf16[512,512]{1,0:T(8,128)(2,1)S(1)}, bf16[4,768,256]{2,1,0:T(8,128)(2,1)S(1)}, bf16[4,768,256]{2,1,0:T(8,128)(2,1)S(1)}) custom-call(f32[4,16,512]{2,1,0:T(8,128)S(1)} %get-tuple-element.116.table_ref.refs_0_, bf16[512,512]{1,0:T(8,128)(2,1)S(1)} %get-tuple-element.131.refs_0_.refs_1_, ...), custom_call_target="tpu_custom_call" | custom-call | flops 536870912 | bytes 262144 | tf_op jit(solution)/shard_map/intra/pallas_call | solution.py:492
  12.8 1.3 %collective-permute-done.1.refs_2_ = bf16[528,128]{1,0:T(8,128)(2,1)S(1)} collective-permute-done((bf16[528,128]{1,0:T(8,128)(2,1)S(1)}, bf16[528,128]{1,0:T(8,128)(2,1)S(1)}, u32[]{:S(2)}, u32[]{:S(2)}) %collective-permute-start.1) | collective-permute-done | bytes 135200 | tf_op jit(solution)/shard_map/ppermute | solution.py:460
  14.3 3.3 %collective-permute-start.3 = (bf16[512,128]{1,0:T(8,128)(2,1)S(1)}, bf16[512,128]{1,0:T(8,128)(2,1)S(1)}, u32[]{:S(2)}, u32[]{:S(2)}) collective-permute-start(bf16[512,128]{1,0:T(8,128)(2,1)S(1)} %get-tuple-element.137), channel_id=1, source_target_pairs={{0,24},{4,28},{8,16},{12,20},{16,8},{20,12},{24,0},{28,4},{1,25},{... | collective-permute-start | bytes 393224 | tf_op jit(solution)/shard_map/ppermute | solution.py:518
  17.6 1.8 %intra.5 = (f32[512,512]{1,0:T(8,128)S(1)}, bf16[512,512]{1,0:T(8,128)(2,1)S(1)}, bf16[4,768,256]{2,1,0:T(8,128)(2,1)S(1)}, bf16[4,768,256]{2,1,0:T(8,128)(2,1)S(1)}) custom-call(f32[4,16,512]{2,1,0:T(8,128)S(1)} %get-tuple-element.116.table_ref.refs_0_, bf16[512,512]{1,0:T(8,128)(2,1)S(1)} %get-tuple-element.122.refs_0_.refs_1_, ...), custom_call_target="tpu_custom_call" | custom-call | flops 536870912 | bytes 262144 | tf_op jit(solution)/shard_map/intra/pallas_call | solution.py:492
  19.4 1.8 %intra.7 = (f32[512,512]{1,0:T(8,128)S(1)}, bf16[512,512]{1,0:T(8,128)(2,1)S(1)}, bf16[4,768,256]{2,1,0:T(8,128)(2,1)S(1)}, bf16[4,768,256]{2,1,0:T(8,128)(2,1)S(1)}) custom-call(f32[4,16,512]{2,1,0:T(8,128)S(1)} %get-tuple-element.116.table_ref.refs_0_, bf16[512,512]{1,0:T(8,128)(2,1)S(1)} %get-tuple-element.138.refs_0_.refs_1_, ...), custom_call_target="tpu_custom_call" | custom-call | flops 536870912 | bytes 262144 | tf_op jit(solution)/shard_map/intra/pallas_call | solution.py:492
  21.3 1.6 %collective-permute-start.6 = (bf16[512,128]{1,0:T(8,128)(2,1)S(1)}, bf16[512,128]{1,0:T(8,128)(2,1)S(1)}, u32[]{:S(2)}, u32[]{:S(2)}) collective-permute-start(bf16[512,128]{1,0:T(8,128)(2,1)S(1)} %get-tuple-element.146), channel_id=1, source_target_pairs={{0,8},{4,12},{8,0},{12,4},{16,24},{20,28},{24,16},{28,20},{1,9},{5... | collective-permute-start | bytes 393224 | tf_op jit(solution)/shard_map/ppermute | solution.py:460
  22.9 1.0 %collective-permute-start.5 = (bf16[512,128]{1,0:T(8,128)(2,1)S(1)}, bf16[512,128]{1,0:T(8,128)(2,1)S(1)}, u32[]{:S(2)}, u32[]{:S(2)}) collective-permute-start(bf16[512,128]{1,0:T(8,128)(2,1)S(1)} %get-tuple-element.144), channel_id=1, source_target_pairs={{0,4},{4,0},{8,12},{12,8},{16,20},{20,16},{24,28},{28,24},{1,5},{5... | collective-permute-start | bytes 393224 | tf_op jit(solution)/shard_map/ppermute | solution.py:460
  23.9 1.0 %collective-permute-start.4 = (bf16[512,128]{1,0:T(8,128)(2,1)S(1)}, bf16[512,128]{1,0:T(8,128)(2,1)S(1)}, u32[]{:S(2)}, u32[]{:S(2)}) collective-permute-start(bf16[512,128]{1,0:T(8,128)(2,1)S(1)} %get-tuple-element.142), channel_id=1, source_target_pairs={{0,12},{4,8},{8,4},{12,0},{16,28},{20,24},{24,20},{28,16},{1,13},{... | collective-permute-start | bytes 393224 | tf_op jit(solution)/shard_map/ppermute | solution.py:460
  25.6 1.4 %collective-permute-done.6.state_ref.refs_8_ = bf16[512,128]{1,0:T(8,128)(2,1)S(1)} collective-permute-done((bf16[512,128]{1,0:T(8,128)(2,1)S(1)}, bf16[512,128]{1,0:T(8,128)(2,1)S(1)}, u32[]{:S(2)}, u32[]{:S(2)}) %collective-permute-start.6) | collective-permute-done | bytes 131104 | tf_op jit(solution)/shard_map/ppermute | solution.py:460
  28.5 1.3 %collective-permute-done.4.state_ref.refs_8_ = bf16[512,128]{1,0:T(8,128)(2,1)S(1)} collective-permute-done((bf16[512,128]{1,0:T(8,128)(2,1)S(1)}, bf16[512,128]{1,0:T(8,128)(2,1)S(1)}, u32[]{:S(2)}, u32[]{:S(2)}) %collective-permute-start.4) | collective-permute-done | bytes 131104 | tf_op jit(solution)/shard_map/ppermute | solution.py:460
  30.7 1.5 %collective-permute-start.9 = (f32[8,128]{1,0:T(8,128)S(1)}, f32[8,128]{1,0:T(8,128)S(1)}, u32[]{:S(2)}, u32[]{:S(2)}) collective-permute-start(f32[8,128]{1,0:T(8,128)S(1)} %sums.1.refs_0_), channel_id=1, source_target_pairs={{0,2},{1,3},{2,0},{3,1},{4,6},{5,7},{6,4},{7,5},{8,10},{9,11},{10,... | collective-permute-start | bytes 12296 | tf_op jit(solution)/shard_map/ppermute | solution.py:594
  32.9 1.5 %collective-permute-done.9.refs_3_ = f32[8,128]{1,0:T(8,128)S(1)} collective-permute-done((f32[8,128]{1,0:T(8,128)S(1)}, f32[8,128]{1,0:T(8,128)S(1)}, u32[]{:S(2)}, u32[]{:S(2)}) %collective-permute-start.9) | collective-permute-done | bytes 4128 | tf_op jit(solution)/shard_map/ppermute | solution.py:594
  34.3 0.9 %collective-permute-done.8.refs_2_ = f32[8,128]{1,0:T(8,128)S(1)} collective-permute-done((f32[8,128]{1,0:T(8,128)S(1)}, f32[8,128]{1,0:T(8,128)S(1)}, u32[]{:S(2)}, u32[]{:S(2)}) %collective-permute-start.8) | collective-permute-done | bytes 4128 | tf_op jit(solution)/shard_map/ppermute | solution.py:594
  35.2 0.8 %gout.4 = (f32[2,512,128]{2,1,0:T(8,128)S(1)}, bf16[512,512]{1,0:T(8,128)(2,1)S(1)}, bf16[512,128]{1,0:T(8,128)(2,1)S(1)}) custom-call(f32[8,128]{1,0:T(8,128)S(1)} %sums.1.refs_0_, f32[8,128]{1,0:T(8,128)S(1)} %collective-permute-done.7.refs_1_, f32[8,128]{1,0:T(8,128)S(1)} %collective-permute-done.8.refs_2_, f32[8,128]{1,0:T(8,128)S(1)} %collective-permute-done.9.refs_3_, ...), custom_call_target="tpu_custom_call" | custom-call | flops 67108864 | bytes 262144 | tf_op jit(solution)/shard_map/gout/pallas_call | solution.py:492
  36.0 1.1 %collective-permute-start.10 = (bf16[512,128]{1,0:T(8,128)(2,1)S(1)}, bf16[512,128]{1,0:T(8,128)(2,1)S(1)}, u32[]{:S(2)}, u32[]{:S(2)}) collective-permute-start(bf16[512,128]{1,0:T(8,128)(2,1)S(1)} %get-tuple-element.191), channel_id=1, source_target_pairs={{0,8},{4,12},{8,0},{12,4},{16,24},{20,28},{24,16},{28,20},{1,9},{5... | collective-permute-start | bytes 393224 | tf_op jit(solution)/shard_map/ppermute | solution.py:460
  37.6 1.4 %collective-permute-start.11 = (bf16[512,128]{1,0:T(8,128)(2,1)S(1)}, bf16[512,128]{1,0:T(8,128)(2,1)S(1)}, u32[]{:S(2)}, u32[]{:S(2)}) collective-permute-start(bf16[512,128]{1,0:T(8,128)(2,1)S(1)} %get-tuple-element.192), channel_id=1, source_target_pairs={{0,4},{4,0},{8,12},{12,8},{16,20},{20,16},{24,28},{28,24},{1,5},{5... | collective-permute-start | bytes 393224 | tf_op jit(solution)/shard_map/ppermute | solution.py:460
  39.5 1.2 %collective-permute-start.12 = (bf16[512,128]{1,0:T(8,128)(2,1)S(1)}, bf16[512,128]{1,0:T(8,128)(2,1)S(1)}, u32[]{:S(2)}, u32[]{:S(2)}) collective-permute-start(bf16[512,128]{1,0:T(8,128)(2,1)S(1)} %get-tuple-element.193), channel_id=1, source_target_pairs={{0,12},{4,8},{8,4},{12,0},{16,28},{20,24},{24,20},{28,16},{1,13},{... | collective-permute-start | bytes 393224 | tf_op jit(solution)/shard_map/ppermute | solution.py:460
  41.8 1.9 %gradient.4 = (bf16[512,2048]{1,0:T(8,128)(2,1)}, bf16[512,512]{1,0:T(8,128)(2,1)S(1)}, f32[512,512]{1,0:T(8,128)S(1)}, f32[512,512]{1,0:T(8,128)S(1)}) custom-call(f32[4,16,512]{2,1,0:T(8,128)S(1)} %get-tuple-element.116.table_ref.refs_0_, bf16[512,512]{1,0:T(8,128)(2,1)S(1)} %get-tuple-element.117.refs_1_, ...), custom_call_target="tpu_custom_call" | custom-call | flops 1073741824 | bytes 262144 | tf_op jit(solution)/shard_map/gradient/pallas_call | solution.py:492
  44.3 1.2 %collective-permute-done.12.refs_3_ = bf16[512,128]{1,0:T(8,128)(2,1)S(1)} collective-permute-done((bf16[512,128]{1,0:T(8,128)(2,1)S(1)}, bf16[512,128]{1,0:T(8,128)(2,1)S(1)}, u32[]{:S(2)}, u32[]{:S(2)}) %collective-permute-start.12) | collective-permute-done | bytes 131104 | tf_op jit(solution)/shard_map/ppermute | solution.py:460
  45.6 2.8 %collective-permute-start.13 = (bf16[512,128]{1,0:T(8,128)(2,1)S(1)}, bf16[512,128]{1,0:T(8,128)(2,1)S(1)}, u32[]{:S(2)}, u32[]{:S(2)}) collective-permute-start(bf16[512,128]{1,0:T(8,128)(2,1)S(1)} %get-tuple-element.198), channel_id=1, source_target_pairs={{0,24},{4,28},{8,16},{12,20},{16,8},{20,12},{24,0},{28,4},{1,25},{... | collective-permute-start | bytes 393224 | tf_op jit(solution)/shard_map/ppermute | solution.py:518
  48.4 1.8 %gradient.5 = (bf16[512,2048]{1,0:T(8,128)(2,1)}, bf16[512,512]{1,0:T(8,128)(2,1)S(1)}, f32[512,512]{1,0:T(8,128)S(1)}, f32[512,512]{1,0:T(8,128)S(1)}) custom-call(f32[4,16,512]{2,1,0:T(8,128)S(1)} %get-tuple-element.116.table_ref.refs_0_, bf16[512,512]{1,0:T(8,128)(2,1)S(1)} %get-tuple-element.131.refs_0_.refs_1_, ...), custom_call_target="tpu_custom_call" | custom-call | flops 1073741824 | bytes 262144 | tf_op jit(solution)/shard_map/gradient/pallas_call | solution.py:492
  50.2 1.9 %gradient.6 = (bf16[512,2048]{1,0:T(8,128)(2,1)}, bf16[512,512]{1,0:T(8,128)(2,1)S(1)}, f32[512,512]{1,0:T(8,128)S(1)}, f32[512,512]{1,0:T(8,128)S(1)}) custom-call(f32[4,16,512]{2,1,0:T(8,128)S(1)} %get-tuple-element.116.table_ref.refs_0_, bf16[512,512]{1,0:T(8,128)(2,1)S(1)} %get-tuple-element.138.refs_0_.refs_1_, ...), custom_call_target="tpu_custom_call", output_to_operand_aliasing={{0}: (10, {})} | custom-call | flops 1073741824 | bytes 262144 | tf_op jit(solution)/shard_map/gradient/pallas_call | solution.py:492
  54.0 2.2 %collective-permute-start.14 = (bf16[512,128]{1,0:T(8,128)(2,1)S(1)}, bf16[512,128]{1,0:T(8,128)(2,1)S(1)}, u32[]{:S(2)}, u32[]{:S(2)}) collective-permute-start(bf16[512,128]{1,0:T(8,128)(2,1)S(1)} %get-tuple-element.201), channel_id=1, source_target_pairs={{0,12},{4,8},{8,4},{12,0},{16,28},{20,24},{24,20},{28,16},{1,13},{... | collective-permute-start | bytes 393224 | tf_op jit(solution)/shard_map/ppermute | solution.py:460
  56.3 1.8 %gradient.7 = (bf16[512,2048]{1,0:T(8,128)(2,1)}, bf16[512,512]{1,0:T(8,128)(2,1)S(1)}, f32[512,512]{1,0:T(8,128)S(1)}, f32[512,512]{1,0:T(8,128)S(1)}) custom-call(f32[4,16,512]{2,1,0:T(8,128)S(1)} %get-tuple-element.116.table_ref.refs_0_, bf16[512,512]{1,0:T(8,128)(2,1)S(1)} %get-tuple-element.122.refs_0_.refs_1_, ...), custom_call_target="tpu_custom_call", output_to_operand_aliasing={{0}: (10, {})} | custom-call | flops 1073741824 | bytes 262144 | tf_op jit(solution)/shard_map/gradient/pallas_call | solution.py:492
  58.1 0.9 %final.4 = (bf16[512,2048]{1,0:T(8,128)(2,1)}, bf16[512,2048]{1,0:T(8,128)(2,1)}, bf16[512,2048]{1,0:T(8,128)(2,1)}, bf16[512,512]{1,0:T(8,128)(2,1)S(1)}, bf16[512,512]{1,0:T(8,128)(2,1)S(1)}) custom-call(f32[4,16,512]{2,1,0:T(8,128)S(1)} %get-tuple-element.116.table_ref.refs_0_, ...), custom_call_target="tpu_custom_call", output_to_operand_aliasing={{0}: (7, {})} | custom-call | flops 134217728 | bytes 262144 | tf_op jit(solution)/shard_map/final/pallas_call | solution.py:492
  59.0 1.0 %final.5 = (bf16[512,2048]{1,0:T(8,128)(2,1)}, bf16[512,2048]{1,0:T(8,128)(2,1)}, bf16[512,2048]{1,0:T(8,128)(2,1)}, bf16[512,512]{1,0:T(8,128)(2,1)S(1)}, bf16[512,512]{1,0:T(8,128)(2,1)S(1)}) custom-call(f32[4,16,512]{2,1,0:T(8,128)S(1)} %get-tuple-element.116.table_ref.refs_0_, ...), custom_call_target="tpu_custom_call", output_to_operand_aliasing={{0}: (8, {}), {1}: (9, {}), {2}: (10, {})} | custom-call | flops 134217728 | bytes 262144 | tf_op jit(solution)/shard_map/final/pallas_call | solution.py:492
  60.0 1.0 %final.6 = (bf16[512,2048]{1,0:T(8,128)(2,1)}, bf16[512,2048]{1,0:T(8,128)(2,1)}, bf16[512,2048]{1,0:T(8,128)(2,1)}, bf16[512,512]{1,0:T(8,128)(2,1)S(1)}, bf16[512,512]{1,0:T(8,128)(2,1)S(1)}) custom-call(f32[4,16,512]{2,1,0:T(8,128)S(1)} %get-tuple-element.116.table_ref.refs_0_, ...), custom_call_target="tpu_custom_call", output_to_operand_aliasing={{0}: (8, {}), {1}: (9, {}), {2}: (10, {})} | custom-call | flops 134217728 | bytes 262144 | tf_op jit(solution)/shard_map/final/pallas_call | solution.py:492
  61.1 2.5 %final.7 = (bf16[512,2048]{1,0:T(8,128)(2,1)}, bf16[512,2048]{1,0:T(8,128)(2,1)}, bf16[512,2048]{1,0:T(8,128)(2,1)}, bf16[512,512]{1,0:T(8,128)(2,1)}, bf16[512,512]{1,0:T(8,128)(2,1)}) custom-call(f32[4,16,512]{2,1,0:T(8,128)S(1)} %get-tuple-element.116.table_ref.refs_0_, ...), custom_call_target="tpu_custom_call", output_to_operand_aliasing={{0}: (8, {}), {1}: (9, {}), {2}: (10, {})} | custom-call | flops 134217728 | bytes 262144 | tf_op jit(solution)/shard_map/final/pallas_call | solution.py:492
  (29 shorter events, 8.9 us)
Async XLA Ops:
  3.1 9.7 %collective-permute-start = (bf16[528,128]{1,0:T(8,128)(2,1)S(1)}, bf16[528,128]{1,0:T(8,128)(2,1)S(1)}, u32[]{:S(2)}, u32[]{:S(2)}) collective-permute-start(bf16[528,128]{1,0:T(8,128)(2,1)S(1)} %get-tuple-element.127), channel_id=1, source_target_pairs={{0,8},{4,12},{8,0},{12,4},{16,24},{20,28},{24,16},{28,20},{1,9},{5... | collective-permute-start | bytes 405512 | tf_op jit(solution)/shard_map/ppermute | solution.py:460
  6.2 7.9 %collective-permute-start.1 = (bf16[528,128]{1,0:T(8,128)(2,1)S(1)}, bf16[528,128]{1,0:T(8,128)(2,1)S(1)}, u32[]{:S(2)}, u32[]{:S(2)}) collective-permute-start(bf16[528,128]{1,0:T(8,128)(2,1)S(1)} %get-tuple-element.128), channel_id=1, source_target_pairs={{0,4},{4,0},{8,12},{12,8},{16,20},{20,16},{24,28},{28,24},{1,5},{5... | collective-permute-start | bytes 405512 | tf_op jit(solution)/shard_map/ppermute | solution.py:460
  7.7 6.5 %collective-permute-start.2 = (bf16[528,128]{1,0:T(8,128)(2,1)S(1)}, bf16[528,128]{1,0:T(8,128)(2,1)S(1)}, u32[]{:S(2)}, u32[]{:S(2)}) collective-permute-start(bf16[528,128]{1,0:T(8,128)(2,1)S(1)} %get-tuple-element.129), channel_id=1, source_target_pairs={{0,12},{4,8},{8,4},{12,0},{16,28},{20,24},{24,20},{28,16},{1,13},{... | collective-permute-start | bytes 405512 | tf_op jit(solution)/shard_map/ppermute | solution.py:460
  14.3 6.9 %collective-permute-start.3 = (bf16[512,128]{1,0:T(8,128)(2,1)S(1)}, bf16[512,128]{1,0:T(8,128)(2,1)S(1)}, u32[]{:S(2)}, u32[]{:S(2)}) collective-permute-start(bf16[512,128]{1,0:T(8,128)(2,1)S(1)} %get-tuple-element.137), channel_id=1, source_target_pairs={{0,24},{4,28},{8,16},{12,20},{16,8},{20,12},{24,0},{28,4},{1,25},{... | collective-permute-start | bytes 393224 | tf_op jit(solution)/shard_map/ppermute | solution.py:518
  21.3 5.6 %collective-permute-start.6 = (bf16[512,128]{1,0:T(8,128)(2,1)S(1)}, bf16[512,128]{1,0:T(8,128)(2,1)S(1)}, u32[]{:S(2)}, u32[]{:S(2)}) collective-permute-start(bf16[512,128]{1,0:T(8,128)(2,1)S(1)} %get-tuple-element.146), channel_id=1, source_target_pairs={{0,8},{4,12},{8,0},{12,4},{16,24},{20,28},{24,16},{28,20},{1,9},{5... | collective-permute-start | bytes 393224 | tf_op jit(solution)/shard_map/ppermute | solution.py:460
  22.9 5.0 %collective-permute-start.5 = (bf16[512,128]{1,0:T(8,128)(2,1)S(1)}, bf16[512,128]{1,0:T(8,128)(2,1)S(1)}, u32[]{:S(2)}, u32[]{:S(2)}) collective-permute-start(bf16[512,128]{1,0:T(8,128)(2,1)S(1)} %get-tuple-element.144), channel_id=1, source_target_pairs={{0,4},{4,0},{8,12},{12,8},{16,20},{20,16},{24,28},{28,24},{1,5},{5... | collective-permute-start | bytes 393224 | tf_op jit(solution)/shard_map/ppermute | solution.py:460
  23.9 5.9 %collective-permute-start.4 = (bf16[512,128]{1,0:T(8,128)(2,1)S(1)}, bf16[512,128]{1,0:T(8,128)(2,1)S(1)}, u32[]{:S(2)}, u32[]{:S(2)}) collective-permute-start(bf16[512,128]{1,0:T(8,128)(2,1)S(1)} %get-tuple-element.142), channel_id=1, source_target_pairs={{0,12},{4,8},{8,4},{12,0},{16,28},{20,24},{24,20},{28,16},{1,13},{... | collective-permute-start | bytes 393224 | tf_op jit(solution)/shard_map/ppermute | solution.py:460
  30.7 3.7 %collective-permute-start.9 = (f32[8,128]{1,0:T(8,128)S(1)}, f32[8,128]{1,0:T(8,128)S(1)}, u32[]{:S(2)}, u32[]{:S(2)}) collective-permute-start(f32[8,128]{1,0:T(8,128)S(1)} %sums.1.refs_0_), channel_id=1, source_target_pairs={{0,2},{1,3},{2,0},{3,1},{4,6},{5,7},{6,4},{7,5},{8,10},{9,11},{10,... | collective-permute-start | bytes 12296 | tf_op jit(solution)/shard_map/ppermute | solution.py:594
  32.2 3.0 %collective-permute-start.8 = (f32[8,128]{1,0:T(8,128)S(1)}, f32[8,128]{1,0:T(8,128)S(1)}, u32[]{:S(2)}, u32[]{:S(2)}) collective-permute-start(f32[8,128]{1,0:T(8,128)S(1)} %sums.1.refs_0_), channel_id=1, source_target_pairs={{0,3},{1,2},{2,1},{3,0},{4,7},{5,6},{6,5},{7,4},{8,11},{9,10},{10,... | collective-permute-start | bytes 12296 | tf_op jit(solution)/shard_map/ppermute | solution.py:594
  32.2 3.0 %collective-permute-start.7 = (f32[8,128]{1,0:T(8,128)S(1)}, f32[8,128]{1,0:T(8,128)S(1)}, u32[]{:S(2)}, u32[]{:S(2)}) collective-permute-start(f32[8,128]{1,0:T(8,128)S(1)} %sums.1.refs_0_), channel_id=1, source_target_pairs={{0,1},{1,0},{2,3},{3,2},{4,5},{5,4},{6,7},{7,6},{8,9},{9,8},{10,11... | collective-permute-start | bytes 12296 | tf_op jit(solution)/shard_map/ppermute | solution.py:594
  36.0 7.7 %collective-permute-start.10 = (bf16[512,128]{1,0:T(8,128)(2,1)S(1)}, bf16[512,128]{1,0:T(8,128)(2,1)S(1)}, u32[]{:S(2)}, u32[]{:S(2)}) collective-permute-start(bf16[512,128]{1,0:T(8,128)(2,1)S(1)} %get-tuple-element.191), channel_id=1, source_target_pairs={{0,8},{4,12},{8,0},{12,4},{16,24},{20,28},{24,16},{28,20},{1,9},{5... | collective-permute-start | bytes 393224 | tf_op jit(solution)/shard_map/ppermute | solution.py:460
  37.6 6.6 %collective-permute-start.11 = (bf16[512,128]{1,0:T(8,128)(2,1)S(1)}, bf16[512,128]{1,0:T(8,128)(2,1)S(1)}, u32[]{:S(2)}, u32[]{:S(2)}) collective-permute-start(bf16[512,128]{1,0:T(8,128)(2,1)S(1)} %get-tuple-element.192), channel_id=1, source_target_pairs={{0,4},{4,0},{8,12},{12,8},{16,20},{20,16},{24,28},{28,24},{1,5},{5... | collective-permute-start | bytes 393224 | tf_op jit(solution)/shard_map/ppermute | solution.py:460
  39.5 5.9 %collective-permute-start.12 = (bf16[512,128]{1,0:T(8,128)(2,1)S(1)}, bf16[512,128]{1,0:T(8,128)(2,1)S(1)}, u32[]{:S(2)}, u32[]{:S(2)}) collective-permute-start(bf16[512,128]{1,0:T(8,128)(2,1)S(1)} %get-tuple-element.193), channel_id=1, source_target_pairs={{0,12},{4,8},{8,4},{12,0},{16,28},{20,24},{24,20},{28,16},{1,13},{... | collective-permute-start | bytes 393224 | tf_op jit(solution)/shard_map/ppermute | solution.py:460
  45.6 7.0 %collective-permute-start.13 = (bf16[512,128]{1,0:T(8,128)(2,1)S(1)}, bf16[512,128]{1,0:T(8,128)(2,1)S(1)}, u32[]{:S(2)}, u32[]{:S(2)}) collective-permute-start(bf16[512,128]{1,0:T(8,128)(2,1)S(1)} %get-tuple-element.198), channel_id=1, source_target_pairs={{0,24},{4,28},{8,16},{12,20},{16,8},{20,12},{24,0},{28,4},{1,25},{... | collective-permute-start | bytes 393224 | tf_op jit(solution)/shard_map/ppermute | solution.py:518
  52.7 6.3 %collective-permute-start.16 = (bf16[512,128]{1,0:T(8,128)(2,1)S(1)}, bf16[512,128]{1,0:T(8,128)(2,1)S(1)}, u32[]{:S(2)}, u32[]{:S(2)}) collective-permute-start(bf16[512,128]{1,0:T(8,128)(2,1)S(1)} %get-tuple-element.205), channel_id=1, source_target_pairs={{0,8},{4,12},{8,0},{12,4},{16,24},{20,28},{24,16},{28,20},{1,9},{5... | collective-permute-start | bytes 393224 | tf_op jit(solution)/shard_map/ppermute | solution.py:460
  53.3 6.7 %collective-permute-start.15 = (bf16[512,128]{1,0:T(8,128)(2,1)S(1)}, bf16[512,128]{1,0:T(8,128)(2,1)S(1)}, u32[]{:S(2)}, u32[]{:S(2)}) collective-permute-start(bf16[512,128]{1,0:T(8,128)(2,1)S(1)} %get-tuple-element.203), channel_id=1, source_target_pairs={{0,4},{4,0},{8,12},{12,8},{16,20},{20,16},{24,28},{28,24},{1,5},{5... | collective-permute-start | bytes 393224 | tf_op jit(solution)/shard_map/ppermute | solution.py:460
  54.0 7.1 %collective-permute-start.14 = (bf16[512,128]{1,0:T(8,128)(2,1)S(1)}, bf16[512,128]{1,0:T(8,128)(2,1)S(1)}, u32[]{:S(2)}, u32[]{:S(2)}) collective-permute-start(bf16[512,128]{1,0:T(8,128)(2,1)S(1)} %get-tuple-element.201), channel_id=1, source_target_pairs={{0,12},{4,8},{8,4},{12,0},{16,28},{20,24},{24,20},{28,16},{1,13},{... | collective-permute-start | bytes 393224 | tf_op jit(solution)/shard_map/ppermute | solution.py:460
